TPU v7x, 32 devices: a whole 2x2x4 slice. The times are simulated.
32 devices in a mesh: dp: 8 (over z, y), mp: 4 (over x, core).
Axes of the slice: x: 2, y: 2, z: 4, core: 2. Of those that a mesh axis runs over, the one named last changes fastest.
Arguments:
- latents: float32 [32, 4, 32, 32], P('dp'), may hold values from -6 to 6
- noise: float32 [32, 4, 32, 32], P('dp'), may hold values from -6 to 6
- timesteps: int32 [32], P('dp'), may hold values from 2 to 999, as said below
- labels: int32 [32], P('dp'), may hold values from 0 to 1000
- loss_weights: float32 [32], P('dp'), may hold values from 0.4 to 8
- slotted_block_weights: float32 [4, 72, 288, 288], P('mp', 'dp'), may hold values from -0.1875 to 0.1875
- statistics: float32 [4, 72, 2, 288, 288], P('mp', 'dp'), as said below
- slot_of_block: int32 [72], replicated, may hold values from 0 to 71, each once
- cond_tables: float32 [2425, 1152], P(None, 'dp'), may hold values from -4 to 4
- head_tables: float32 [1152, 2336], P('dp'), may hold values from -0.1875 to 0.1875
- slice_bias: float32 [4, 3456], P('mp'), may hold values from -1.2 to 1.2
- side_bias: float32 [8096], replicated, may hold values from -1.2 to 1.2
- cond_m: float32 [2425, 1152], P(None, 'dp'), may hold values from -0.0007377806 to 0.0007377806
- cond_v: float32 [2425, 1152], P(None, 'dp'), may hold values from 3.402001e-08 to 1.3608005e-07
- head_m: float32 [1152, 2336], P('dp'), may hold values from -0.0007377806 to 0.0007377806
- head_v: float32 [1152, 2336], P('dp'), may hold values from 3.402001e-08 to 1.3608005e-07
- slice_m: float32 [4, 3456], P('mp'), may hold values from -0.0029511224 to 0.0029511224
- slice_v: float32 [4, 3456], P('mp'), may hold values from 5.443202e-07 to 2.1772807e-06
- side_m: float32 [8096], replicated, may hold values from -0.0029511224 to 0.0029511224
- side_v: float32 [8096], replicated, may hold values from 5.443202e-07 to 2.1772807e-06
Outputs:
- loss_sum: float32 [], replicated
- weight_total: float32 [], replicated
- grad_norm: float32 [], replicated
- clipped_block_gradients: float32 [4, 72, 288, 288], P('mp', 'dp')
- new_statistics: float32 [4, 72, 2, 288, 288], P('mp', 'dp')
- new_blocks: float32 [4, 72, 288, 288], P('mp', 'dp')
- new_blocks_bf16: bfloat16 [4, 72, 288, 288], P('mp', 'dp')
- cond_first: float32 [2425, 1152], P(None, 'dp')
- cond_second: float32 [2425, 1152], P(None, 'dp')
- new_cond: float32 [2425, 1152], P(None, 'dp')
- new_cond_bf16: bfloat16 [2425, 1152], P(None, 'dp')
- head_first: float32 [1152, 2336], P('dp')
- head_second: float32 [1152, 2336], P('dp')
- new_head: float32 [1152, 2336], P('dp')
- new_head_bf16: bfloat16 [1152, 2336], P('dp')
- slice_first: float32 [4, 3456], P('mp')
- slice_second: float32 [4, 3456], P('mp')
- new_slice: float32 [4, 3456], P('mp')
- side_first: float32 [8096], replicated
- side_second: float32 [8096], replicated
- new_side: float32 [8096], replicated
Inputs may be any that keep to these rules, and one draw needn't show every extreme that they name: `timesteps`: skewed towards high noise. Block b (b < 72) lies at slot slot_of_block[b], owned by the dp index slot_of_block[b] // 9. `statistics`: each statistic is symmetric positive definite.
All inputs are finite; a program needn't handle non-finite values.
Results may differ from a plain program's by a relative error of at most 0.0086.
Values may be sent and summed in bfloat16 or wider, within the bound.
A program may use at most 320 MiB of HBM per device.

v0:
```python
import math

import jax
import jax.numpy as jnp
from jax import lax
from jax.sharding import PartitionSpec as P

MODEL_WIDTH = 1152
HEADS = 16
HD = 72
FF = 4608
FREQ = 256
CLASSES = 1001
LATENT_SIDE = 32
PATCH_VALUES = 16
BLOCK_SIDE = 288
NEWTON = 6
STEP = 5


exact_precision_flag = lax.Precision.HIGHEST
shampoo_rate = 0.5
adam_rate = 0.05
decay_rate = 0.01


def matmul(operand, other):
    return jnp.matmul(operand, other, precision=exact_precision_flag)


def dense(operand, weight):
    return jnp.dot(operand, weight, preferred_element_type=jnp.float32)


def back_dense(gradient, weight):
    return jnp.einsum("...j,ij->...i", gradient, weight, preferred_element_type=jnp.float32)


def weight_grad(operand, gradient):
    return jnp.einsum("...i,...j->ij", operand, gradient, preferred_element_type=jnp.float32)


def total_of(inputs):
    return jnp.sum(inputs.astype(jnp.float32), axis=tuple(range(inputs.ndim - 1)))


def swish_unit(inputs):
    return inputs / (1.0 + jnp.exp(-inputs))


def swish_slope(inputs):
    sigmoid = 1.0 / (1.0 + jnp.exp(-inputs))
    return sigmoid * (1.0 + inputs * (1.0 - sigmoid))


def tanh_gelu_activation(inputs):
    return (
        0.5
        * inputs
        * (1.0 + jnp.tanh(0.7978845608028654 * (inputs + 0.044715 * inputs * inputs * inputs)))
    )


def gelu_slope(inputs):
    inner = jnp.tanh(0.7978845608028654 * (inputs + 0.044715 * inputs * inputs * inputs))
    return 0.5 * (1.0 + inner) + 0.5 * inputs * (1.0 - inner * inner) * 0.7978845608028654 * (
        1.0 + 3.0 * 0.044715 * inputs * inputs
    )


def layer_norm(inputs):
    centred = inputs - jnp.mean(inputs, -1, keepdims=True)
    inv_std = lax.rsqrt(jnp.mean(centred * centred, -1, keepdims=True) + 1e-06)
    return (centred * inv_std, inv_std)


def norm_back(gradient, normed, inv_std):
    return inv_std * (
        gradient
        - jnp.mean(gradient, -1, keepdims=True)
        - normed * jnp.mean(gradient * normed, -1, keepdims=True)
    )


def coefficients(step_ids):
    grid = jnp.arange(1000).astype(jnp.float32)
    betas = 0.0001 + (0.02 - 0.0001) * grid / 999.0
    cumul = jnp.exp(jnp.cumsum(jnp.log(1.0 - betas)))
    before = jnp.concatenate([jnp.ones((1,), jnp.float32), cumul[:-1]])
    picked = (step_ids[:, None] == jnp.arange(1000, dtype=jnp.int32)[None, :]).astype(jnp.float32)
    beta_t = jnp.sum(picked * betas[None, :], 1)
    cumul_t = jnp.sum(picked * cumul[None, :], 1)
    before_t = jnp.sum(picked * before[None, :], 1)
    keep_rate = jnp.sqrt(cumul_t)
    noise_rate = jnp.sqrt(1.0 - cumul_t)
    upper_log = jnp.log(beta_t)
    lower_log = jnp.log(beta_t * (1.0 - before_t) / (1.0 - cumul_t))
    mean_gap = beta_t * jnp.sqrt(before_t) / (1.0 - cumul_t) * jnp.sqrt(1.0 / cumul_t - 1.0)
    return (keep_rate, noise_rate, upper_log, lower_log, mean_gap)


def time_features(step_ids, feat_width):
    half_width = feat_width // 2
    frequencies = jnp.exp(
        -math.log(10000.0) * jnp.arange(half_width).astype(jnp.float32) / half_width
    )
    phases = step_ids.astype(jnp.float32)[:, None] * frequencies[None, :]
    return jnp.concatenate([jnp.cos(phases), jnp.sin(phases)], 1)


def position_embedding(grid_side, feat_width):
    quarter = feat_width // 4
    omegas = jnp.exp(-math.log(10000.0) * jnp.arange(quarter).astype(jnp.float32) / quarter)
    coords = jnp.arange(grid_side).astype(jnp.float32)
    angles = coords[:, None] * omegas[None, :]
    waves = jnp.concatenate([jnp.sin(angles), jnp.cos(angles)], 1)
    half_width = feat_width // 2
    rows_part = jnp.broadcast_to(waves[:, None, :], (grid_side, grid_side, half_width))
    cols_part = jnp.broadcast_to(waves[None, :, :], (grid_side, grid_side, half_width))
    return jnp.concatenate([rows_part, cols_part], 2).reshape(grid_side * grid_side, feat_width)


def patchify(latent):
    samples_n, channels, height, breadth = latent.shape
    shaped = latent.reshape(samples_n, channels, height // 2, 2, breadth // 2, 2).transpose(
        0, 2, 4, 3, 5, 1
    )
    return shaped.reshape(samples_n, height // 2 * (breadth // 2), 4 * channels)


def assemble(blocks, slot_of_block, first_block, row_count, col_count):
    picked = blocks[slot_of_block[first_block : first_block + row_count * col_count]]
    return (
        picked.reshape(row_count, col_count, BLOCK_SIDE, BLOCK_SIDE)
        .transpose(0, 2, 1, 3)
        .reshape(row_count * BLOCK_SIDE, col_count * BLOCK_SIDE)
    )


def split_blocks(matrix, row_count, col_count):
    return (
        matrix.reshape(row_count, BLOCK_SIDE, col_count, BLOCK_SIDE)
        .transpose(0, 2, 1, 3)
        .reshape(row_count * col_count, BLOCK_SIDE, BLOCK_SIDE)
    )


def loss_terms(result, frozen, target, weights, upper_log, lower_log, mean_gap):
    samples_n = result.shape[0]
    shaped = result.reshape(samples_n, -1, 4, 8)
    predicted = shaped[..., :4]
    var_raw = shaped[..., 4:]
    frozen_pred = frozen.reshape(samples_n, -1, 4, 8)[..., :4]
    upper = upper_log[:, None, None, None]
    lower = lower_log[:, None, None, None]
    squared = jnp.mean((target - predicted) ** 2, axis=(1, 2, 3))
    fraction = (var_raw + 1.0) / 2.0
    log_var = fraction * upper + (1.0 - fraction) * lower
    mean_diff = mean_gap[:, None, None, None] * (frozen_pred - target)
    diverge = 0.5 * (
        -1.0
        + log_var
        - lower
        + jnp.exp(lower - log_var)
        + mean_diff * mean_diff * jnp.exp(-log_var)
    )
    var_bound = jnp.mean(diverge, axis=(1, 2, 3)) / math.log(2.0)
    return jnp.sum(weights * (squared + var_bound))


def inverse_root(matrix):
    size_b = matrix.shape[-1]
    identity = jnp.eye(size_b, dtype=jnp.float32)
    traces = jnp.trace(matrix, axis1=-2, axis2=-1)
    shifted = matrix + (0.0001 * traces / size_b)[..., None, None] * identity
    factor_z = 2.5 / jnp.sqrt(jnp.sum(shifted * shifted, axis=(-2, -1)))
    contracted = shifted * factor_z[..., None, None]
    estimate = identity * jnp.sqrt(jnp.sqrt(factor_z))[..., None, None]
    for newton_step in range(NEWTON):
        factor = (5.0 * identity - contracted) / 4.0
        estimate = matmul(estimate, factor)
        factor_sq = matmul(factor, factor)
        contracted = matmul(matmul(factor_sq, factor_sq), contracted)
    return estimate


def adam_update(weight, gradient, moment_one, second):
    moment_one = 0.5 * moment_one + 0.5 * gradient
    second = 0.5 * second + 0.5 * gradient * gradient
    correct = 1.0 - 0.5**STEP
    updated = weight - adam_rate * (
        moment_one / correct / (jnp.sqrt(second / correct) + 1e-08) + decay_rate * weight
    )
    return (moment_one, second, updated)


def per_device(
    latents,
    noise,
    timesteps,
    labels,
    loss_weights,
    slotted_block_weights,
    statistics,
    slot_of_block,
    cond_tables,
    head_tables,
    slice_bias,
    side_bias,
    cond_m,
    cond_v,
    head_m,
    head_v,
    slice_m,
    slice_v,
    side_m,
    side_v,
):
    model_parallel_ways = lax.axis_size("mp")
    data_ways = lax.axis_size("dp")
    query_width = HEADS * HD // model_parallel_ways
    feedforward_width = FF // model_parallel_ways
    ada_width = 6 * MODEL_WIDTH // model_parallel_ways
    adaptive_column = 3 * query_width + feedforward_width
    row_blocks = MODEL_WIDTH // BLOCK_SIDE
    col_blocks = (adaptive_column + ada_width) // BLOCK_SIDE
    out_blocks = (query_width + feedforward_width) // BLOCK_SIDE
    first_out = row_blocks * col_blocks
    occupied_blocks = first_out + out_blocks * row_blocks
    t2_row = PATCH_VALUES + FREQ
    class_row = PATCH_VALUES + FREQ + MODEL_WIDTH
    local_heads = query_width // HD
    score_scale = HD ** (-0.5)

    def fetch_weights():
        blocks, condition_vectors, head_condition_table = (
            lax.all_gather(slotted_block_weights[0].astype(jnp.bfloat16), "dp", axis=0, tiled=True),
            lax.all_gather(cond_tables.astype(jnp.bfloat16), "dp", axis=1, tiled=True),
            lax.all_gather(head_tables.astype(jnp.bfloat16), "dp", axis=0, tiled=True),
        )
        input_weight = assemble(blocks, slot_of_block, 0, row_blocks, col_blocks)
        output_weight = assemble(blocks, slot_of_block, first_out, out_blocks, row_blocks)
        return (input_weight, output_weight, condition_vectors, head_condition_table)

    def across_model(inputs):
        return lax.psum(inputs, "mp")

    input_weight, output_weight, condition_vectors, head_condition_table = fetch_weights()
    keep_rate, noise_rate, upper_log, lower_log, mean_gap = coefficients(timesteps)
    noisy_lat = keep_rate[:, None, None, None] * latents + noise_rate[:, None, None, None] * noise
    latent_patches = patchify(noisy_lat).astype(jnp.bfloat16)
    batch_rows, seq_len = (latent_patches.shape[0], latent_patches.shape[1])
    target = patchify(noise).reshape(batch_rows, seq_len, 4, 4)
    time_freq = time_features(timesteps, FREQ).astype(jnp.bfloat16)
    onehot = (labels[:, None] == jnp.arange(CLASSES, dtype=jnp.int32)[None, :]).astype(jnp.bfloat16)
    own_bias = slice_bias[0]
    initial_rows = (
        dense(latent_patches, condition_vectors[:PATCH_VALUES])
        + side_bias[:MODEL_WIDTH]
        + position_embedding(LATENT_SIDE // 2, MODEL_WIDTH)
    )
    first_t = (
        dense(time_freq, condition_vectors[PATCH_VALUES:t2_row])
        + side_bias[MODEL_WIDTH : 2 * MODEL_WIDTH]
    )
    first_s = swish_unit(first_t).astype(jnp.bfloat16)
    cond_vec = (
        dense(first_s, condition_vectors[t2_row:class_row])
        + side_bias[2 * MODEL_WIDTH : 3 * MODEL_WIDTH]
        + dense(onehot, condition_vectors[class_row:])
    )
    signal = swish_unit(cond_vec).astype(jnp.bfloat16)
    modul = lax.all_gather(
        dense(signal, input_weight[:, adaptive_column:])
        + own_bias[2 * query_width + feedforward_width :],
        "mp",
        axis=1,
        tiled=True,
    )

    def modulation_part(position):
        return modul[:, None, position * MODEL_WIDTH : (position + 1) * MODEL_WIDTH]

    def heads_of(inputs):
        return inputs.reshape(batch_rows, seq_len, local_heads, HD)

    normed_a, inv_std_a = layer_norm(initial_rows)
    attention_input = (normed_a * (1.0 + modulation_part(1)) + modulation_part(0)).astype(
        jnp.bfloat16
    )
    projected_output = dense(attention_input, input_weight[:, : 3 * query_width])
    queries = heads_of(
        (projected_output[..., :query_width] + own_bias[:query_width]).astype(jnp.bfloat16)
    )
    key_heads = heads_of(projected_output[..., query_width : 2 * query_width].astype(jnp.bfloat16))
    values = heads_of(
        (projected_output[..., 2 * query_width :] + own_bias[query_width : 2 * query_width]).astype(
            jnp.bfloat16
        )
    )

    def score_of():
        return (
            jnp.einsum("slhe,smhe->shlm", queries, key_heads, preferred_element_type=jnp.float32)
            * score_scale
        )

    scores = score_of()
    row_peak = jnp.max(scores, -1, keepdims=True)
    shifted = jnp.exp(scores - row_peak)
    row_total = jnp.sum(shifted, -1, keepdims=True)
    attn_probs = shifted / row_total
    log_total = row_peak + jnp.log(row_total)
    merged_head_outputs = jnp.einsum(
        "shlm,smhe->slhe",
        attn_probs.astype(jnp.bfloat16),
        values,
        preferred_element_type=jnp.float32,
    )
    merged_head_outputs = merged_head_outputs.reshape(batch_rows, seq_len, query_width).astype(
        jnp.bfloat16
    )
    attention_output = (
        across_model(dense(merged_head_outputs, output_weight[:query_width]))
        + side_bias[3 * MODEL_WIDTH : 4 * MODEL_WIDTH]
    )
    middle = initial_rows + modulation_part(2) * attention_output
    normed_m, inv_std_m = layer_norm(middle)
    perceptron_input = (normed_m * (1.0 + modulation_part(4)) + modulation_part(3)).astype(
        jnp.bfloat16
    )
    hidden_activations = (
        dense(perceptron_input, input_weight[:, 3 * query_width : adaptive_column])
        + own_bias[2 * query_width : 2 * query_width + feedforward_width]
    )
    active = tanh_gelu_activation(hidden_activations).astype(jnp.bfloat16)
    branch_output = (
        across_model(dense(active, output_weight[query_width:]))
        + side_bias[4 * MODEL_WIDTH : 5 * MODEL_WIDTH]
    )
    final_rows = middle + modulation_part(5) * branch_output
    final_mod = (
        dense(signal, head_condition_table[:, : 2 * MODEL_WIDTH])
        + side_bias[5 * MODEL_WIDTH : 7 * MODEL_WIDTH]
    )
    normed_f, inv_std_f = layer_norm(final_rows)
    head_input = (
        normed_f * (1.0 + final_mod[:, None, MODEL_WIDTH:]) + final_mod[:, None, :MODEL_WIDTH]
    ).astype(jnp.bfloat16)
    output = (
        dense(head_input, head_condition_table[:, 2 * MODEL_WIDTH :]) + side_bias[7 * MODEL_WIDTH :]
    )

    def objective(result):
        return loss_terms(result, output, target, loss_weights, upper_log, lower_log, mean_gap)

    loss_part, loss_pull = jax.vjp(objective, output)
    loss_sum, weight_total = lax.psum((loss_part, jnp.sum(loss_weights)), "dp")
    (seed_grad,) = loss_pull(jnp.ones_like(loss_part) / weight_total)
    input_weight, output_weight, condition_vectors, head_condition_table = fetch_weights()
    d_out = seed_grad.astype(jnp.bfloat16)
    g_head = weight_grad(head_input, d_out)
    d_headin = back_dense(d_out, head_condition_table[:, 2 * MODEL_WIDTH :])
    d_fshift = jnp.sum(d_headin, 1)
    d_fscale = jnp.sum(d_headin * normed_f, 1)
    d_final = norm_back(d_headin * (1.0 + final_mod[:, None, MODEL_WIDTH:]), normed_f, inv_std_f)
    d_fmod = jnp.concatenate([d_fshift, d_fscale], 1).astype(jnp.bfloat16)
    g_fada = weight_grad(signal, d_fmod)
    d_signal = back_dense(d_fmod, head_condition_table[:, : 2 * MODEL_WIDTH])
    d_branch = (modulation_part(5) * d_final).astype(jnp.bfloat16)
    d_gate2 = jnp.sum(d_final * branch_output, 1)
    g_down = weight_grad(active, d_branch)
    d_active = back_dense(d_branch, output_weight[query_width:])
    d_hidden = (d_active * gelu_slope(hidden_activations)).astype(jnp.bfloat16)
    g_up = weight_grad(perceptron_input, d_hidden)
    d_mlpin = across_model(back_dense(d_hidden, input_weight[:, 3 * query_width : adaptive_column]))
    d_shift2 = jnp.sum(d_mlpin, 1)
    d_scale2 = jnp.sum(d_mlpin * normed_m, 1)
    d_middle = d_final + norm_back(d_mlpin * (1.0 + modulation_part(4)), normed_m, inv_std_m)
    d_attn = (modulation_part(2) * d_middle).astype(jnp.bfloat16)
    d_gate1 = jnp.sum(d_middle * attention_output, 1)
    g_outp = weight_grad(merged_head_outputs, d_attn)
    d_mixed = heads_of(back_dense(d_attn, output_weight[:query_width]).astype(jnp.bfloat16))
    attn_probs = jnp.exp(score_of() - log_total)
    d_values = jnp.einsum(
        "shlm,slhe->smhe",
        attn_probs.astype(jnp.bfloat16),
        d_mixed,
        preferred_element_type=jnp.float32,
    ).astype(jnp.bfloat16)
    d_probs = jnp.einsum("slhe,smhe->shlm", d_mixed, values, preferred_element_type=jnp.float32)
    d_scores = (attn_probs * (d_probs - jnp.sum(d_probs * attn_probs, -1, keepdims=True))).astype(
        jnp.bfloat16
    )
    d_query = (
        jnp.einsum("shlm,smhe->slhe", d_scores, key_heads, preferred_element_type=jnp.float32)
        * score_scale
    ).astype(jnp.bfloat16)
    d_keys = (
        jnp.einsum("shlm,slhe->smhe", d_scores, queries, preferred_element_type=jnp.float32)
        * score_scale
    ).astype(jnp.bfloat16)
    flat_q = d_query.reshape(batch_rows, seq_len, query_width)
    flat_v = d_values.reshape(batch_rows, seq_len, query_width)
    d_proj = jnp.concatenate([flat_q, d_keys.reshape(batch_rows, seq_len, query_width), flat_v], 2)
    g_qkv = weight_grad(attention_input, d_proj)
    d_attnin = across_model(back_dense(d_proj, input_weight[:, : 3 * query_width]))
    d_shift1 = jnp.sum(d_attnin, 1)
    d_scale1 = jnp.sum(d_attnin * normed_a, 1)
    d_start = (
        d_middle + norm_back(d_attnin * (1.0 + modulation_part(1)), normed_a, inv_std_a)
    ).astype(jnp.bfloat16)
    d_modfull = jnp.concatenate([d_shift1, d_scale1, d_gate1, d_shift2, d_scale2, d_gate2], 1)
    d_modul = lax.dynamic_slice_in_dim(
        d_modfull, lax.axis_index("mp") * ada_width, ada_width, 1
    ).astype(jnp.bfloat16)
    g_ada = weight_grad(signal, d_modul)
    d_signal = d_signal + across_model(back_dense(d_modul, input_weight[:, adaptive_column:]))
    d_cond = d_signal * swish_slope(cond_vec)
    d_second = d_cond.astype(jnp.bfloat16)
    g_second = weight_grad(first_s, d_second)
    d_first = (
        back_dense(d_second, condition_vectors[t2_row:class_row]) * swish_slope(first_t)
    ).astype(jnp.bfloat16)
    g_first = weight_grad(time_freq, d_first)
    g_patch = weight_grad(latent_patches, d_start)
    g_inside = jnp.concatenate([g_qkv, g_up, g_ada], 1)
    g_outside = jnp.concatenate([g_outp, g_down], 0)
    split_pieces = jnp.concatenate(
        [
            split_blocks(g_inside, row_blocks, col_blocks),
            split_blocks(g_outside, out_blocks, row_blocks),
        ],
        0,
    )
    slot_grad = (
        jnp.zeros((slot_of_block.shape[0], BLOCK_SIDE, BLOCK_SIDE), jnp.float32)
        .at[slot_of_block[:occupied_blocks]]
        .set(split_pieces)
    )
    g_headall = jnp.concatenate([g_fada, g_head], 1)
    g_slice = jnp.concatenate(
        [total_of(flat_q), total_of(flat_v), total_of(d_hidden), total_of(d_modul)], 0
    )
    g_side = jnp.concatenate(
        [
            total_of(d_start),
            total_of(d_first),
            total_of(d_second),
            total_of(d_attn),
            total_of(d_branch),
            total_of(d_fmod),
            total_of(d_out),
        ],
        0,
    )
    g_class = jnp.einsum(
        "sc,sd->cd", onehot.astype(jnp.float32), d_cond, precision=exact_precision_flag
    )
    g_cond = jnp.concatenate([g_patch, g_first, g_second, g_class], 0)
    red_blocks, red_cond, red_head = (
        lax.psum_scatter(slot_grad, "dp", scatter_dimension=0, tiled=True),
        lax.psum_scatter(g_cond, "dp", scatter_dimension=1, tiled=True),
        lax.psum_scatter(g_headall, "dp", scatter_dimension=0, tiled=True),
    )
    red_slice, red_side = lax.psum((g_slice, g_side), "dp")
    local_squares = (
        jnp.sum(red_blocks * red_blocks)
        + (jnp.sum(red_cond * red_cond) + jnp.sum(red_head * red_head)) / model_parallel_ways
        + jnp.sum(red_slice * red_slice) / data_ways
        + jnp.sum(red_side * red_side) / (data_ways * model_parallel_ways)
    )
    grad_norm = jnp.sqrt(lax.psum(local_squares, ("dp", "mp")))
    clip_factor = 1.0 / jnp.maximum(grad_norm, 1.0)
    clipped = red_blocks * clip_factor
    flipped = jnp.swapaxes(clipped, -1, -2)
    old_stats = statistics[0]
    left_stat = 0.5 * old_stats[:, 0] + 0.5 * matmul(clipped, flipped)
    right_stat = 0.5 * old_stats[:, 1] + 0.5 * matmul(flipped, clipped)
    new_stats = jnp.stack([left_stat, right_stat], 1)
    inverse_roots = inverse_root(new_stats)
    direction = matmul(matmul(inverse_roots[:, 0], clipped), inverse_roots[:, 1])
    old_blocks = slotted_block_weights[0]
    new_blocks = old_blocks - shampoo_rate * (direction + decay_rate * old_blocks)
    cond_one, cond_two, new_cond = adam_update(cond_tables, red_cond * clip_factor, cond_m, cond_v)
    head_one, head_two, new_head = adam_update(head_tables, red_head * clip_factor, head_m, head_v)
    slice_one, slice_two, new_slice = adam_update(
        slice_bias[0], red_slice * clip_factor, slice_m[0], slice_v[0]
    )
    side_one, side_two, new_side = adam_update(side_bias, red_side * clip_factor, side_m, side_v)
    return (
        loss_sum,
        weight_total,
        grad_norm,
        clipped[None],
        new_stats[None],
        new_blocks[None],
        new_blocks[None].astype(jnp.bfloat16),
        cond_one,
        cond_two,
        new_cond,
        new_cond.astype(jnp.bfloat16),
        head_one,
        head_two,
        new_head,
        new_head.astype(jnp.bfloat16),
        slice_one[None],
        slice_two[None],
        new_slice[None],
        side_one,
        side_two,
        new_side,
    )


def solution(mesh):
    return jax.shard_map(
        per_device,
        mesh=mesh,
        in_specs=(
            P("dp", None, None, None),
            P("dp", None, None, None),
            P("dp"),
            P("dp"),
            P("dp"),
            P("mp", "dp", None, None),
            P("mp", "dp", None, None, None),
            P(),
            P(None, "dp"),
            P("dp", None),
            P("mp", None),
            P(),
            P(None, "dp"),
            P(None, "dp"),
            P("dp", None),
            P("dp", None),
            P("mp", None),
            P("mp", None),
            P(),
            P(),
        ),
        out_specs=(
            P(),
            P(),
            P(),
            P("mp", "dp", None, None),
            P("mp", "dp", None, None, None),
            P("mp", "dp", None, None),
            P("mp", "dp", None, None),
            P(None, "dp"),
            P(None, "dp"),
            P(None, "dp"),
            P(None, "dp"),
            P("dp", None),
            P("dp", None),
            P("dp", None),
            P("dp", None),
            P("mp", None),
            P("mp", None),
            P("mp", None),
            P(),
            P(),
            P(),
        ),
        check_vma=False,
    )
```

profile of v0, /device:TPU:0, one launch (start us, length us, event | category | flops | bytes accessed | tf_op | source)
XLA Modules:
  0.0 2399.7 jit_solution(9281876301725216699)
XLA Ops:
  20.0 84.2 %all-gather.5.cloned.1.call-done = bf16[2425,1152]{0,1:T(8,128)(2,1)} async-done(((bf16[2425,144]{0,1:T(8,128)(2,1)}), bf16[2425,1152]{0,1:T(8,128)(2,1)}) %all-gather.5.cloned.1.call-update) | async-done | bytes 5587216 | tf_op jit(solution)/shard_map/all_gather | solution.py:238
  112.2 210.2 %all-gather.7.cloned.1.call-done = bf16[72,288,288]{2,1,0:T(8,128)(2,1)} async-done(((bf16[9,288,288]{2,1,0:T(8,128)(2,1)}), bf16[72,288,288]{2,1,0:T(8,128)(2,1)}) %all-gather.7.cloned.1.call-update) | async-done | bytes 11943952 | tf_op jit(solution)/shard_map/all_gather | solution.py:237
  322.4 13.2 gather_fusion
  335.6 26.8 %copy.281 = bf16[4,13,288,288]{2,0,3,1:T(4,128)(2,1)} copy(bf16[4,13,288,288]{3,2,1,0:T(8,128)(2,1)} %bitcast.224) | data formatting | bytes 17252352 | tf_op jit(solution)/shard_map/reshape | solution.py:134
  362.3 18.4 reshape.320
  434.9 83.1 %all-reduce.9.cloned.1.call-done = f32[4,256,1152]{2,1,0:T(8,128)} async-done(((f32[4,256,1152]{2,1,0:T(8,128)}), f32[4,256,1152]{2,1,0:T(8,128)}) %all-reduce.9.cloned.1.call-update) | async-done | bytes 4718608 | tf_op jit(solution)/shard_map/psum | solution.py:246
  542.5 68.9 %all-gather.9.cloned.1.call-done = bf16[1152,2336]{1,0:T(8,128)(2,1)} async-done(((bf16[144,2336]{1,0:T(8,128)(2,1)}), bf16[1152,2336]{1,0:T(8,128)(2,1)}) %all-gather.9.cloned.1.call-update) | async-done | bytes 5382160 | tf_op jit(solution)/shard_map/all_gather | solution.py:239
  614.8 91.1 %all-reduce.11.cloned.1.call-done = f32[4,256,1152]{2,1,0:T(8,128)} async-done(((f32[4,256,1152]{2,1,0:T(8,128)}), f32[4,256,1152]{2,1,0:T(8,128)}) %all-reduce.11.cloned.1.call-update) | async-done | bytes 4718608 | tf_op jit(solution)/shard_map/psum | solution.py:246
  714.4 22.0 psum.73
  760.5 89.9 %all-reduce.13.cloned.1.call-done = f32[4,256,1152]{2,1,0:T(8,128)} async-done(((f32[4,256,1152]{2,1,0:T(8,128)}), f32[4,256,1152]{2,1,0:T(8,128)}) %all-reduce.13.cloned.1.call-update) | async-done | bytes 4718608 | tf_op jit(solution)/shard_map/psum | solution.py:246
  892.5 81.9 %all-reduce.15.cloned.1.call-done = f32[4,256,1152]{2,1,0:T(8,128)} async-done(((f32[4,256,1152]{2,1,0:T(8,128)}), f32[4,256,1152]{2,1,0:T(8,128)}) %all-reduce.15.cloned.1.call-update) | async-done | bytes 4718608 | tf_op jit(solution)/shard_map/psum | solution.py:246
  990.1 11.3 psum.76
  1018.0 13.3 copy.341
  1049.7 11.0 reshape.332
  1080.0 25.2 %reshape.330 = f32[4,288,13,288]{1,0,3,2:T(4,128)} reshape(f32[1152,3744]{0,1:T(8,128)} %pad_maximum_fusion.1) | data formatting | bytes 34504704 | tf_op jit(solution)/shard_map/reshape | solution.py:142
  1105.2 32.8 %copy.292 = f32[4,13,288,288]{3,2,1,0:T(8,128)} copy(f32[4,13,288,288]{2,0,3,1:T(4,128)} %bitcast.220) | data formatting | bytes 34504704 | tf_op jit(solution)/shard_map/transpose | solution.py:143
  1138.0 24.3 %pad_maximum_fusion = f32[72,288,288]{2,1,0:T(8,128)} fusion(f32[20,288,288]{2,1,0:T(8,128)} %bitcast.228, f32[52,288,288]{2,1,0:T(8,128)} %bitcast.221), kind=kLoop, calls=%fused_computation.3 | loop fusion | flops 5971968 | bytes 47775744 | tf_op jit(solution)/shard_map/concatenate | solution.py:429
  1173.0 62.0 %scatter_fusion = f32[72,288,288]{2,1,0:T(8,128)} fusion(f32[72,288,288]{2,1,0:T(8,128)} %broadcast_in_dim.39, s32[72]{0:T(128)S(1)} %copy-done.125, f32[72,288,288]{2,1,0:T(8,128)} %pad_maximum_fusion), kind=kCustom, calls=%fused_computation.2 | custom fusion | bytes 71663904 | tf_op jit(solution)/shard_map/scatter | solution.py:439
  1243.9 40.3 %all-reduce.3 = (f32[]{:T(128)}, f32[3456]{0:T(1024)S(1)}, f32[8096]{0:T(1024)S(1)}) all-reduce(f32[]{:T(128)} %get-tuple-element.164, f32[3456]{0:T(1024)S(1)} %concatenate.56, f32[8096]{0:T(1024)S(1)} %constant_dynamic-update-slice_fusion.12), channel_id=1, replica_groups=mesh['dp'=8,'mp'=4] {'dp'}, use_global_device_ids=true, to_apply=%region_18.19 | all-reduce | flops 11553 | bytes 92424 | tf_op jit(solution)/shard_map/psum | solution.py:358
  1289.1 71.0 %reduce-scatter.10.cloned.1.call-done = f32[144,2425]{1,0:T(8,128)} async-done(((f32[1152,2425]{1,0:T(8,128)}), f32[144,2425]{1,0:T(8,128)}) %reduce-scatter.10.cloned.1.call-update) | async-done | bytes 1396816
  1364.9 510.4 %reduce-scatter.6.cloned.1.call-done = f32[9,288,288]{2,1,0:T(8,128)} async-done(((f32[72,288,288]{2,1,0:T(8,128)}), f32[9,288,288]{2,1,0:T(8,128)}) %reduce-scatter.6.cloned.1.call-update) | async-done | bytes 2986000 | tf_op jit(solution)/shard_map/reduce_scatter | solution.py:462
  1880.4 39.5 %psum.79 = f32[]{:T(128)} all-reduce(f32[]{:T(128)S(6)} %add.473), channel_id=1, replica_groups=mesh['dp'=8,'mp'=4] {'dp','mp'}, use_global_device_ids=true, to_apply=%region_61.62 | all-reduce | flops 1 | bytes 8 | tf_op jit(solution)/shard_map/psum | solution.py:473
  1920.6 14.1 fusion.50
  1934.8 11.8 fusion.47
  1949.4 11.7 subtract_multiply_fusion.3
  1961.1 16.9 fusion.29
  1978.1 16.5 fusion.178
  1994.6 19.0 fusion.8
  2013.6 17.4 fusion.25
  2031.0 18.3 fusion.179
  2049.3 19.2 fusion.180
  2068.5 17.2 fusion.21
  2085.7 18.2 fusion.181
  2104.0 19.0 fusion.182
  2123.0 18.4 fusion.16
  2141.4 21.1 fusion.183
  2162.5 22.4 subtract_multiply_fusion.1
  2184.9 19.5 fusion.12
  2204.4 17.9 fusion
  2222.3 19.3 fusion.10
  2241.7 17.8 fusion.27
  2259.4 19.1 fusion.23
  2278.6 16.6 fusion.18
  2295.2 17.1 fusion.14
  2312.3 19.3 subtract_multiply_fusion
  2331.7 16.8 fusion.4
  2348.6 10.7 fusion.44
  2359.3 11.2 bitcast_subtract_fusion
  (503 shorter events, 299.8 us)
Async XLA Ops:
  7.2 97.0 %all-gather.5.cloned.1.call-start = ((), (), s32[]{:S(2)}) async-start(), calls=%async_computation.3 | async-start | bytes 6303744 | tf_op jit(solution)/shard_map/all_gather | solution.py:238
  9.6 312.8 %all-gather.7.cloned.1.call-start = ((), (), s32[]{:S(2)}) async-start(), calls=%async_computation.4 | async-start | bytes 17915904 | tf_op jit(solution)/shard_map/all_gather | solution.py:237
  13.4 504.6 %all-reduce.9.cloned.1.call-start = ((), (), s32[]{:S(2)}) async-start(), calls=%async_computation.5 | async-start | bytes 9437184 | tf_op jit(solution)/shard_map/psum | solution.py:246
  18.3 88.0 %copy-start.53 = (bf16[4,256,16]{1,2,0:T(8,128)(2,1)}, bf16[4,256,16]{1,2,0:T(8,128)(2,1)S(1)}, u32[]{:S(2)}) copy-start(bf16[4,256,16]{1,2,0:T(8,128)(2,1)S(1)} %convert_element_type.221) | copy-start | bytes 98308
  19.0 90.1 %copy-start.107 = (bf16[4,128]{1,0:T(4,128)(2,1)}, bf16[4,128]{1,0:T(4,128)(2,1)S(1)}, u32[]{:S(2)}) copy-start(bf16[4,128]{1,0:T(4,128)(2,1)S(1)} %get-tuple-element.228) | copy-start | bytes 3076
  19.0 90.1 %copy-start.109 = (bf16[4,128]{1,0:T(4,128)(2,1)}, bf16[4,128]{1,0:T(4,128)(2,1)S(1)}, u32[]{:S(2)}) copy-start(bf16[4,128]{1,0:T(4,128)(2,1)S(1)} %get-tuple-element.229) | copy-start | bytes 3076
  106.3 284.1 %copy-start.73 = (f32[4,256]{1,0:T(4,128)}, f32[4,256]{1,0:T(4,128)S(1)}, u32[]{:S(2)}) copy-start(f32[4,256]{1,0:T(4,128)S(1)} %broadcast_multiply_fusion.9) | copy-start | bytes 12292
  109.1 281.3 %copy-start.86 = (f32[4,256]{1,0:T(4,128)}, f32[4,256]{1,0:T(4,128)S(1)}, u32[]{:S(2)}) copy-start(f32[4,256]{1,0:T(4,128)S(1)} %add_rsqrt_fusion.2) | copy-start | bytes 12292
  112.2 268.5 %copy-start.51 = (f32[4,1152]{1,0:T(4,128)}, f32[4,1152]{1,0:T(4,128)S(1)}, u32[]{:S(2)}) copy-start(f32[4,1152]{1,0:T(4,128)S(1)} %fusion.75) | copy-start | bytes 55300
  398.5 19.0 copy-start.26
  425.6 185.8 %all-gather.9.cloned.1.call-start = ((), (), s32[]{:S(2)}) async-start(), calls=%async_computation.7 | async-start | bytes 6303744 | tf_op jit(solution)/shard_map/all_gather | solution.py:239
  426.6 279.3 %all-reduce.11.cloned.1.call-start = ((), (), s32[]{:S(2)}) async-start(), calls=%async_computation.6 | async-start | bytes 9437184 | tf_op jit(solution)/shard_map/psum | solution.py:246
  522.6 332.8 %copy-start.82 = (f32[4,256]{1,0:T(4,128)}, f32[4,256]{1,0:T(4,128)S(1)}, u32[]{:S(2)}) copy-start(f32[4,256]{1,0:T(4,128)S(1)} %broadcast_multiply_fusion.8) | copy-start | bytes 12292
  523.2 332.2 %copy-start.93 = (f32[4,256]{1,0:T(4,128)}, f32[4,256]{1,0:T(4,128)S(1)}, u32[]{:S(2)}) copy-start(f32[4,256]{1,0:T(4,128)S(1)} %add_rsqrt_fusion.1) | copy-start | bytes 12292
  537.6 73.8 %copy-start.52 = (f32[4,1152]{1,0:T(4,128)S(1)}, f32[4,1152]{1,0:T(4,128)}, u32[]{:S(2)}) copy-start(f32[4,1152]{1,0:T(4,128)} %copy-done.51) | copy-start | bytes 55300
  537.7 312.8 %all-reduce.13.cloned.1.call-start = ((), (), s32[]{:S(2)}) async-start(), calls=%async_computation.8 | async-start | bytes 9437184 | tf_op jit(solution)/shard_map/psum | solution.py:246
  540.1 165.8 %copy-start.62 = (f32[4,1152]{1,0:T(4,128)S(1)}, f32[4,1152]{1,0:T(4,128)}, u32[]{:S(2)}) copy-start(f32[4,1152]{1,0:T(4,128)} %get-tuple-element.209) | copy-start | bytes 55300
  540.1 165.8 %copy-start.70 = (f32[1152]{0:T(1024)S(1)}, f32[1152]{0:T(1024)}, u32[]{:S(2)}) copy-start(f32[1152]{0:T(1024)} %get-tuple-element.217) | copy-start | bytes 13828
  710.5 26.6 %copy-start.120 = (f32[4]{0:T(128)S(1)}, f32[4]{0:T(128)}, u32[]{:S(2)}) copy-start(f32[4]{0:T(128)} %get-tuple-element.232) | copy-start | bytes 52
  737.3 142.8 %copy-start.56 = (f32[4,256,4,4]{1,3,2,0:T(4,128)}, f32[4,256,4,4]{1,3,2,0:T(4,128)S(1)}, u32[]{:S(2)}) copy-start(f32[4,256,4,4]{1,3,2,0:T(4,128)S(1)} %get-tuple-element.207) | copy-start | bytes 196612
  737.3 142.8 %copy-start.58 = (f32[4,256,4,4]{1,3,2,0:T(4,128)}, f32[4,256,4,4]{1,3,2,0:T(4,128)S(1)}, u32[]{:S(2)}) copy-start(f32[4,256,4,4]{1,3,2,0:T(4,128)S(1)} %get-tuple-element.208) | copy-start | bytes 196612
  741.8 259.9 %copy-start.89 = (bf16[4,1152]{1,0:T(4,128)(2,1)}, bf16[4,1152]{1,0:T(4,128)(2,1)S(1)}, u32[]{:S(2)}) copy-start(bf16[4,1152]{1,0:T(4,128)(2,1)S(1)} %get-tuple-element.149) | copy-start | bytes 27652
  741.8 259.9 %copy-start.91 = (bf16[4,1152]{1,0:T(4,128)(2,1)}, bf16[4,1152]{1,0:T(4,128)(2,1)S(1)}, u32[]{:S(2)}) copy-start(bf16[4,1152]{1,0:T(4,128)(2,1)S(1)} %get-tuple-element.157) | copy-start | bytes 27652
  759.8 214.6 %all-reduce.15.cloned.1.call-start = ((), (), s32[]{:S(2)}) async-start(), calls=%async_computation.9 | async-start | bytes 9437184 | tf_op jit(solution)/shard_map/psum | solution.py:246
  760.5 94.9 %copy-start.66 = (f32[4,1152]{1,0:T(4,128)S(1)}, f32[4,1152]{1,0:T(4,128)}, u32[]{:S(2)}) copy-start(f32[4,1152]{1,0:T(4,128)} %get-tuple-element.214) | copy-start | bytes 55300
  880.0 406.7 %reduce-scatter.8.cloned.1.call-start = ((), (), s32[]{:S(2)}) async-start(), calls=%async_computation.11 | async-start | bytes 12607488 | tf_op jit(solution)/shard_map/reduce_scatter | solution.py:464
  892.0 82.4 %copy-start.64 = (f32[4,1152]{1,0:T(4,128)S(1)}, f32[4,1152]{1,0:T(4,128)}, u32[]{:S(2)}) copy-start(f32[4,1152]{1,0:T(4,128)} %copy-done.63) | copy-start | bytes 55300
  892.0 82.4 %copy-start.74 = (f32[4,256]{1,0:T(4,128)S(1)}, f32[4,256]{1,0:T(4,128)}, u32[]{:S(2)}) copy-start(f32[4,256]{1,0:T(4,128)} %copy-done.73) | copy-start | bytes 12292
  892.0 82.4 %copy-start.87 = (f32[4,256]{1,0:T(4,128)S(1)}, f32[4,256]{1,0:T(4,128)}, u32[]{:S(2)}) copy-start(f32[4,256]{1,0:T(4,128)} %copy-done.86) | copy-start | bytes 12292
  892.0 468.0 %reduce-scatter.10.cloned.1.call-start = ((), (), s32[]{:S(2)}) async-start(), calls=%async_computation.12 | async-start | bytes 12607488
  892.5 86.8 %copy-start.69 = (f32[1152]{0:T(1024)S(1)}, f32[1152]{0:T(1024)}, u32[]{:S(2)}) copy-start(f32[1152]{0:T(1024)} %get-tuple-element.218) | copy-start | bytes 13828
  979.5 21.8 copy-start.54
  1031.3 844.0 %reduce-scatter.6.cloned.1.call-start = ((), (), s32[]{:S(2)}) async-start(), calls=%async_computation.10 | async-start | bytes 35831808 | tf_op jit(solution)/shard_map/reduce_scatter | solution.py:462
  1049.7 19.4 slice-start.4
  1243.2 770.4 %copy-start.6 = (f32[288,288]{1,0:T(8,128)}, f32[288,288]{1,0:T(8,128)S(1)}, u32[]{:S(2)}) copy-start(f32[288,288]{1,0:T(8,128)S(1)} %fusion.126) | copy-start | bytes 995332
  1284.2 75.9 %copy-start.67 = (f32[8096]{0:T(1024)}, f32[8096]{0:T(1024)S(1)}, u32[]{:S(2)}) copy-start(f32[8096]{0:T(1024)S(1)} %get-tuple-element.170) | copy-start | bytes 97156
  1284.2 75.9 %copy-start.77 = (f32[3456]{0:T(1024)}, f32[3456]{0:T(1024)S(1)}, u32[]{:S(2)}) copy-start(f32[3456]{0:T(1024)S(1)} %get-tuple-element.169) | copy-start | bytes 41476
  1360.1 519.6 %copy-start.85 = (f32[1,3456]{1,0:T(1,128)S(1)}, f32[1,3456]{1,0:T(1,128)}, u32[]{:S(2)}) copy-start(f32[1,3456]{1,0:T(1,128)} %param.30) | copy-start | bytes 41476
  1961.1 17.0 copy-start.3
  2049.3 19.2 copy-start.7
  2123.0 18.4 copy-start
  2184.9 37.4 %slice-start.6 = ((s8[7962624]{0:T(1024)(128)(4,1)}), s8[4194304]{0:T(1024)(128)(4,1)S(1)}, s32[]{:S(2)}) async-start(s8[7962624]{0:T(1024)(128)(4,1)} %bitcast.216), calls=%async_computation.19 | async-start | bytes 8388608
  2184.9 37.4 %slice-start.7 = ((s8[7962624]{0:T(1024)(128)(4,1)}), s8[3768320]{0:T(1024)(128)(4,1)S(1)}, s32[]{:S(2)}) async-start(s8[7962624]{0:T(1024)(128)(4,1)} %bitcast.216), calls=%async_computation.20 | async-start | bytes 7536640
  2222.3 19.3 copy-start.8
  2241.6 36.9 %slice-start = ((s8[7962624]{0:T(1024)(128)(4,1)}), s8[4194304]{0:T(1024)(128)(4,1)S(1)}, s32[]{:S(2)}) async-start(s8[7962624]{0:T(1024)(128)(4,1)} %bitcast.210), calls=%async_computation.13 | async-start | bytes 8388608
  2259.4 19.1 slice-start.1
  2259.4 35.8 %slice-start.8 = ((s8[7962624]{0:T(1024)(128)(4,1)}), s8[4194304]{0:T(1024)(128)(4,1)S(1)}, s32[]{:S(2)}) async-start(s8[7962624]{0:T(1024)(128)(4,1)} %bitcast.218), calls=%async_computation.21 | async-start | bytes 8388608
  2348.5 27.3 %slice-start.12 = ((s8[7962624]{0:T(1024)(128)(4,1)}), s8[4194304]{0:T(1024)(128)(4,1)S(1)}, s32[]{:S(2)}) async-start(s8[7962624]{0:T(1024)(128)(4,1)} %bitcast.231), calls=%async_computation.25 | async-start | bytes 8388608
  (112 other events, 625.5 us)
Sparse Core Ops, SparseCore 0:
  10.8 93.3 all-gather.4
  107.0 215.3 all-gather.6
  425.7 92.1 all-reduce.8
  520.6 90.8 all-gather.8
  613.6 92.1 all-reduce.10
  759.9 90.4 all-reduce.12
  880.2 94.1 all-reduce.14
  978.1 188.7 reduce-scatter.7
  1171.0 189.0 reduce-scatter.9
  1363.8 511.4 reduce-scatter.5
where the time goes:
time: 2410 us; the launch traced here: 2400 us
  waiting for transfers between devices  1290 us (54%)
  matrix products  538 us (22%)
  local copies, waits for them, and re-layouts  290 us (12%)
  other arithmetic  138 us (6%)
  blocking collectives  119 us (5%)
    reduce_scatter x1, waiting for transfers between devices, per_device(): lax.psum_scatter(slot_grad, 'dp', scatter_dimension=0, tiled=True)  510 us
    dot_general x25, matrix products, matmul(): return jnp.matmul(operand, other, precision=exact_precision_flag)  435 us
    psum x4, waiting for transfers between devices, across_model(): return lax.psum(inputs, 'mp')  346 us
    all_gather x1, waiting for transfers between devices, fetch_weights(): lax.all_gather(slotted_block_weights[0].astype(jnp.bfloat16), 'dp', axis=...  210 us
    all_gather x1, waiting for transfers between devices, fetch_weights(): lax.all_gather(cond_tables.astype(jnp.bfloat16), 'dp', axis=1, tiled=True)  84.2 us
    unnamed x11, waiting for transfers between devices  71.2 us
    all_gather x1, waiting for transfers between devices, fetch_weights(): lax.all_gather(head_tables.astype(jnp.bfloat16), 'dp', axis=0, tiled=True)  68.9 us
    psum x2, blocking collectives, per_device(): loss_sum, weight_total = lax.psum((loss_part, jnp.sum(loss_weights)), 'dp')  62.3 us
  transfers between devices with their start and end apart: 10, of which 9 were waited for; matrix products, arithmetic and copies ran while one was open for 14% of the time, Pallas kernels for 0%

commit v1 on v0

v1 whole, which is shorter than its diff:
```python
import math

import jax
import jax.numpy as jnp
from jax import lax
from jax.experimental import pallas as pl
from jax.experimental.pallas import tpu as pltpu
from jax.sharding import PartitionSpec as P

MODEL_WIDTH = 1152
HEADS = 16
HD = 72
FF = 4608
FREQ = 256
CLASSES = 1001
LATENT_SIDE = 32
PATCH_VALUES = 16
BLOCK_SIDE = 288
NEWTON = 6
STEP = 5
LANES = 256
TAIL = BLOCK_SIDE - LANES


exact_precision_flag = lax.Precision.HIGHEST
shampoo_rate = 0.5
adam_rate = 0.05
decay_rate = 0.01


def dense(operand, weight):
    return jnp.dot(operand, weight, preferred_element_type=jnp.float32)


def back_dense(gradient, weight):
    return jnp.einsum("...j,ij->...i", gradient, weight, preferred_element_type=jnp.float32)


def weight_grad(operand, gradient):
    return jnp.einsum("...i,...j->ij", operand, gradient, preferred_element_type=jnp.float32)


def total_of(inputs):
    return jnp.sum(inputs.astype(jnp.float32), axis=tuple(range(inputs.ndim - 1)))


def swish_unit(inputs):
    return inputs / (1.0 + jnp.exp(-inputs))


def swish_slope(inputs):
    sigmoid = 1.0 / (1.0 + jnp.exp(-inputs))
    return sigmoid * (1.0 + inputs * (1.0 - sigmoid))


def tanh_gelu_activation(inputs):
    return (
        0.5
        * inputs
        * (1.0 + jnp.tanh(0.7978845608028654 * (inputs + 0.044715 * inputs * inputs * inputs)))
    )


def gelu_slope(inputs):
    inner = jnp.tanh(0.7978845608028654 * (inputs + 0.044715 * inputs * inputs * inputs))
    return 0.5 * (1.0 + inner) + 0.5 * inputs * (1.0 - inner * inner) * 0.7978845608028654 * (
        1.0 + 3.0 * 0.044715 * inputs * inputs
    )


def layer_norm(inputs):
    centred = inputs - jnp.mean(inputs, -1, keepdims=True)
    inv_std = lax.rsqrt(jnp.mean(centred * centred, -1, keepdims=True) + 1e-06)
    return (centred * inv_std, inv_std)


def norm_back(gradient, normed, inv_std):
    return inv_std * (
        gradient
        - jnp.mean(gradient, -1, keepdims=True)
        - normed * jnp.mean(gradient * normed, -1, keepdims=True)
    )


def coefficients(step_ids):
    grid = jnp.arange(1000).astype(jnp.float32)
    betas = 0.0001 + (0.02 - 0.0001) * grid / 999.0
    logs = jnp.log(1.0 - betas)[None, :]
    index = jnp.arange(1000, dtype=jnp.int32)[None, :]
    beta_t = 0.0001 + (0.02 - 0.0001) * step_ids.astype(jnp.float32) / 999.0
    cumul_t = jnp.exp(jnp.sum(jnp.where(index <= step_ids[:, None], logs, 0.0), 1))
    before_t = jnp.exp(jnp.sum(jnp.where(index < step_ids[:, None], logs, 0.0), 1))
    keep_rate = jnp.sqrt(cumul_t)
    noise_rate = jnp.sqrt(1.0 - cumul_t)
    upper_log = jnp.log(beta_t)
    lower_log = jnp.log(beta_t * (1.0 - before_t) / (1.0 - cumul_t))
    mean_gap = beta_t * jnp.sqrt(before_t) / (1.0 - cumul_t) * jnp.sqrt(1.0 / cumul_t - 1.0)
    return (keep_rate, noise_rate, upper_log, lower_log, mean_gap)


def time_features(step_ids, feat_width):
    half_width = feat_width // 2
    frequencies = jnp.exp(
        -math.log(10000.0) * jnp.arange(half_width).astype(jnp.float32) / half_width
    )
    phases = step_ids.astype(jnp.float32)[:, None] * frequencies[None, :]
    return jnp.concatenate([jnp.cos(phases), jnp.sin(phases)], 1)


def position_embedding(grid_side, feat_width):
    quarter = feat_width // 4
    omegas = jnp.exp(-math.log(10000.0) * jnp.arange(quarter).astype(jnp.float32) / quarter)
    coords = jnp.arange(grid_side).astype(jnp.float32)
    angles = coords[:, None] * omegas[None, :]
    waves = jnp.concatenate([jnp.sin(angles), jnp.cos(angles)], 1)
    half_width = feat_width // 2
    rows_part = jnp.broadcast_to(waves[:, None, :], (grid_side, grid_side, half_width))
    cols_part = jnp.broadcast_to(waves[None, :, :], (grid_side, grid_side, half_width))
    return jnp.concatenate([rows_part, cols_part], 2).reshape(grid_side * grid_side, feat_width)


def patchify(latent):
    samples_n, channels, height, breadth = latent.shape
    shaped = latent.reshape(samples_n, channels, height // 2, 2, breadth // 2, 2).transpose(
        0, 2, 4, 3, 5, 1
    )
    return shaped.reshape(samples_n, height // 2 * (breadth // 2), 4 * channels)


PACK_ROWS = 656


def pack(x):
    quarter = BLOCK_SIDE // 4
    tail = x[:, LANES:].astype(jnp.float32)
    tail = jnp.concatenate([tail[i * quarter : (i + 1) * quarter] for i in range(4)], axis=1)
    fill = jnp.zeros((PACK_ROWS - 2 * BLOCK_SIDE - quarter, LANES // 2), jnp.float32)
    tail = jnp.concatenate([tail, fill], axis=0)
    half = LANES // 2
    return x[:, :half], x[:, half:LANES], tail.astype(x.dtype)


def unpack(x):
    side, quarter = BLOCK_SIDE, BLOCK_SIDE // 4
    tail = x[2 * side :].astype(jnp.float32)[:quarter]
    tail = jnp.concatenate([tail[:, i * TAIL : (i + 1) * TAIL] for i in range(4)], axis=0)
    main = jnp.concatenate([x[:side], x[side : 2 * side]], axis=1)
    return main, tail.astype(x.dtype)


def store_packed(ref, index, x):
    a, b, c = pack(x)
    side = BLOCK_SIDE
    ref[index + (slice(0, side),)] = a
    ref[index + (slice(side, 2 * side),)] = b
    ref[index + (slice(2 * side, PACK_ROWS),)] = c


def pack_blocks(blocks):
    count, side = blocks.shape[0], BLOCK_SIDE

    def body(x_ref, out_ref):
        store_packed(out_ref, (0,), x_ref[0].astype(jnp.bfloat16))

    return pl.pallas_call(
        body,
        grid=(count,),
        in_specs=[pl.BlockSpec((1, side, side), lambda i: (i, 0, 0))],
        out_specs=pl.BlockSpec((1, PACK_ROWS, LANES // 2), lambda i: (i, 0, 0)),
        out_shape=jax.ShapeDtypeStruct((count, PACK_ROWS, LANES // 2), jnp.bfloat16),
        name="pack_blocks",
    )(blocks)


def remote(source, target, send, receive, place):
    return pltpu.make_async_remote_copy(
        src_ref=source,
        dst_ref=target,
        send_sem=send,
        recv_sem=receive,
        device_id=place,
        device_id_type=pl.DeviceIdType.MESH,
    )


def signal_to(semaphore, place):
    pl.semaphore_signal(semaphore, inc=1, device_id=place, device_id_type=pl.DeviceIdType.MESH)


COLUMNS = 2
LAYERS = 4


def grid_place():
    me = lax.axis_index("dp")
    return me // COLUMNS, me % COLUMNS


def greet_neighbours(z, y):
    barrier = pltpu.get_barrier_semaphore()
    signal_to(barrier, {"dp": z * COLUMNS + 1 - y})

    @pl.when(z < LAYERS - 1)
    def _():
        signal_to(barrier, {"dp": (z + 1) * COLUMNS + y})

    @pl.when(z > 0)
    def _():
        signal_to(barrier, {"dp": (z - 1) * COLUMNS + y})

    pl.semaphore_wait(barrier, jnp.where((z > 0) & (z < LAYERS - 1), 3, 2))


def gather_body(x_ref, out_ref, local_sem, up_sem, down_sem, side_sem, recv_sem):
    count = x_ref.shape[0]
    z, y = grid_place()
    greet_neighbours(z, y)
    peer = {"dp": z * COLUMNS + 1 - y}
    above = {"dp": jnp.minimum(z + 1, LAYERS - 1) * COLUMNS + y}
    below = {"dp": jnp.maximum(z - 1, 0) * COLUMNS + y}

    def block(layer, column, k):
        return out_ref.at[(layer * COLUMNS + column) * count + k]

    def move(source, layer, k, send, place):
        return remote(
            source, block(layer, y, k), send.at[layer, k], recv_sem.at[layer, y, k], place
        )

    def arrival(layer, column, k):
        here = block(layer, column, k)
        return remote(here, here, side_sem.at[0, 0], recv_sem.at[layer, column, k], peer)

    def send_own(k, _):
        own = x_ref.at[k]

        @pl.when(z < LAYERS - 1)
        def _():
            move(own, z, k, up_sem, above).start()

        @pl.when(z > 0)
        def _():
            move(own, z, k, down_sem, below).start()

        move(own, z, k, side_sem, peer).start()
        pltpu.make_async_copy(own, block(z, y, k), local_sem.at[k]).start()
        return 0

    lax.fori_loop(0, count, send_own, 0)

    for hop in range(1, LAYERS):

        def pass_on(k, _):
            @pl.when(z >= hop)
            def _():
                layer = z - hop
                arrival(layer, y, k).wait_recv()

                @pl.when(z < LAYERS - 1)
                def _():
                    move(block(layer, y, k), layer, k, up_sem, above).start()

                move(block(layer, y, k), layer, k, side_sem, peer).start()

            @pl.when(z + hop < LAYERS)
            def _():
                layer = z + hop
                arrival(layer, y, k).wait_recv()

                @pl.when(z > 0)
                def _():
                    move(block(layer, y, k), layer, k, down_sem, below).start()

                move(block(layer, y, k), layer, k, side_sem, peer).start()

            return 0

        lax.fori_loop(0, count, pass_on, 0)

    def finish(k, _):
        pltpu.make_async_copy(x_ref.at[k], block(z, y, k), local_sem.at[k]).wait()
        for layer in range(LAYERS):
            arrival(layer, 1 - y, k).wait_recv()
            move(block(layer, y, k), layer, k, side_sem, peer).wait_send()

            @pl.when((z < LAYERS - 1) & (layer <= z))
            def _():
                move(block(layer, y, k), layer, k, up_sem, above).wait_send()

            @pl.when((z > 0) & (layer >= z))
            def _():
                move(block(layer, y, k), layer, k, down_sem, below).wait_send()

        return 0

    lax.fori_loop(0, count, finish, 0)


def gather_blocks(packed):
    ways = lax.axis_size("dp")
    if ways != COLUMNS * LAYERS:
        return lax.all_gather(packed, "dp", axis=0, tiled=True)
    count = packed.shape[0]
    dma = pltpu.SemaphoreType.DMA
    return pl.pallas_call(
        gather_body,
        in_specs=[pl.BlockSpec(memory_space=pl.ANY)],
        out_specs=pl.BlockSpec(memory_space=pl.ANY),
        out_shape=jax.ShapeDtypeStruct((count * ways,) + packed.shape[1:], packed.dtype),
        scratch_shapes=[
            dma((count,)),
            dma((LAYERS, count)),
            dma((LAYERS, count)),
            dma((LAYERS, count)),
            dma((LAYERS, COLUMNS, count)),
        ],
        compiler_params=pltpu.CompilerParams(collective_id=0, has_side_effects=True),
        name="gather_blocks",
    )(packed)


def reduce_body(
    x_ref, out_ref, side_buf, up_buf, down_buf, side_send, line_send, side_recv, up_recv, down_recv
):
    count = out_ref.shape[0]
    z, y = grid_place()
    greet_neighbours(z, y)
    peer = {"dp": z * COLUMNS + 1 - y}
    above = {"dp": jnp.minimum(z + 1, LAYERS - 1) * COLUMNS + y}
    below = {"dp": jnp.maximum(z - 1, 0) * COLUMNS + y}

    def across(layer, k):
        return remote(
            x_ref.at[(layer * COLUMNS + 1 - y) * count + k],
            side_buf.at[layer, k],
            side_send.at[layer, k],
            side_recv.at[layer, k],
            peer,
        )

    def upward(layer, k):
        return remote(
            side_buf.at[layer, k], up_buf.at[layer, k], line_send.at[layer, k], up_recv.at[layer, k], above
        )

    def downward(layer, k):
        return remote(
            side_buf.at[layer, k], down_buf.at[layer, k], line_send.at[layer, k], down_recv.at[layer, k], below
        )

    def pair_sum(layer, k):
        across(layer, k).wait_recv()
        own = x_ref[(layer * COLUMNS + y) * count + k].astype(jnp.float32)
        return own + side_buf[layer, k].astype(jnp.float32)

    for hop in range(LAYERS - 1, -1, -1):

        def start(k, _):
            @pl.when(z + hop < LAYERS)
            def _():
                across(z + hop, k).start()

            if hop > 0:

                @pl.when(z >= hop)
                def _():
                    across(z - hop, k).start()

            return 0

        lax.fori_loop(0, count, start, 0)

    for hop in range(LAYERS - 1, 0, -1):

        def step(k, _):
            @pl.when(z + hop < LAYERS)
            def _():
                layer = z + hop
                total = pair_sum(layer, k)

                @pl.when(z > 0)
                def _():
                    upward(layer, k).wait_recv()
                    side_buf[layer, k] = (total + up_buf[layer, k].astype(jnp.float32)).astype(
                        jnp.bfloat16
                    )

                @pl.when(z == 0)
                def _():
                    side_buf[layer, k] = total.astype(jnp.bfloat16)

                upward(layer, k).start()

            @pl.when(z >= hop)
            def _():
                layer = z - hop
                total = pair_sum(layer, k)

                @pl.when(z < LAYERS - 1)
                def _():
                    downward(layer, k).wait_recv()
                    side_buf[layer, k] = (total + down_buf[layer, k].astype(jnp.float32)).astype(
                        jnp.bfloat16
                    )

                @pl.when(z == LAYERS - 1)
                def _():
                    side_buf[layer, k] = total.astype(jnp.bfloat16)

                downward(layer, k).start()

            return 0

        lax.fori_loop(0, count, step, 0)

    def last(k, _):
        out_ref[k] = pair_sum(z, k)

        @pl.when(z > 0)
        def _():
            upward(z, k).wait_recv()
            out_ref[k] += up_buf[z, k].astype(jnp.float32)

        @pl.when(z < LAYERS - 1)
        def _():
            downward(z, k).wait_recv()
            out_ref[k] += down_buf[z, k].astype(jnp.float32)

        for layer in range(LAYERS):
            across(layer, k).wait_send()

            @pl.when(layer > z)
            def _():
                upward(layer, k).wait_send()

            @pl.when(layer < z)
            def _():
                downward(layer, k).wait_send()

        return 0

    lax.fori_loop(0, count, last, 0)


def reduce_blocks(slots):
    ways = lax.axis_size("dp")
    if ways != COLUMNS * LAYERS:
        return lax.psum_scatter(slots, "dp", scatter_dimension=0, tiled=True).astype(jnp.float32)
    count = slots.shape[0] // ways
    dma = pltpu.SemaphoreType.DMA
    landing = pltpu.VMEM((LAYERS, count) + slots.shape[1:], jnp.bfloat16)
    return pl.pallas_call(
        reduce_body,
        in_specs=[pl.BlockSpec(memory_space=pltpu.VMEM)],
        out_specs=pl.BlockSpec(memory_space=pltpu.VMEM),
        out_shape=jax.ShapeDtypeStruct((count,) + slots.shape[1:], jnp.float32),
        scratch_shapes=[landing] * 3 + [dma((LAYERS, count))] * 5,
        compiler_params=pltpu.CompilerParams(
            collective_id=1, has_side_effects=True, vmem_limit_bytes=52 * 2**20
        ),
        name="reduce_blocks",
    )(slots)


EVERY = ("dp", "mp")


def exchange(items, axes, number):
    mp, dp = lax.axis_size("mp"), lax.axis_size("dp")
    n = {"dp": dp, "mp": mp, EVERY: dp * mp}[axes]

    def place(i):
        return {"dp": i // mp, "mp": i % mp} if axes == EVERY else {axes: i}

    def row(i):
        return i // mp if axes == EVERY else i

    def body(*refs):
        m = len(items)
        sources, outs, send, receive = refs[:m], refs[m : 2 * m], refs[-2], refs[-1]
        me = lax.axis_index("dp") * mp + lax.axis_index("mp") if axes == EVERY else lax.axis_index(axes)
        barrier = pltpu.get_barrier_semaphore()

        def greet(i, _):
            signal_to(barrier, place(lax.rem(me + i, n)))
            return 0

        lax.fori_loop(1, n, greet, 0)
        pl.semaphore_wait(barrier, n - 1)

        def piece(j, to):
            return sources[j].at[row(to)] if items[j][1] == "scatter" else sources[j]

        def start(i, _):
            to = lax.rem(me + i, n)
            for j in range(m):
                remote(piece(j, to), outs[j].at[me], send.at[j, i], receive.at[j, me], place(to)).start()
            return 0

        lax.fori_loop(1, n, start, 0)
        for j in range(m):
            outs[j][me] = sources[j][row(me)] if items[j][1] == "scatter" else sources[j][...]

        def finish(i, _):
            to = lax.rem(me + i, n)
            for j in range(m):
                copy = remote(piece(j, to), outs[j].at[to], send.at[j, i], receive.at[j, to], place(to))
                copy.wait_recv()
                copy.wait_send()
            return 0

        lax.fori_loop(1, n, finish, 0)

    arrays = [a for a, _ in items]
    shapes = [
        jax.ShapeDtypeStruct((n,) + (a.shape[1:] if kind == "scatter" else a.shape), a.dtype)
        for a, kind in items
    ]
    vmem = pl.BlockSpec(memory_space=pltpu.VMEM)
    return pl.pallas_call(
        body,
        in_specs=[vmem] * len(arrays),
        out_specs=[vmem] * len(arrays),
        out_shape=shapes,
        scratch_shapes=[pltpu.SemaphoreType.DMA((len(arrays), n))] * 2,
        compiler_params=pltpu.CompilerParams(
            collective_id=number, has_side_effects=True, vmem_limit_bytes=40 * 2**20
        ),
        name=f"exchange_{number}",
    )(*arrays)


def assemble(blocks, slots, first, rows, cols):
    side = BLOCK_SIDE

    def body(ids, *refs):
        parts = [part for r in refs[:-1] for part in unpack(r[0])]
        refs[-1][...] = jnp.concatenate(parts, axis=1)

    def spec(c):
        return pl.BlockSpec(
            (1, PACK_ROWS, LANES // 2), lambda r, ids: (ids[first + r * cols + c], 0, 0)
        )

    return pl.pallas_call(
        body,
        grid_spec=pltpu.PrefetchScalarGridSpec(
            num_scalar_prefetch=1,
            grid=(rows,),
            in_specs=[spec(c) for c in range(cols)],
            out_specs=pl.BlockSpec((side, side * cols), lambda r, ids: (r, 0)),
        ),
        out_shape=jax.ShapeDtypeStruct((rows * side, cols * side), jnp.bfloat16),
        compiler_params=pltpu.CompilerParams(vmem_limit_bytes=40 * 2**20),
        cost_estimate=pl.CostEstimate(
            flops=0, bytes_accessed=4 * rows * cols * side * side, transcendentals=0
        ),
        name="assemble",
    )(slots, *([blocks] * cols))


def to_slots(g_in, g_out, slots, total):
    side = BLOCK_SIDE
    ri, ci = g_in.shape[0] // side, g_in.shape[1] // side
    ro, co = g_out.shape[0] // side, g_out.shape[1] // side
    steps = ri + ro

    def body(ids, gi, go, *rest):
        out, buf, sem = rest[-3:]
        s = pl.program_id(0)
        half = lax.rem(s, 2)

        def drain(which, count):
            for c in range(count):
                pltpu.make_async_copy(buf.at[which, c], out.at[0], sem.at[which, c]).wait()

        def send(source, count, base):
            for c in range(count):
                store_packed(buf, (half, c), source[:, c * side : (c + 1) * side])
                pltpu.make_async_copy(
                    buf.at[half, c], out.at[ids[base + c]], sem.at[half, c]
                ).start()

        @pl.when(jnp.logical_and(s >= 2, s - 2 < ri))
        def _():
            drain(half, ci)

        @pl.when(s - 2 >= ri)
        def _():
            drain(half, co)

        @pl.when(s < ri)
        def _():
            send(gi, ci, s * ci)

        @pl.when(s >= ri)
        def _():
            send(go, co, ri * ci + (s - ri) * co)

        @pl.when(s == steps - 1)
        def _():
            drain(1 - half, co)
            drain(half, co)

    extra, aliases = [], {}
    if total != ri * ci + ro * co:
        extra = [jnp.zeros((total, PACK_ROWS, LANES // 2), jnp.bfloat16)]
        aliases = {3: 0}
    return pl.pallas_call(
        body,
        grid_spec=pltpu.PrefetchScalarGridSpec(
            num_scalar_prefetch=1,
            grid=(steps,),
            in_specs=[
                pl.BlockSpec((side, ci * side), lambda s, ids: (jnp.minimum(s, ri - 1), 0)),
                pl.BlockSpec((side, co * side), lambda s, ids: (jnp.maximum(s - ri, 0), 0)),
            ]
            + [pl.BlockSpec(memory_space=pl.ANY)] * len(extra),
            out_specs=pl.BlockSpec(memory_space=pl.ANY),
            scratch_shapes=[
                pltpu.VMEM((2, max(ci, co), PACK_ROWS, LANES // 2), jnp.bfloat16),
                pltpu.SemaphoreType.DMA((2, max(ci, co))),
            ],
        ),
        out_shape=jax.ShapeDtypeStruct((total, PACK_ROWS, LANES // 2), jnp.bfloat16),
        compiler_params=pltpu.CompilerParams(vmem_limit_bytes=40 * 2**20),
        cost_estimate=pl.CostEstimate(
            flops=0, bytes_accessed=4 * (ri * ci + ro * co) * side * side, transcendentals=0
        ),
        input_output_aliases=aliases,
        name="to_slots",
    )(slots, g_in, g_out, *extra)


def loss_terms(result, frozen, target, weights, upper_log, lower_log, mean_gap):
    samples_n = result.shape[0]
    shaped = result.reshape(samples_n, -1, 4, 8)
    predicted = shaped[..., :4]
    var_raw = shaped[..., 4:]
    frozen_pred = frozen.reshape(samples_n, -1, 4, 8)[..., :4]
    upper = upper_log[:, None, None, None]
    lower = lower_log[:, None, None, None]
    squared = jnp.mean((target - predicted) ** 2, axis=(1, 2, 3))
    fraction = (var_raw + 1.0) / 2.0
    log_var = fraction * upper + (1.0 - fraction) * lower
    mean_diff = mean_gap[:, None, None, None] * (frozen_pred - target)
    diverge = 0.5 * (
        -1.0
        + log_var
        - lower
        + jnp.exp(lower - log_var)
        + mean_diff * mean_diff * jnp.exp(-log_var)
    )
    var_bound = jnp.mean(diverge, axis=(1, 2, 3)) / math.log(2.0)
    return jnp.sum(weights * (squared + var_bound))


def halves(x):
    high = x.astype(jnp.bfloat16)
    return high, (x - high.astype(jnp.float32)).astype(jnp.bfloat16)


def left_form(main, tail):
    mh, ml = halves(main)
    th, tl = halves(tail)
    return jnp.concatenate([mh, mh, ml, th, th, tl], axis=1)


def right_form(x):
    h, l = halves(x)
    return jnp.concatenate(
        [h[:LANES], l[:LANES], h[:LANES], h[LANES:], l[LANES:], h[LANES:]], axis=0
    )


def product(left, right):
    return jnp.dot(left, right, preferred_element_type=jnp.float32)


def symmetric_product(left, right_main, right_tail):
    main = product(left, right_main)
    corner = product(left[LANES:], right_tail)
    return main, jnp.concatenate([main[LANES:].T, corner], axis=0)


def inverse_roots(pairs, eye_main, eye_tail):
    contracted, scales = [], []
    for main, tail in pairs:
        trace = jnp.sum(main * eye_main) + jnp.sum(tail * eye_tail)
        shift = 0.0001 * trace / BLOCK_SIDE
        main = main + shift * eye_main
        tail = tail + shift * eye_tail
        square = jnp.sum(main * main, axis=(0, 1), keepdims=True) + jnp.sum(
            tail * tail, axis=(0, 1), keepdims=True
        )
        factor_z = 2.5 / jnp.sqrt(square)
        contracted.append((main * factor_z, tail * factor_z))
        scales.append(jnp.sqrt(jnp.sqrt(factor_z)))
    estimates = None
    for newton_step in range(NEWTON):
        more = newton_step < NEWTON - 1
        factors = [((5.0 * eye_main - m) * 0.25, (5.0 * eye_tail - t) * 0.25) for m, t in contracted]
        rights = [(right_form(m), right_form(t)) for m, t in factors]
        lefts = [left_form(m, t) for m, t in factors]
        if more:
            powers = [symmetric_product(l, *r) for l, r in zip(lefts, rights)]
        if estimates is None:
            estimates = [(m * s, t * s) for (m, t), s in zip(factors, scales)]
        else:
            estimates = [
                symmetric_product(left_form(*e), *r) for e, r in zip(estimates, rights)
            ]
        if more:
            powers = [
                symmetric_product(left_form(*q), right_form(q[0]), right_form(q[1])) for q in powers
            ]
            contracted = [
                symmetric_product(left_form(*q), right_form(m), right_form(t))
                for q, (m, t) in zip(powers, contracted)
            ]
    return estimates


def shampoo_body(clip_ref, g_ref, stat_ref, old_ref, clipped_ref, new_stat_ref, new_ref, low_ref):
    side = BLOCK_SIDE
    g_main, g_tail = unpack(g_ref[0] * clip_ref[0])
    clipped_ref[0, :, :LANES] = g_main
    clipped_ref[0, :, LANES:] = g_tail
    g = jnp.concatenate([g_main, g_tail], axis=1)

    def unit(width, offset):
        row = lax.broadcasted_iota(jnp.int32, (side, width), 0)
        col = lax.broadcasted_iota(jnp.int32, (side, width), 1) + offset
        return (row == col).astype(jnp.float32)

    eye_main, eye_tail = unit(LANES, 0), unit(TAIL, LANES)
    flipped = g.T
    g_right = (right_form(g[:, :LANES]), right_form(g[:, LANES:]))
    f_right = (right_form(flipped[:, :LANES]), right_form(flipped[:, LANES:]))
    g_left = left_form(g[:, :LANES], g[:, LANES:])
    f_left = left_form(flipped[:, :LANES], flipped[:, LANES:])
    pairs = []
    for k, (left, right) in enumerate(((g_left, f_right), (f_left, g_right))):
        main, tail = symmetric_product(left, *right)
        main = 0.5 * stat_ref[0, k, :, :LANES] + 0.5 * main
        tail = 0.5 * stat_ref[0, k, :, LANES:] + 0.5 * tail
        new_stat_ref[0, k, :, :LANES] = main
        new_stat_ref[0, k, :, LANES:] = tail
        pairs.append((main, tail))
    left_root, right_root = inverse_roots(pairs, eye_main, eye_tail)
    root_left = left_form(*left_root)
    half = left_form(product(root_left, g_right[0]), product(root_left, g_right[1]))
    for part, (a, b) in zip(right_root, ((0, LANES), (LANES, side))):
        direction = product(half, right_form(part))
        old = old_ref[0, :, a:b]
        new = old - shampoo_rate * (direction + decay_rate * old)
        new_ref[0, :, a:b] = new
        low_ref[0, :, a:b] = new.astype(jnp.bfloat16)


def shampoo(clip_factor, gradients, stats, old_blocks):
    count, side = gradients.shape[0], BLOCK_SIDE
    one = pl.BlockSpec((1, side, side), lambda i: (i, 0, 0))
    two = pl.BlockSpec((1, 2, side, side), lambda i: (i, 0, 0, 0))
    block = jax.ShapeDtypeStruct((count, side, side), jnp.float32)
    return pl.pallas_call(
        shampoo_body,
        grid=(count,),
        in_specs=[
            pl.BlockSpec(memory_space=pltpu.SMEM),
            pl.BlockSpec((1, PACK_ROWS, LANES // 2), lambda i: (i, 0, 0)),
            two,
            one,
        ],
        out_specs=[one, two, one, one],
        out_shape=[
            block,
            jax.ShapeDtypeStruct((count, 2, side, side), jnp.float32),
            block,
            jax.ShapeDtypeStruct((count, side, side), jnp.bfloat16),
        ],
        compiler_params=pltpu.CompilerParams(vmem_limit_bytes=56 * 2**20),
        cost_estimate=pl.CostEstimate(
            flops=count * 44 * 6 * side**3, bytes_accessed=count * 34 * side * side, transcendentals=0
        ),
        name="shampoo",
    )(clip_factor.reshape(1), gradients, stats, old_blocks)


def adam_update(weight, gradient, moment_one, second):
    moment_one = 0.5 * moment_one + 0.5 * gradient
    second = 0.5 * second + 0.5 * gradient * gradient
    correct = 1.0 - 0.5**STEP
    updated = weight - adam_rate * (
        moment_one / correct / (jnp.sqrt(second / correct) + 1e-08) + decay_rate * weight
    )
    return (moment_one, second, updated)


def per_device(
    latents,
    noise,
    timesteps,
    labels,
    loss_weights,
    slotted_block_weights,
    statistics,
    slot_of_block,
    cond_tables,
    head_tables,
    slice_bias,
    side_bias,
    cond_m,
    cond_v,
    head_m,
    head_v,
    slice_m,
    slice_v,
    side_m,
    side_v,
):
    bf16, f32 = jnp.bfloat16, jnp.float32
    width = MODEL_WIDTH
    mp, dp = lax.axis_size("mp"), lax.axis_size("dp")
    my_mp, my_dp = lax.axis_index("mp"), lax.axis_index("dp")
    query_width, ff_width, ada_width = HEADS * HD // mp, FF // mp, 6 * width // mp
    ada_column = 3 * query_width + ff_width
    row_blocks = width // BLOCK_SIDE
    col_blocks = (ada_column + ada_width) // BLOCK_SIDE
    out_blocks = (query_width + ff_width) // BLOCK_SIDE
    first_out = row_blocks * col_blocks
    t2_row = PATCH_VALUES + FREQ
    class_row = t2_row + width
    local_heads = query_width // HD
    score_scale = HD ** (-0.5)
    batch = latents.shape[0]
    own_n = batch // mp
    cols = cond_tables.shape[1]
    samples = batch * dp

    def own(x):
        return lax.dynamic_slice_in_dim(x, my_mp * own_n, own_n, 0)

    def my_cols(x):
        return lax.dynamic_slice_in_dim(x, my_dp * cols, cols, x.ndim - 1)

    def all_columns(x):
        return x.transpose(1, 0, 2).reshape(x.shape[1], -1)

    def by_columns(x):
        return x.reshape(x.shape[0], dp, cols).transpose(1, 0, 2)

    def reduce_rows(x):
        return lax.psum_scatter(
            x.astype(bf16), "mp", scatter_dimension=0, tiled=True
        ).astype(f32)

    def share_rows(x):
        return lax.all_gather(x, "mp", axis=0, tiled=True)

    blocks = gather_blocks(pack_blocks(slotted_block_weights[0]))

    cond_low, head_low = cond_tables.astype(bf16), head_tables.astype(bf16)
    facts, shared = exchange(
        [
            (jnp.stack([timesteps.astype(f32), labels.astype(f32), loss_weights], 1), "gather"),
            (jnp.concatenate([cond_low[:PATCH_VALUES].T, head_low[:, 2 * width :]], 1), "gather"),
        ],
        "dp",
        2,
    )
    facts, shared = facts.reshape(samples, 3), shared.reshape(width, -1)
    all_steps, all_labels = facts[:, 0].astype(jnp.int32), facts[:, 1].astype(jnp.int32)
    weight_total = jnp.sum(facts[:, 2])
    w_patch, w_head = shared[:, :PATCH_VALUES].T, shared[:, PATCH_VALUES:]
    time_freq = time_features(all_steps, FREQ).astype(bf16)
    onehot = all_labels[:, None] == jnp.arange(CLASSES, dtype=jnp.int32)[None, :]
    first_t = dense(time_freq, cond_low[PATCH_VALUES:t2_row]) + my_cols(side_bias[width : 2 * width])
    (first_s,) = exchange([(swish_unit(first_t).astype(bf16), "gather")], "dp", 3)
    first_s = all_columns(first_s)
    cond_vec = (
        dense(first_s, cond_low[t2_row:class_row])
        + my_cols(side_bias[2 * width : 3 * width])
        + dense(onehot.astype(bf16), cond_low[class_row:])
    )
    signal_cols = swish_unit(cond_vec).astype(bf16)
    signal, final_mod = exchange(
        [
            (signal_cols.reshape(dp, batch, cols), "scatter"),
            (dense(signal_cols, head_low[:, : 2 * width]).reshape(dp, batch, 2 * width), "scatter"),
        ],
        "dp",
        4,
    )
    signal = all_columns(signal)
    final_mod = own(jnp.sum(final_mod, 0) + side_bias[5 * width : 7 * width])

    w_in = assemble(blocks, slot_of_block, 0, row_blocks, col_blocks)
    w_out = assemble(blocks, slot_of_block, first_out, out_blocks, row_blocks)
    own_bias = slice_bias[0]
    modul = lax.all_gather(
        dense(signal, w_in[:, ada_column:]) + own_bias[2 * query_width + ff_width :],
        "mp",
        axis=1,
        tiled=True,
    )
    own_modul = own(modul)

    def part(position, source=own_modul):
        return source[:, None, position * width : (position + 1) * width]

    def heads_of(inputs):
        return inputs.reshape(batch, -1, local_heads, HD)

    keep_rate, noise_rate, upper_log, lower_log, mean_gap = coefficients(timesteps)
    noisy = keep_rate[:, None, None, None] * latents + noise_rate[:, None, None, None] * noise
    patches = patchify(noisy).astype(bf16)
    seq_len = patches.shape[1]
    initial = (
        dense(patches, w_patch) + side_bias[:width] + position_embedding(LATENT_SIDE // 2, width)
    )
    normed_all, inv_std_all = layer_norm(initial)
    attn_in = (normed_all * (1.0 + part(1, modul)) + part(0, modul)).astype(bf16)
    start, normed_a, inv_std_a = own(initial), own(normed_all), own(inv_std_all)
    own_patches = own(patches)
    target = patchify(own(noise)).reshape(own_n, seq_len, 4, 4)

    projected = dense(attn_in, w_in[:, : 3 * query_width])
    queries = heads_of((projected[..., :query_width] + own_bias[:query_width]).astype(bf16))
    keys = heads_of(projected[..., query_width : 2 * query_width].astype(bf16))
    values = heads_of(
        (projected[..., 2 * query_width :] + own_bias[query_width : 2 * query_width]).astype(bf16)
    )
    scores = (
        jnp.einsum("slhe,smhe->shlm", queries, keys, preferred_element_type=f32) * score_scale
    )
    row_peak = jnp.max(scores, -1, keepdims=True)
    shifted = jnp.exp(scores - row_peak)
    row_total = jnp.sum(shifted, -1, keepdims=True)
    probs = shifted / row_total
    log_total = row_peak + jnp.log(row_total)
    mixed = (
        jnp.einsum("shlm,smhe->slhe", probs.astype(bf16), values, preferred_element_type=f32)
        .reshape(batch, seq_len, query_width)
        .astype(bf16)
    )
    attn = reduce_rows(dense(mixed, w_out[:query_width])) + side_bias[3 * width : 4 * width]
    middle = start + part(2) * attn
    normed_m, inv_std_m = layer_norm(middle)
    mlp_in = share_rows((normed_m * (1.0 + part(4)) + part(3)).astype(bf16))
    hidden = (
        dense(mlp_in, w_in[:, 3 * query_width : ada_column])
        + own_bias[2 * query_width : 2 * query_width + ff_width]
    )
    active = tanh_gelu_activation(hidden).astype(bf16)
    branch = reduce_rows(dense(active, w_out[query_width:])) + side_bias[4 * width : 5 * width]
    final = middle + part(5) * branch
    normed_f, inv_std_f = layer_norm(final)
    fscale, fshift = final_mod[:, None, width:], final_mod[:, None, :width]
    head_in = (normed_f * (1.0 + fscale) + fshift).astype(bf16)
    output = dense(head_in, w_head) + side_bias[7 * width :]

    def objective(result):
        return loss_terms(
            result, output, target, own(loss_weights), own(upper_log), own(lower_log), own(mean_gap)
        )

    loss_part, loss_pull = jax.vjp(objective, output)
    (seed_grad,) = loss_pull(jnp.ones_like(loss_part) / weight_total)

    d_out = seed_grad.astype(bf16)
    d_headin = back_dense(d_out, w_head)
    d_final = norm_back(d_headin * (1.0 + fscale), normed_f, inv_std_f)
    d_fmod = jnp.concatenate([jnp.sum(d_headin, 1), jnp.sum(d_headin * normed_f, 1)], 1).astype(bf16)
    own_branch = (part(5) * d_final).astype(bf16)
    d_gate2 = jnp.sum(d_final * branch, 1)
    d_branch = share_rows(own_branch)
    g_down = weight_grad(active, d_branch).astype(bf16)
    d_active = back_dense(d_branch, w_out[query_width:])
    d_hidden = (d_active * gelu_slope(hidden)).astype(bf16)
    g_up = weight_grad(mlp_in, d_hidden).astype(bf16)
    d_mlpin = reduce_rows(back_dense(d_hidden, w_in[:, 3 * query_width : ada_column]))
    d_shift2 = jnp.sum(d_mlpin, 1)
    d_scale2 = jnp.sum(d_mlpin * normed_m, 1)
    d_middle = d_final + norm_back(d_mlpin * (1.0 + part(4)), normed_m, inv_std_m)
    own_attn = (part(2) * d_middle).astype(bf16)
    d_gate1 = jnp.sum(d_middle * attn, 1)
    d_attn = share_rows(own_attn)
    g_outp = weight_grad(mixed, d_attn).astype(bf16)
    d_mixed = heads_of(back_dense(d_attn, w_out[:query_width]).astype(bf16))
    probs = jnp.exp(
        jnp.einsum("slhe,smhe->shlm", queries, keys, preferred_element_type=f32) * score_scale
        - log_total
    )
    d_values = jnp.einsum(
        "shlm,slhe->smhe", probs.astype(bf16), d_mixed, preferred_element_type=f32
    ).astype(bf16)
    d_probs = jnp.einsum("slhe,smhe->shlm", d_mixed, values, preferred_element_type=f32)
    d_scores = (probs * (d_probs - jnp.sum(d_probs * probs, -1, keepdims=True))).astype(bf16)
    d_query = (
        jnp.einsum("shlm,smhe->slhe", d_scores, keys, preferred_element_type=f32) * score_scale
    ).astype(bf16)
    d_keys = (
        jnp.einsum("shlm,slhe->smhe", d_scores, queries, preferred_element_type=f32) * score_scale
    ).astype(bf16)
    flat_q = d_query.reshape(batch, seq_len, query_width)
    flat_v = d_values.reshape(batch, seq_len, query_width)
    d_proj = jnp.concatenate([flat_q, d_keys.reshape(batch, seq_len, query_width), flat_v], 2)
    g_qkv = weight_grad(attn_in, d_proj).astype(bf16)
    d_attnin = reduce_rows(back_dense(d_proj, w_in[:, : 3 * query_width]))
    d_shift1 = jnp.sum(d_attnin, 1)
    d_scale1 = jnp.sum(d_attnin * normed_a, 1)
    d_start = (
        d_middle + norm_back(d_attnin * (1.0 + part(1)), normed_a, inv_std_a)
    ).astype(bf16)
    d_mod_own = jnp.concatenate([d_shift1, d_scale1, d_gate1, d_shift2, d_scale2, d_gate2], 1)
    d_modul = lax.dynamic_slice_in_dim(
        share_rows(d_mod_own.astype(bf16)), my_mp * ada_width, ada_width, 1
    )
    g_ada = weight_grad(signal, d_modul).astype(bf16)

    slot_grad = to_slots(
        jnp.concatenate([g_qkv, g_up, g_ada], 1),
        jnp.concatenate([g_outp, g_down], 0),
        slot_of_block,
        slot_of_block.shape[0],
    )
    red_blocks = reduce_blocks(slot_grad)

    d_fmod_all, d_signal = exchange(
        [(d_fmod, "gather"), (by_columns(back_dense(d_modul, w_in[:, ada_column:])), "scatter")],
        EVERY,
        5,
    )
    d_fmod_all = d_fmod_all.reshape(samples, 2 * width)
    g_fada = weight_grad(signal_cols, d_fmod_all)
    d_signal = jnp.sum(d_signal.reshape(dp, mp, batch, cols), 1).reshape(samples, cols)
    d_signal = d_signal + back_dense(d_fmod_all, head_low[:, : 2 * width])
    d_cond = d_signal * swish_slope(cond_vec)
    d_second = d_cond.astype(bf16)
    g_second = weight_grad(first_s, d_second)
    g_class = jnp.einsum("sc,sd->cd", onehot.astype(f32), d_cond, precision=exact_precision_flag)
    small = jnp.concatenate(
        [weight_grad(own_patches, d_start), jnp.einsum("...i,...j->ij", d_out, head_in, preferred_element_type=f32)], 0
    )
    slice_part = jnp.concatenate(
        [total_of(flat_q), total_of(flat_v), total_of(d_hidden), total_of(d_modul)]
    )
    side_part = jnp.concatenate(
        [total_of(d_start), total_of(own_attn), total_of(own_branch), total_of(d_out), loss_part[None]]
    )
    bias_part = jnp.concatenate([slice_part, side_part])
    rows = -(-bias_part.shape[0] // 1024) * 8
    bias_part = jnp.pad(bias_part, (0, rows * 128 - bias_part.shape[0])).reshape(rows, 128)
    d_first, small, bias_part = exchange(
        [
            (by_columns(back_dense(d_second, cond_low[t2_row:class_row])), "scatter"),
            (by_columns(small), "scatter"),
            (bias_part, "gather"),
        ],
        "dp",
        6,
    )
    d_first = (jnp.sum(d_first, 0) * swish_slope(first_t)).astype(bf16)
    g_first = weight_grad(time_freq, d_first)
    bias_part = jnp.sum(bias_part, 0).reshape(-1)
    red_slice = bias_part[: slice_part.shape[0]]
    side_rows = bias_part[slice_part.shape[0] // 128 * 128 :].reshape(-1, 128)
    small, side_rows = exchange([(jnp.sum(small, 0), "gather"), (side_rows, "gather")], "mp", 7)
    small, side_sum = jnp.sum(small, 0), jnp.sum(side_rows, 0).reshape(-1)
    loss_sum = side_sum[side_part.shape[0] - 1]
    side_sum = side_sum[: side_part.shape[0] - 1]
    side_mod = total_of(d_fmod_all)
    red_cond = jnp.concatenate([small[:PATCH_VALUES], g_first, g_second, g_class], 0)
    red_head = jnp.concatenate([g_fada, small[PATCH_VALUES:].T], 1)
    side_cols = jnp.stack([total_of(d_first), total_of(d_second)])

    local_squares = (
        jnp.sum(red_blocks * red_blocks)
        + (jnp.sum(red_cond * red_cond) + jnp.sum(red_head * red_head) + jnp.sum(side_cols * side_cols)) / mp
        + jnp.sum(red_slice * red_slice) / dp
        + (jnp.sum(side_sum * side_sum) + jnp.sum(side_mod * side_mod)) / (dp * mp)
    )
    last = jnp.concatenate([side_cols, jnp.broadcast_to(local_squares, (2, 1))], 1)
    (last,) = exchange([(last, "gather")], EVERY, 8)
    grad_norm = jnp.sqrt(jnp.sum(last[:, 0, cols]))
    side_cols = last[:, :, :cols].reshape(dp, mp, 2, cols)[:, 0].transpose(1, 0, 2).reshape(2 * width)
    red_side = jnp.concatenate(
        [side_sum[:width], side_cols, side_sum[width : 3 * width], side_mod, side_sum[3 * width :]]
    )
    clip_factor = 1.0 / jnp.maximum(grad_norm, 1.0)
    clipped, new_stats, new_blocks, new_low = shampoo(
        clip_factor, red_blocks, statistics[0], slotted_block_weights[0]
    )
    cond_one, cond_two, new_cond = adam_update(cond_tables, red_cond * clip_factor, cond_m, cond_v)
    head_one, head_two, new_head = adam_update(head_tables, red_head * clip_factor, head_m, head_v)
    slice_one, slice_two, new_slice = adam_update(
        slice_bias[0], red_slice * clip_factor, slice_m[0], slice_v[0]
    )
    side_one, side_two, new_side = adam_update(side_bias, red_side * clip_factor, side_m, side_v)
    return (
        loss_sum,
        weight_total,
        grad_norm,
        clipped[None],
        new_stats[None],
        new_blocks[None],
        new_low[None],
        cond_one,
        cond_two,
        new_cond,
        new_cond.astype(bf16),
        head_one,
        head_two,
        new_head,
        new_head.astype(bf16),
        slice_one[None],
        slice_two[None],
        new_slice[None],
        side_one,
        side_two,
        new_side,
    )


def solution(mesh):
    return jax.shard_map(
        per_device,
        mesh=mesh,
        in_specs=(
            P("dp", None, None, None),
            P("dp", None, None, None),
            P("dp"),
            P("dp"),
            P("dp"),
            P("mp", "dp", None, None),
            P("mp", "dp", None, None, None),
            P(),
            P(None, "dp"),
            P("dp", None),
            P("mp", None),
            P(),
            P(None, "dp"),
            P(None, "dp"),
            P("dp", None),
            P("dp", None),
            P("mp", None),
            P("mp", None),
            P(),
            P(),
        ),
        out_specs=(
            P(),
            P(),
            P(),
            P("mp", "dp", None, None),
            P("mp", "dp", None, None, None),
            P("mp", "dp", None, None),
            P("mp", "dp", None, None),
            P(None, "dp"),
            P(None, "dp"),
            P(None, "dp"),
            P(None, "dp"),
            P("dp", None),
            P("dp", None),
            P("dp", None),
            P("dp", None),
            P("mp", None),
            P("mp", None),
            P("mp", None),
            P(),
            P(),
            P(),
        ),
        check_vma=False,
    )
```

time: 2410 us -> 957 us (0.40)
  waiting for transfers between devices: 1290 us -> 161 us
  Pallas kernels: 0 us -> 484 us
  matrix products: 538 us -> 102 us
  local copies, waits for them, and re-layouts: 290 us -> 95.4 us
  blocking collectives: 119 us -> 10.9 us
  other arithmetic: 138 us -> 67.4 us
    pallas_call x0 -> x14, Pallas kernels: none -> 484 us  [the longest x1 147 us: reduce_blocks(): pl.pallas_call(reduce_body, in_specs=[pl.BlockSpec(memory_space=pltpu.VME...]
    dot_general x32 -> x8, matrix products: 444 us -> 7.51 us  [the longest x1 2.03 us: per_device(): jnp.einsum('sc,sd->cd', onehot.astype(f32), d_cond, precision=exact_preci...]
    reduce_scatter x2 -> x4, waiting for transfers between devices: 510 us -> 89.4 us  [reduce_rows(): lax.psum_scatter(x.astype(bf16), 'mp', scatter_dimension=0, tiled=True)]
    psum x4 -> x0, waiting for transfers between devices: 346 us -> none  [across_model(): return lax.psum(inputs, 'mp')]
    all_gather x3, waiting for transfers between devices: 363 us -> 71.1 us  [share_rows(): return lax.all_gather(x, 'mp', axis=0, tiled=True)]
    psum x4 -> x0, blocking collectives: 113 us -> none  [the longest x2 62.3 us: per_device(): loss_sum, weight_total = lax.psum((loss_part, jnp.sum(loss_weights)), 'dp')]
    reshape x6 -> x13, local copies, waits for them, and re-layouts: 85.9 us -> 9.34 us  [the longest x6 6.59 us: by_columns(): return x.reshape(x.shape[0], dp, cols).transpose(1, 0, 2)]
    unnamed x11 -> x7, waiting for transfers between devices: 71.2 us -> 0.11 us
  transfers between devices with their start and end apart: 10 -> 7, of which waited for: 9 -> 7; matrix products, arithmetic and copies ran while one was open for 14% -> 4% of each run, Pallas kernels for 0% -> 0%
where the time goes in v1:
time: 957 us; the launch traced here: 947 us
  Pallas kernels  484 us (51%)
  waiting for transfers between devices  161 us (17%)
  matrix products  102 us (11%)
  local copies, waits for them, and re-layouts  95.4 us (10%)
  other arithmetic  67.4 us (7%)
  between operations  26 us (3%)
  blocking collectives  10.9 us (1%)
    pallas_call x1, Pallas kernels, reduce_blocks(): pl.pallas_call(reduce_body, in_specs=[pl.BlockSpec(memory_space=pltpu.VME...  147 us
    pallas_call x1, Pallas kernels, gather_blocks(): pl.pallas_call(gather_body, in_specs=[pl.BlockSpec(memory_space=pl.ANY)],...  133 us
    pallas_call x1, Pallas kernels, shampoo(): pl.pallas_call(shampoo_body, grid=(count,), in_specs=[pl.BlockSpec(memory...  101 us
    reduce_scatter x4, waiting for transfers between devices, reduce_rows(): lax.psum_scatter(x.astype(bf16), 'mp', scatter_dimension=0, tiled=True)  89.4 us
    pallas_call x7, Pallas kernels, exchange(): pl.pallas_call(body, in_specs=[vmem] * len(arrays), out_specs=[vmem] * le...  75.9 us
    all_gather x3, waiting for transfers between devices, share_rows(): return lax.all_gather(x, 'mp', axis=0, tiled=True)  71.1 us
    dot_general x8, matrix products, back_dense(): jnp.einsum('...j,ij->...i', gradient, weight, preferred_element_type=jnp....  33.6 us
    dot_general x9, matrix products, weight_grad(): jnp.einsum('...i,...j->ij', operand, gradient, preferred_element_type=jnp...  33.1 us
  transfers between devices with their start and end apart: 7, of which 7 were waited for; matrix products, arithmetic and copies ran while one was open for 4% of the time, Pallas kernels for 0%

profile of v1, /device:TPU:0, one launch (start us, length us, event | category | flops | bytes accessed | tf_op | source)
XLA Modules:
  0.0 947.0 jit_solution(6018107972123589234)
XLA Ops:
  15.1 11.6 %exchange_2.1 = (f32[8,4,3]{2,1,0:T(4,128)S(1)}, bf16[8,144,48]{2,1,0:T(8,128)(2,1)S(1)}) custom-call(f32[4,3]{1,0:T(4,128)S(1)} %pad_maximum_fusion.13.refs_0_, bf16[144,48]{1,0:T(8,128)(2,1)S(1)} %pad_maximum_fusion.8.refs_1_), custom_call_target="tpu_custom_call" | custom-call | tf_op jit(solution)/shard_map/exchange_2/pallas_call | solution.py:520
  29.3 8.8 exchange_3.1
  40.5 6.6 pack_blocks.1.x_ref
  47.2 132.9 %gather_blocks.1.refs_0_.refs_1_.refs_2_.refs_3_.refs_4_.refs_5_.refs_6_.refs_7_.refs_8_.refs_9_.refs_10_.refs_11_.refs_12_ = bf16[72,656,128]{2,1,0:T(8,128)(2,1)} custom-call(bf16[9,656,128]{2,1,0:T(8,128)(2,1)} %pack_blocks.1.x_ref), custom_call_target="tpu_custom_call" | custom-call | tf_op jit(solution)/shard_map/gather_blocks/pallas_call | solution.py:305
  180.1 5.1 assemble.3
  185.2 6.8 assemble.2
  192.1 3.4 copy-done.1
  198.4 7.3 exchange_4.1
  210.0 4.2 copy.169
  222.2 3.6 fusion.19
  225.9 5.5 all-gather
  231.6 5.6 fusion.27
  241.2 2.9 convolution_convert_fusion.2
  244.8 33.8 %reduce-scatter.5.cloned.1.call-done = bf16[1,256,1152]{2,1,0:T(8,128)(2,1)} async-done(((bf16[4,256,1152]{2,1,0:T(8,128)(2,1)}), bf16[1,256,1152]{2,1,0:T(8,128)(2,1)}) %reduce-scatter.5.cloned.1.call-update) | async-done | bytes 589840 | tf_op jit(solution)/shard_map/reduce_scatter | solution.py:854
  283.5 23.2 %all-gather.6.cloned.1.call-done = bf16[4,256,1152]{2,1,0:T(8,128)(2,1)} async-done(((bf16[1,256,1152]{2,1,0:T(8,128)(2,1)}), bf16[4,256,1152]{2,1,0:T(8,128)(2,1)}) %all-gather.6.cloned.1.call-update) | async-done | bytes 2359312 | tf_op jit(solution)/shard_map/all_gather | solution.py:859
  306.7 6.2 convolution_add_fusion.1
  315.1 5.4 convolution_convert_fusion.4
  332.7 21.1 %reduce-scatter.7.cloned.1.call-done = bf16[1,256,1152]{2,1,0:T(8,128)(2,1)} async-done(((bf16[4,256,1152]{2,1,0:T(8,128)(2,1)}), bf16[1,256,1152]{2,1,0:T(8,128)(2,1)}) %reduce-scatter.7.cloned.1.call-update) | async-done | bytes 589840 | tf_op jit(solution)/shard_map/reduce_scatter | solution.py:854
  362.8 23.8 %all-gather.8.cloned.1.call-done = bf16[4,256,1152]{2,1,0:T(8,128)(2,1)} async-done(((bf16[1,256,1152]{2,1,0:T(8,128)(2,1)}), bf16[4,256,1152]{2,1,0:T(8,128)(2,1)}) %all-gather.8.cloned.1.call-update) | async-done | bytes 2359312 | tf_op jit(solution)/shard_map/all_gather | solution.py:859
  386.6 9.5 convert_reduce_fusion
  397.6 6.9 convolution_convert_fusion.3
  404.5 33.2 %reduce-scatter.9.cloned.1.call-done = bf16[1,256,1152]{2,1,0:T(8,128)(2,1)} async-done(((bf16[4,256,1152]{2,1,0:T(8,128)(2,1)}), bf16[1,256,1152]{2,1,0:T(8,128)(2,1)}) %reduce-scatter.9.cloned.1.call-update) | async-done | bytes 589840 | tf_op jit(solution)/shard_map/reduce_scatter | solution.py:854
  437.7 2.7 fusion.46
  440.4 4.2 convert_reduce_fusion.2
  444.7 24.1 %all-gather.10.cloned.1.call-done = bf16[4,256,1152]{2,1,0:T(8,128)(2,1)} async-done(((bf16[1,256,1152]{2,1,0:T(8,128)(2,1)}), bf16[4,256,1152]{2,1,0:T(8,128)(2,1)}) %all-gather.10.cloned.1.call-update) | async-done | bytes 2359312 | tf_op jit(solution)/shard_map/all_gather | solution.py:859
  468.8 2.8 convolution_convert_fusion.5
  477.5 6.0 convolution_convert_fusion.1
  487.7 7.7 fusion
  495.4 7.6 fusion.1
  504.4 5.0 bitcast_convert_fusion
  509.4 2.9 copy.191
  512.3 2.8 fusion.15
  523.6 5.4 all-gather.1
  529.2 4.3 fusion.10
  542.8 13.1 %exchange_5.1 = (bf16[32,1,2304]{2,1,0:T(2,128)(2,1)S(1)}, f32[32,4,144]{2,1,0:T(4,128)S(1)}) custom-call(bf16[1,2304]{1,0:T(2,128)(2,1)S(1)} %pad_maximum_fusion.12.refs_0_, f32[8,4,144]{2,1,0:T(4,128)S(1)} %bitcast.237), custom_call_target="tpu_custom_call" | custom-call | tf_op jit(solution)/shard_map/exchange_5/pallas_call | solution.py:520
  565.4 21.8 %exchange_6.1 = (f32[8,32,144]{2,1,0:T(8,128)S(1)}, f32[8,48,144]{2,1,0:T(8,128)S(1)}, f32[8,56,128]{2,1,0:T(8,128)S(1)}) custom-call(f32[8,32,144]{2,1,0:T(8,128)S(1)} %bitcast.233, f32[8,48,144]{2,1,0:T(8,128)S(1)} %bitcast.232, f32[56,128]{1,0:T(8,128)S(1)} %copy-done.12), custom_call_target="tpu_custom_call" | custom-call | tf_op jit(solution)/shard_map/exchange_6/pallas_call | solution.py:520
  593.7 5.0 exchange_7.1
  613.3 3.2 convolution_convert_fusion
  627.5 6.3 copy.192
  633.8 15.7 %concatenate.97.gi = bf16[1152,3744]{1,0:T(8,128)(2,1)} concatenate(bf16[1152,864]{1,0:T(8,128)(2,1)} %copy.191, bf16[1152,1152]{1,0:T(8,128)(2,1)} %fusion, bf16[1152,1728]{1,0:T(8,128)(2,1)} %copy.192), dimensions={1} | concatenate | bytes 17252352 | tf_op jit(solution)/shard_map/concatenate | solution.py:1023
  649.6 3.5 copy-done
  653.1 8.0 to_slots.1.x_ref
  661.1 146.7 %reduce_blocks.1.g_ref = f32[9,656,128]{2,1,0:T(8,128)} custom-call(bf16[72,656,128]{2,1,0:T(8,128)(2,1)} %to_slots.1.x_ref), custom_call_target="tpu_custom_call" | custom-call | tf_op jit(solution)/shard_map/reduce_blocks/pallas_call | solution.py:452
  807.9 3.4 multiply_reduce_fusion.3
  817.4 8.3 exchange_8.1
  827.4 5.4 fusion.118
  832.8 3.1 fusion.116
  836.0 101.4 %shampoo.1 = (f32[9,288,288]{2,1,0:T(8,128)}, f32[9,2,288,288]{3,2,1,0:T(8,128)}, f32[9,288,288]{2,1,0:T(8,128)}, bf16[9,288,288]{2,1,0:T(8,128)(2,1)}) custom-call(f32[1]{0:T(128)} %bitcast.70.clip_ref, f32[9,656,128]{2,1,0:T(8,128)} %reduce_blocks.1.g_ref, f32[9,2,288,288]{3,2,1,0:T(8,128)} %bitcast.278, f32[9,288,288]{2,1,0:T(8,128)} %bitcast.246), custom_call_target="tpu_custom_call" | custom-call | flops 56757583872 | bytes 25380864 | tf_op jit(solution)/shard_map/shampoo/pallas_call | solution.py:766
  (388 shorter events, 133.2 us)
Async XLA Ops:
  7.2 7.6 copy-start.22
  7.2 271.4 %reduce-scatter.5.cloned.1.call-start = ((), (), s32[]{:S(2)}) async-start(), calls=%async_computation.4 | async-start | bytes 2949120 | tf_op jit(solution)/shard_map/reduce_scatter | solution.py:854
  14.8 25.7 %copy-start.31 = (bf16[2425,144]{0,1:T(8,128)(2,1)}, bf16[2425,144]{0,1:T(8,128)(2,1)S(1)}, u32[]{:S(2)}) copy-start(bf16[2425,144]{0,1:T(8,128)(2,1)S(1)} %convert_element_type.271) | copy-start | bytes 2095204
  14.9 32.2 %copy-start.32 = (bf16[144,2336]{1,0:T(8,128)(2,1)}, bf16[144,2336]{1,0:T(8,128)(2,1)S(1)}, u32[]{:S(2)}) copy-start(bf16[144,2336]{1,0:T(8,128)(2,1)S(1)} %convert_element_type.272) | copy-start | bytes 2018308
  28.2 19.0 %copy-start.88 = (s32[32,1]{0,1:T(1,128)}, s32[32,1]{0,1:T(1,128)S(1)}, u32[]{:S(2)}) copy-start(s32[32,1]{0,1:T(1,128)S(1)} %copy.222) | copy-start | bytes 388
  28.4 10.2 %copy-start.68 = (bf16[32,128]{1,0:T(8,128)(2,1)}, bf16[32,128]{1,0:T(8,128)(2,1)S(1)}, u32[]{:S(2)}) copy-start(bf16[32,128]{1,0:T(8,128)(2,1)S(1)} %get-tuple-element.124) | copy-start | bytes 24580
  28.4 10.2 %copy-start.70 = (bf16[32,128]{1,0:T(8,128)(2,1)}, bf16[32,128]{1,0:T(8,128)(2,1)S(1)}, u32[]{:S(2)}) copy-start(bf16[32,128]{1,0:T(8,128)(2,1)S(1)} %get-tuple-element.125) | copy-start | bytes 24580
  38.3 8.9 copy-start.38
  39.6 7.6 copy-start.50
  47.2 133.0 %copy-start.14 = (s32[72]{0:T(128)S(1)}, s32[72]{0:T(128)}, u32[]{:S(2)}) copy-start(s32[72]{0:T(128)} %ids.5) | copy-start | bytes 868
  185.2 10.3 %copy-start.87 = (s32[4]{0:T(128)S(1)}, s32[4]{0:T(128)}, u32[]{:S(2)}) copy-start(s32[4]{0:T(128)} %param.22) | copy-start | bytes 52
  206.5 15.7 %copy-start.51 = (bf16[4,1152]{1,0:T(4,128)(2,1)}, bf16[4,1152]{1,0:T(4,128)(2,1)S(1)}, u32[]{:S(2)}) copy-start(bf16[4,1152]{1,0:T(4,128)(2,1)S(1)} %reshape.614) | copy-start | bytes 27652
  244.1 34.5 %copy-start.55 = (f32[1152]{0:T(1024)S(1)}, f32[1152]{0:T(1024)}, u32[]{:S(2)}) copy-start(f32[1152]{0:T(1024)} %get-tuple-element.111) | copy-start | bytes 13828
  244.1 62.6 %all-gather.6.cloned.1.call-start = ((), (), s32[]{:S(2)}) async-start(), calls=%async_computation.5 | async-start | bytes 2949120 | tf_op jit(solution)/shard_map/all_gather | solution.py:859
  280.6 32.3 %copy-start.78 = (f32[256]{0:T(256)}, f32[256]{0:T(256)S(1)}, u32[]{:S(2)}) copy-start(f32[256]{0:T(256)S(1)} %add_rsqrt_fusion.2) | copy-start | bytes 3076
  282.5 71.3 %reduce-scatter.7.cloned.1.call-start = ((), (), s32[]{:S(2)}) async-start(), calls=%async_computation.6 | async-start | bytes 2949120 | tf_op jit(solution)/shard_map/reduce_scatter | solution.py:854
  320.5 33.2 %copy-start.57 = (f32[1152]{0:T(1024)S(1)}, f32[1152]{0:T(1024)}, u32[]{:S(2)}) copy-start(f32[1152]{0:T(1024)} %get-tuple-element.110) | copy-start | bytes 13828
  320.6 66.1 %all-gather.8.cloned.1.call-start = ((), (), s32[]{:S(2)}) async-start(), calls=%async_computation.7 | async-start | bytes 2949120 | tf_op jit(solution)/shard_map/all_gather | solution.py:859
  362.4 75.3 %reduce-scatter.9.cloned.1.call-start = ((), (), s32[]{:S(2)}) async-start(), calls=%async_computation.8 | async-start | bytes 2949120 | tf_op jit(solution)/shard_map/reduce_scatter | solution.py:854
  404.4 33.2 %copy-start.79 = (f32[256]{0:T(256)S(1)}, f32[256]{0:T(256)}, u32[]{:S(2)}) copy-start(f32[256]{0:T(256)} %copy-done.78) | copy-start | bytes 3076
  404.4 64.4 %all-gather.10.cloned.1.call-start = ((), (), s32[]{:S(2)}) async-start(), calls=%async_computation.9 | async-start | bytes 2949120 | tf_op jit(solution)/shard_map/all_gather | solution.py:859
  444.6 72.2 %reduce-scatter.11.cloned.1.call-start = ((), (), s32[]{:S(2)}) async-start(), calls=%async_computation.10 | async-start | bytes 2949120 | tf_op jit(solution)/shard_map/reduce_scatter | solution.py:854
  487.6 7.7 copy-start.96
  495.3 7.6 copy-start.24
  495.3 9.0 copy-start.74
  495.4 9.0 copy-start.76
  529.1 6.0 copy-start.41
  529.1 6.0 copy-start.63
  529.1 6.0 copy-start.64
  529.1 5.9 copy-start.84
  529.1 5.9 copy-start.85
  529.2 5.9 copy-start.86
  556.7 50.1 %copy-start.89 = (s32[32,1]{0,1:T(1,128)S(1)}, s32[32,1]{0,1:T(1,128)}, u32[]{:S(2)}) copy-start(s32[32,1]{0,1:T(1,128)} %copy-done.88) | copy-start | bytes 388
  599.4 13.9 %copy-start.42 = (bf16[4,1,1728]{2,1,0:T(2,128)(2,1)S(1)}, bf16[4,1,1728]{2,1,0:T(2,128)(2,1)}, u32[]{:S(2)}) copy-start(bf16[4,1,1728]{2,1,0:T(2,128)(2,1)} %copy-done.41) | copy-start | bytes 41476
  604.1 9.2 copy-start.52
  613.3 5.8 copy-start.45
  807.8 6.0 copy-start.21
  807.8 19.4 %copy-start.44 = (f32[56,128]{1,0:T(8,128)S(1)}, f32[56,128]{1,0:T(8,128)}, u32[]{:S(2)}) copy-start(f32[56,128]{1,0:T(8,128)} %reduce_sum.528) | copy-start | bytes 86020
  807.8 19.5 %copy-start.67 = (f32[8096]{0:T(1024)S(1)}, f32[8096]{0:T(1024)}, u32[]{:S(2)}) copy-start(f32[8096]{0:T(1024)} %constant_dynamic-update-slice_fusion.6) | copy-start | bytes 97156
  807.8 19.5 %copy-start.46 = (f32[29,128]{1,0:T(8,128)S(1)}, f32[29,128]{1,0:T(8,128)}, u32[]{:S(2)}) copy-start(f32[29,128]{1,0:T(8,128)} %reduce_sum.529) | copy-start | bytes 44548
  807.9 19.5 %copy-start.54 = (f32[2304]{0:T(1024)S(1)}, f32[2304]{0:T(1024)}, u32[]{:S(2)}) copy-start(f32[2304]{0:T(1024)} %convert_reduce_fusion.6) | copy-start | bytes 27652
  807.9 19.5 %copy-start.20 = (f32[2425,144]{0,1:T(8,128)S(1)}, f32[2425,144]{0,1:T(8,128)}, u32[]{:S(2)}) copy-start(f32[2425,144]{0,1:T(8,128)} %concatenate.99) | copy-start | bytes 4190404
  835.9 101.5 %copy-start.62 = (f32[1,3456]{1,0:T(1,128)S(1)}, f32[1,3456]{1,0:T(1,128)}, u32[]{:S(2)}) copy-start(f32[1,3456]{1,0:T(1,128)} %param.30) | copy-start | bytes 41476
  835.9 101.5 %copy-start.81 = (f32[1,3456]{1,0:T(1,128)S(1)}, f32[1,3456]{1,0:T(1,128)}, u32[]{:S(2)}) copy-start(f32[1,3456]{1,0:T(1,128)} %param.37) | copy-start | bytes 41476
  835.9 101.5 %copy-start.82 = (f32[1,3456]{1,0:T(1,128)S(1)}, f32[1,3456]{1,0:T(1,128)}, u32[]{:S(2)}) copy-start(f32[1,3456]{1,0:T(1,128)} %param.36) | copy-start | bytes 41476
  836.0 102.2 %copy-start.43 = (f32[8096]{0:T(1024)S(1)}, f32[8096]{0:T(1024)}, u32[]{:S(2)}) copy-start(f32[8096]{0:T(1024)} %param.31) | copy-start | bytes 97156
  836.0 102.2 %copy-start.65 = (f32[8096]{0:T(1024)S(1)}, f32[8096]{0:T(1024)}, u32[]{:S(2)}) copy-start(f32[8096]{0:T(1024)} %param.39) | copy-start | bytes 97156
  836.0 102.2 %copy-start.66 = (f32[8096]{0:T(1024)S(1)}, f32[8096]{0:T(1024)}, u32[]{:S(2)}) copy-start(f32[8096]{0:T(1024)} %param.38) | copy-start | bytes 97156
  (60 other events, 154.2 us)
Sparse Core Ops, SparseCore 0:
  244.2 34.3 reduce-scatter.4
  282.6 24.0 all-gather.5
  320.7 33.0 reduce-scatter.6
  362.5 24.0 all-gather.7
  404.6 33.0 reduce-scatter.8
  444.7 24.0 all-gather.9
  483.7 33.0 reduce-scatter.10

commit v2 on v1

--- a/solution.py
+++ b/solution.py
@@ -530,12 +530,15 @@
     )(*arrays)
 
 
-def assemble(blocks, slots, first, rows, cols):
-    side = BLOCK_SIDE
+def assemble(blocks, slots, first, rows, widths):
+    side, cols = BLOCK_SIDE, sum(widths)
 
     def body(ids, *refs):
-        parts = [part for r in refs[:-1] for part in unpack(r[0])]
-        refs[-1][...] = jnp.concatenate(parts, axis=1)
+        base = 0
+        for out, width in zip(refs[cols:], widths):
+            parts = [part for r in refs[base : base + width] for part in unpack(r[0])]
+            out[...] = jnp.concatenate(parts, axis=1)
+            base += width
 
     def spec(c):
         return pl.BlockSpec(
@@ -548,9 +551,9 @@
             num_scalar_prefetch=1,
             grid=(rows,),
             in_specs=[spec(c) for c in range(cols)],
-            out_specs=pl.BlockSpec((side, side * cols), lambda r, ids: (r, 0)),
+            out_specs=[pl.BlockSpec((side, side * w), lambda r, ids: (r, 0)) for w in widths],
         ),
-        out_shape=jax.ShapeDtypeStruct((rows * side, cols * side), jnp.bfloat16),
+        out_shape=[jax.ShapeDtypeStruct((rows * side, w * side), jnp.bfloat16) for w in widths],
         compiler_params=pltpu.CompilerParams(vmem_limit_bytes=40 * 2**20),
         cost_estimate=pl.CostEstimate(
             flops=0, bytes_accessed=4 * rows * cols * side * side, transcendentals=0
@@ -559,14 +562,17 @@
     )(slots, *([blocks] * cols))
 
 
-def to_slots(g_in, g_out, slots, total):
+def to_slots(inner, outer, slots, total):
     side = BLOCK_SIDE
-    ri, ci = g_in.shape[0] // side, g_in.shape[1] // side
-    ro, co = g_out.shape[0] // side, g_out.shape[1] // side
+    ri, widths = inner[0].shape[0] // side, [g.shape[1] // side for g in inner]
+    ci, co = sum(widths), outer[0].shape[1] // side
+    heights = [g.shape[0] // side for g in outer]
+    ro = sum(heights)
     steps = ri + ro
-
-    def body(ids, gi, go, *rest):
-        out, buf, sem = rest[-3:]
+    n = len(inner) + len(outer)
+
+    def body(ids, *refs):
+        sources, (out, buf, sem) = refs[:n], refs[-3:]
         s = pl.program_id(0)
         half = lax.rem(s, 2)
 
@@ -574,11 +580,11 @@
             for c in range(count):
                 pltpu.make_async_copy(buf.at[which, c], out.at[0], sem.at[which, c]).wait()
 
-        def send(source, count, base):
+        def send(source, count, base, first=0):
             for c in range(count):
-                store_packed(buf, (half, c), source[:, c * side : (c + 1) * side])
+                store_packed(buf, (half, first + c), source[:, c * side : (c + 1) * side])
                 pltpu.make_async_copy(
-                    buf.at[half, c], out.at[ids[base + c]], sem.at[half, c]
+                    buf.at[half, first + c], out.at[ids[base + c]], sem.at[half, first + c]
                 ).start()
 
         @pl.when(jnp.logical_and(s >= 2, s - 2 < ri))
@@ -591,11 +597,19 @@
 
         @pl.when(s < ri)
         def _():
-            send(gi, ci, s * ci)
-
-        @pl.when(s >= ri)
-        def _():
-            send(go, co, ri * ci + (s - ri) * co)
+            first = 0
+            for source, width in zip(sources, widths):
+                send(source, width, s * ci + first, first)
+                first += width
+
+        base = ri
+        for source, height in zip(sources[len(inner) :], heights):
+
+            @pl.when(jnp.logical_and(s >= base, s < base + height))
+            def _():
+                send(source, co, ri * ci + (s - ri) * co)
+
+            base += height
 
         @pl.when(s == steps - 1)
         def _():
@@ -605,17 +619,25 @@
     extra, aliases = [], {}
     if total != ri * ci + ro * co:
         extra = [jnp.zeros((total, PACK_ROWS, LANES // 2), jnp.bfloat16)]
-        aliases = {3: 0}
+        aliases = {1 + n: 0}
+    specs = [
+        pl.BlockSpec((side, w * side), lambda s, ids: (jnp.minimum(s, ri - 1), 0)) for w in widths
+    ]
+    base = ri
+    for height in heights:
+        specs.append(
+            pl.BlockSpec(
+                (side, co * side),
+                lambda s, ids, base=base, height=height: (jnp.clip(s - base, 0, height - 1), 0),
+            )
+        )
+        base += height
     return pl.pallas_call(
         body,
         grid_spec=pltpu.PrefetchScalarGridSpec(
             num_scalar_prefetch=1,
             grid=(steps,),
-            in_specs=[
-                pl.BlockSpec((side, ci * side), lambda s, ids: (jnp.minimum(s, ri - 1), 0)),
-                pl.BlockSpec((side, co * side), lambda s, ids: (jnp.maximum(s - ri, 0), 0)),
-            ]
-            + [pl.BlockSpec(memory_space=pl.ANY)] * len(extra),
+            in_specs=specs + [pl.BlockSpec(memory_space=pl.ANY)] * len(extra),
             out_specs=pl.BlockSpec(memory_space=pl.ANY),
             scratch_shapes=[
                 pltpu.VMEM((2, max(ci, co), PACK_ROWS, LANES // 2), jnp.bfloat16),
@@ -629,30 +651,333 @@
         ),
         input_output_aliases=aliases,
         name="to_slots",
-    )(slots, g_in, g_out, *extra)
-
-
-def loss_terms(result, frozen, target, weights, upper_log, lower_log, mean_gap):
-    samples_n = result.shape[0]
-    shaped = result.reshape(samples_n, -1, 4, 8)
-    predicted = shaped[..., :4]
-    var_raw = shaped[..., 4:]
-    frozen_pred = frozen.reshape(samples_n, -1, 4, 8)[..., :4]
-    upper = upper_log[:, None, None, None]
-    lower = lower_log[:, None, None, None]
-    squared = jnp.mean((target - predicted) ** 2, axis=(1, 2, 3))
-    fraction = (var_raw + 1.0) / 2.0
-    log_var = fraction * upper + (1.0 - fraction) * lower
-    mean_diff = mean_gap[:, None, None, None] * (frozen_pred - target)
-    diverge = 0.5 * (
-        -1.0
-        + log_var
-        - lower
-        + jnp.exp(lower - log_var)
-        + mean_diff * mean_diff * jnp.exp(-log_var)
-    )
-    var_bound = jnp.mean(diverge, axis=(1, 2, 3)) / math.log(2.0)
-    return jnp.sum(weights * (squared + var_bound))
+    )(slots, *inner, *outer, *extra)
+
+
+CHUNK = 64
+
+
+def mean_of(x):
+    return jnp.sum(x, axis=-1, keepdims=True) * (1.0 / x.shape[-1])
+
+
+def norm_rows(x):
+    centred = x - mean_of(x)
+    inv_std = lax.rsqrt(mean_of(centred * centred) + 1e-06)
+    return centred * inv_std, inv_std
+
+
+def norm_rows_back(gradient, normed, inv_std):
+    return inv_std * (gradient - mean_of(gradient) - normed * mean_of(gradient * normed))
+
+
+def column_sum(x):
+    return jnp.sum(x, axis=0, keepdims=True)
+
+
+def times(a, b):
+    return jnp.dot(a, b, preferred_element_type=jnp.float32)
+
+
+def times_flipped(a, b):
+    return lax.dot_general(a, b, (((1,), (1,)), ((), ())), preferred_element_type=jnp.float32)
+
+
+def stage(number, inputs, outputs, shared, make):
+    rows, width = inputs[0].shape[1], MODEL_WIDTH
+    pieces = rows // CHUNK
+    n_in, n_out = len(inputs), len(outputs)
+
+    def body(*refs):
+        ins, outs = refs[:n_in], refs[n_in : n_in + n_out]
+        rest = refs[n_in + n_out :]
+        share = None
+        if shared:
+            share, rest = rest[0], rest[1:]
+        a_out, a_in, b_out, b_in, c_out, c_in, total, near, far = rest
+        me = lax.axis_index("mp")
+        core = me + 1 - 2 * lax.rem(me, 2)
+        across = lax.rem(me + 2, 4)
+        other = lax.rem(core + 2, 4)
+        to_core, to_across = {"mp": core}, {"mp": across}
+        partial, own, after = make(ins, outs, share)
+        barrier = pltpu.get_barrier_semaphore()
+        signal_to(barrier, to_core)
+        signal_to(barrier, to_across)
+        pl.semaphore_wait(barrier, 2)
+
+        copy_a = remote(a_out, a_in, near.at[0, 0], near.at[1, 0], to_core)
+        copy_c = remote(c_out, c_in, near.at[0, 1], near.at[1, 1], to_core)
+
+        def piece(i):
+            return pl.ds(i * CHUNK, CHUNK)
+
+        def copy_b(i):
+            return remote(
+                b_out.at[piece(i)], b_in.at[piece(i)], far.at[0, i], far.at[1, i], to_across
+            )
+
+        def share_far(group, i):
+            part = share.at[group, piece(i)]
+            return remote(part, part, far.at[2, i], far.at[3, i], to_across)
+
+        def share_near(group, i):
+            part = share.at[group, piece(i)]
+            return remote(part, part, near.at[2, i], near.at[3, i], to_core)
+
+        def pass_near(group, i):
+            part = share.at[group, piece(i)]
+            return remote(part, part, near.at[4, i], near.at[5, i], to_core)
+
+        a_out[...] = partial(other).astype(jnp.bfloat16)
+        copy_a.start()
+        total[...] = partial(across)
+        copy_a.wait_recv()
+        for i in range(pieces):
+            at = piece(i)
+            b_out[at] = (total[at] + a_in[at].astype(jnp.float32)).astype(jnp.bfloat16)
+            copy_b(i).start()
+        c_out[...] = partial(core).astype(jnp.bfloat16)
+        copy_c.start()
+        total[...] = partial(me)
+        copy_c.wait_recv()
+        for i in range(pieces):
+            at = piece(i)
+            copy_b(i).wait_recv()
+            result = own(
+                i * CHUNK, total[at] + c_in[at].astype(jnp.float32) + b_in[at].astype(jnp.float32)
+            )
+            if shared:
+                share[me, at] = result
+                share_far(me, i).start()
+                share_near(me, i).start()
+        if shared:
+            after(me)
+            for i in range(pieces):
+                share_near(core, i).wait_recv()
+            after(core)
+            for i in range(pieces):
+                share_far(across, i).wait_recv()
+                pass_near(across, i).start()
+            after(across)
+            for i in range(pieces):
+                pass_near(other, i).wait_recv()
+            after(other)
+        copy_a.wait_send()
+        copy_c.wait_send()
+        for i in range(pieces):
+            copy_b(i).wait_send()
+            if shared:
+                share_far(me, i).wait_send()
+                share_near(me, i).wait_send()
+                pass_near(across, i).wait_send()
+
+    vmem = pl.BlockSpec(memory_space=pltpu.VMEM)
+    out_shape = [jax.ShapeDtypeStruct(shape, dtype) for shape, dtype in outputs]
+    if shared:
+        out_shape.append(jax.ShapeDtypeStruct((4, rows, width), jnp.bfloat16))
+    landing = pltpu.VMEM((rows, width), jnp.bfloat16)
+    return pl.pallas_call(
+        body,
+        in_specs=[vmem] * n_in,
+        out_specs=[vmem] * len(out_shape),
+        out_shape=out_shape,
+        scratch_shapes=[landing] * 6
+        + [
+            pltpu.VMEM((rows, width), jnp.float32),
+            pltpu.SemaphoreType.DMA((6, max(pieces, 2))),
+            pltpu.SemaphoreType.DMA((4, pieces)),
+        ],
+        compiler_params=pltpu.CompilerParams(
+            collective_id=number, has_side_effects=True, vmem_limit_bytes=56 * 2**20
+        ),
+        name=f"stage_{number}",
+    )(*inputs)
+
+
+def attention_out_stage(mixed, w_o, w_up, start, rows, up_bias):
+    n, width, f32 = mixed.shape[1], MODEL_WIDTH, jnp.float32
+
+    def make(ins, outs, share):
+        mixed_ref, w_o_ref, w_up_ref, start_ref, rows_ref, up_ref = ins
+        attn_ref, middle_ref, hidden_ref, active_ref = outs
+
+        def partial(group):
+            return times(mixed_ref[group], w_o_ref[...])
+
+        def own(at, total):
+            at = slice(at, at + CHUNK)
+            attn = total + rows_ref[0:1]
+            middle = start_ref[at] + rows_ref[1:2] * attn
+            attn_ref[at] = attn
+            middle_ref[at] = middle
+            normed, _ = norm_rows(middle)
+            return (normed * (1.0 + rows_ref[2:3]) + rows_ref[3:4]).astype(jnp.bfloat16)
+
+        def after(group):
+            for at in range(0, n, CHUNK):
+                at = slice(at, at + CHUNK)
+                hidden = times(share[group, at], w_up_ref[...]) + up_ref[...]
+                hidden_ref[group, at] = hidden
+                active_ref[group, at] = tanh_gelu_activation(hidden).astype(jnp.bfloat16)
+
+        return partial, own, after
+
+    inner = w_up.shape[1]
+    return stage(
+        9,
+        [mixed, w_o, w_up, start, rows, up_bias],
+        [((n, width), f32), ((n, width), f32), ((4, n, inner), f32), ((4, n, inner), jnp.bfloat16)],
+        True,
+        make,
+    )
+
+
+def loss_stage(active, w_down, hidden, middle, rows, target, w_pred, w_raw, head_bias, facts):
+    n, width, f32, bf16 = active.shape[1], MODEL_WIDTH, jnp.float32, jnp.bfloat16
+    inner = active.shape[2]
+
+    def make(ins, outs, share):
+        active_ref, w_ref, hidden_ref, middle_ref, rows_ref, target_ref, wp_ref, wr_ref, bias_ref, facts_ref = ins
+        d_final_ref, head_in_ref, d_pred_ref, d_raw_ref, sums_ref, loss_ref, d_hidden_ref, up_sum_ref = outs
+        sums_ref[...] = jnp.zeros_like(sums_ref)
+        loss_ref[...] = jnp.zeros_like(loss_ref)
+        up_sum_ref[...] = jnp.zeros_like(up_sum_ref)
+
+        def partial(group):
+            return times(active_ref[group], w_ref[...])
+
+        def own(at, total):
+            at = slice(at, at + CHUNK)
+            branch = total + rows_ref[0:1]
+            gate, fscale = rows_ref[1:2], 1.0 + rows_ref[2:3]
+            normed, inv_std = norm_rows(middle_ref[at] + gate * branch)
+            head_in = (normed * fscale + rows_ref[3:4]).astype(bf16)
+            head_in_ref[at] = head_in
+            upper, lower, gap = facts_ref[0:1], facts_ref[1:2], facts_ref[2:3]
+            weight, share_of = facts_ref[3:4], facts_ref[4:5]
+            error = times(head_in, wp_ref[...]) + bias_ref[0:1] - target_ref[at]
+            fraction = (times(head_in, wr_ref[...]) + bias_ref[1:2] + 1.0) / 2.0
+            log_var = fraction * upper + (1.0 - fraction) * lower
+            gap = gap * error
+            ratio = jnp.exp(lower - log_var)
+            spread = gap * gap * jnp.exp(-log_var)
+            diverge = 0.5 * (-1.0 + log_var - lower + ratio + spread)
+            cells = 1.0 / (n * error.shape[1])
+            per_bit = cells / math.log(2.0)
+            loss_ref[...] += weight * column_sum(error * error * cells + diverge * per_bit)
+            d_pred = (share_of * (2.0 * cells) * error).astype(bf16)
+            d_raw = (
+                share_of * per_bit * 0.25 * (upper - lower) * (1.0 - ratio - spread)
+            ).astype(bf16)
+            d_pred_ref[at] = d_pred
+            d_raw_ref[at] = d_raw
+            d_head = times_flipped(d_pred, wp_ref[...]) + times_flipped(d_raw, wr_ref[...])
+            d_final = norm_rows_back(d_head * fscale, normed, inv_std)
+            d_final_ref[at] = d_final
+            d_branch = (gate * d_final).astype(bf16)
+            sums_ref[0:1] += column_sum(d_head)
+            sums_ref[1:2] += column_sum(d_head * normed)
+            sums_ref[2:3] += column_sum(d_final * branch)
+            sums_ref[3:4] += column_sum(d_branch.astype(f32))
+            return d_branch
+
+        def after(group):
+            for at in range(0, n, CHUNK):
+                at = slice(at, at + CHUNK)
+                d_active = times_flipped(share[group, at], w_ref[...])
+                d_hidden = (d_active * gelu_slope(hidden_ref[group, at])).astype(bf16)
+                d_hidden_ref[group, at] = d_hidden
+                up_sum_ref[...] += column_sum(d_hidden.astype(f32))
+
+        return partial, own, after
+
+    half = w_pred.shape[1]
+    return stage(
+        10,
+        [active, w_down, hidden, middle, rows, target, w_pred, w_raw, head_bias, facts],
+        [
+            ((n, width), f32),
+            ((n, width), bf16),
+            ((n, half), bf16),
+            ((n, half), bf16),
+            ((4, width), f32),
+            ((1, half), f32),
+            ((4, n, inner), bf16),
+            ((1, inner), f32),
+        ],
+        True,
+        make,
+    )
+
+
+def middle_back_stage(d_hidden, w_up, w_o, middle, d_final, attn, rows):
+    n, width, f32, bf16 = d_hidden.shape[1], MODEL_WIDTH, jnp.float32, jnp.bfloat16
+
+    def make(ins, outs, share):
+        d_hidden_ref, w_up_ref, w_o_ref, middle_ref, d_final_ref, attn_ref, rows_ref = ins
+        d_middle_ref, sums_ref, d_mixed_ref = outs
+        sums_ref[...] = jnp.zeros_like(sums_ref)
+
+        def partial(group):
+            return times_flipped(d_hidden_ref[group], w_up_ref[...])
+
+        def own(at, total):
+            at = slice(at, at + CHUNK)
+            normed, inv_std = norm_rows(middle_ref[at])
+            d_middle = d_final_ref[at] + norm_rows_back(total * (1.0 + rows_ref[0:1]), normed, inv_std)
+            d_middle_ref[at] = d_middle
+            d_attn = (rows_ref[1:2] * d_middle).astype(bf16)
+            sums_ref[0:1] += column_sum(total)
+            sums_ref[1:2] += column_sum(total * normed)
+            sums_ref[2:3] += column_sum(d_middle * attn_ref[at])
+            sums_ref[3:4] += column_sum(d_attn.astype(f32))
+            return d_attn
+
+        def after(group):
+            d_mixed_ref[group] = times_flipped(share[group], w_o_ref[...]).astype(bf16)
+
+        return partial, own, after
+
+    return stage(
+        11,
+        [d_hidden, w_up, w_o, middle, d_final, attn, rows],
+        [((n, width), f32), ((4, width), f32), ((4, n, w_o.shape[0]), bf16)],
+        True,
+        make,
+    )
+
+
+def start_back_stage(d_proj, w_qkv, start, d_middle, rows):
+    n, width, f32, bf16 = d_proj.shape[1], MODEL_WIDTH, jnp.float32, jnp.bfloat16
+
+    def make(ins, outs, share):
+        d_proj_ref, w_ref, start_ref, d_middle_ref, rows_ref = ins
+        d_start_ref, sums_ref = outs
+        sums_ref[...] = jnp.zeros_like(sums_ref)
+
+        def partial(group):
+            return times_flipped(d_proj_ref[group], w_ref[...])
+
+        def own(at, total):
+            at = slice(at, at + CHUNK)
+            normed, inv_std = norm_rows(start_ref[at])
+            d_start = d_middle_ref[at] + norm_rows_back(total * (1.0 + rows_ref[0:1]), normed, inv_std)
+            d_start = d_start.astype(bf16)
+            d_start_ref[at] = d_start
+            sums_ref[0:1] += column_sum(total)
+            sums_ref[1:2] += column_sum(total * normed)
+            sums_ref[2:3] += column_sum(d_start.astype(f32))
+
+        return partial, own, None
+
+    return stage(
+        12,
+        [d_proj, w_qkv, start, d_middle, rows],
+        [((n, width), bf16), ((3, width), f32)],
+        False,
+        make,
+    )
 
 
 def halves(x):
@@ -850,11 +1175,6 @@
     def by_columns(x):
         return x.reshape(x.shape[0], dp, cols).transpose(1, 0, 2)
 
-    def reduce_rows(x):
-        return lax.psum_scatter(
-            x.astype(bf16), "mp", scatter_dimension=0, tiled=True
-        ).astype(f32)
-
     def share_rows(x):
         return lax.all_gather(x, "mp", axis=0, tiled=True)
 
@@ -895,19 +1215,32 @@
     signal = all_columns(signal)
     final_mod = own(jnp.sum(final_mod, 0) + side_bias[5 * width : 7 * width])
 
-    w_in = assemble(blocks, slot_of_block, 0, row_blocks, col_blocks)
-    w_out = assemble(blocks, slot_of_block, first_out, out_blocks, row_blocks)
+    w_qkv, w_up, w_ada = assemble(
+        blocks,
+        slot_of_block,
+        0,
+        row_blocks,
+        [3 * query_width // BLOCK_SIDE, ff_width // BLOCK_SIDE, ada_width // BLOCK_SIDE],
+    )
+    (w_o,) = assemble(blocks, slot_of_block, first_out, query_width // BLOCK_SIDE, [row_blocks])
+    (w_down,) = assemble(
+        blocks,
+        slot_of_block,
+        first_out + query_width // BLOCK_SIDE * row_blocks,
+        ff_width // BLOCK_SIDE,
+        [row_blocks],
+    )
     own_bias = slice_bias[0]
     modul = lax.all_gather(
-        dense(signal, w_in[:, ada_column:]) + own_bias[2 * query_width + ff_width :],
+        dense(signal, w_ada) + own_bias[2 * query_width + ff_width :],
         "mp",
         axis=1,
         tiled=True,
     )
     own_modul = own(modul)
 
-    def part(position, source=own_modul):
-        return source[:, None, position * width : (position + 1) * width]
+    def part(position):
+        return modul[:, None, position * width : (position + 1) * width]
 
     def heads_of(inputs):
         return inputs.reshape(batch, -1, local_heads, HD)
@@ -919,13 +1252,13 @@
     initial = (
         dense(patches, w_patch) + side_bias[:width] + position_embedding(LATENT_SIDE // 2, width)
     )
-    normed_all, inv_std_all = layer_norm(initial)
-    attn_in = (normed_all * (1.0 + part(1, modul)) + part(0, modul)).astype(bf16)
-    start, normed_a, inv_std_a = own(initial), own(normed_all), own(inv_std_all)
+    normed_all, _ = layer_norm(initial)
+    attn_in = (normed_all * (1.0 + part(1)) + part(0)).astype(bf16)
+    start = own(initial)[0]
     own_patches = own(patches)
-    target = patchify(own(noise)).reshape(own_n, seq_len, 4, 4)
-
-    projected = dense(attn_in, w_in[:, : 3 * query_width])
+    target = patchify(own(noise))[0]
+
+    projected = dense(attn_in, w_qkv)
     queries = heads_of((projected[..., :query_width] + own_bias[:query_width]).astype(bf16))
     keys = heads_of(projected[..., query_width : 2 * query_width].astype(bf16))
     values = heads_of(
@@ -944,50 +1277,48 @@
         .reshape(batch, seq_len, query_width)
         .astype(bf16)
     )
-    attn = reduce_rows(dense(mixed, w_out[:query_width])) + side_bias[3 * width : 4 * width]
-    middle = start + part(2) * attn
-    normed_m, inv_std_m = layer_norm(middle)
-    mlp_in = share_rows((normed_m * (1.0 + part(4)) + part(3)).astype(bf16))
-    hidden = (
-        dense(mlp_in, w_in[:, 3 * query_width : ada_column])
-        + own_bias[2 * query_width : 2 * query_width + ff_width]
-    )
-    active = tanh_gelu_activation(hidden).astype(bf16)
-    branch = reduce_rows(dense(active, w_out[query_width:])) + side_bias[4 * width : 5 * width]
-    final = middle + part(5) * branch
-    normed_f, inv_std_f = layer_norm(final)
-    fscale, fshift = final_mod[:, None, width:], final_mod[:, None, :width]
-    head_in = (normed_f * (1.0 + fscale) + fshift).astype(bf16)
-    output = dense(head_in, w_head) + side_bias[7 * width :]
-
-    def objective(result):
-        return loss_terms(
-            result, output, target, own(loss_weights), own(upper_log), own(lower_log), own(mean_gap)
-        )
-
-    loss_part, loss_pull = jax.vjp(objective, output)
-    (seed_grad,) = loss_pull(jnp.ones_like(loss_part) / weight_total)
-
-    d_out = seed_grad.astype(bf16)
-    d_headin = back_dense(d_out, w_head)
-    d_final = norm_back(d_headin * (1.0 + fscale), normed_f, inv_std_f)
-    d_fmod = jnp.concatenate([jnp.sum(d_headin, 1), jnp.sum(d_headin * normed_f, 1)], 1).astype(bf16)
-    own_branch = (part(5) * d_final).astype(bf16)
-    d_gate2 = jnp.sum(d_final * branch, 1)
-    d_branch = share_rows(own_branch)
+
+    def rows_of(*rows):
+        return jnp.concatenate([r.reshape(1, width) for r in rows], 0)
+
+    shift1, scale1, gate1, shift2, scale2, gate2 = (own_modul[0, i * width : (i + 1) * width] for i in range(6))
+    attn, middle, hidden, active, mlp_in = attention_out_stage(
+        mixed,
+        w_o,
+        w_up,
+        start,
+        rows_of(side_bias[3 * width : 4 * width], gate1, scale2, shift2),
+        own_bias[2 * query_width : 2 * query_width + ff_width].reshape(1, ff_width),
+    )
+
+    def halves_of(x):
+        x = x.reshape(x.shape[:-1] + (4, 8))
+        return x[..., :4].reshape(x.shape[:-2] + (16,)), x[..., 4:].reshape(x.shape[:-2] + (16,))
+
+    w_pred, w_raw = halves_of(w_head)
+    own_weight = own(loss_weights)
+    facts = [own(upper_log), own(lower_log), own(mean_gap), own_weight, own_weight / weight_total]
+    d_final, head_in, d_pred, d_raw, sums_f, loss_part, d_hidden, up_sum, d_branch = loss_stage(
+        active,
+        w_down,
+        hidden,
+        middle,
+        rows_of(side_bias[4 * width : 5 * width], gate2, final_mod[0, width:], final_mod[0, :width]),
+        target,
+        w_pred,
+        w_raw,
+        jnp.stack(halves_of(side_bias[7 * width :])),
+        jnp.broadcast_to(jnp.stack(facts), (5, 16)),
+    )
+    loss_part = jnp.sum(loss_part)
+    d_fmod = sums_f[:2].reshape(1, 2 * width).astype(bf16)
     g_down = weight_grad(active, d_branch).astype(bf16)
-    d_active = back_dense(d_branch, w_out[query_width:])
-    d_hidden = (d_active * gelu_slope(hidden)).astype(bf16)
+    d_middle, sums_m, d_mixed, d_attn = middle_back_stage(
+        d_hidden, w_up, w_o, middle, d_final, attn, rows_of(scale2, gate1)
+    )
     g_up = weight_grad(mlp_in, d_hidden).astype(bf16)
-    d_mlpin = reduce_rows(back_dense(d_hidden, w_in[:, 3 * query_width : ada_column]))
-    d_shift2 = jnp.sum(d_mlpin, 1)
-    d_scale2 = jnp.sum(d_mlpin * normed_m, 1)
-    d_middle = d_final + norm_back(d_mlpin * (1.0 + part(4)), normed_m, inv_std_m)
-    own_attn = (part(2) * d_middle).astype(bf16)
-    d_gate1 = jnp.sum(d_middle * attn, 1)
-    d_attn = share_rows(own_attn)
     g_outp = weight_grad(mixed, d_attn).astype(bf16)
-    d_mixed = heads_of(back_dense(d_attn, w_out[:query_width]).astype(bf16))
+    d_mixed = heads_of(d_mixed)
     probs = jnp.exp(
         jnp.einsum("slhe,smhe->shlm", queries, keys, preferred_element_type=f32) * score_scale
         - log_total
@@ -1007,28 +1338,22 @@
     flat_v = d_values.reshape(batch, seq_len, query_width)
     d_proj = jnp.concatenate([flat_q, d_keys.reshape(batch, seq_len, query_width), flat_v], 2)
     g_qkv = weight_grad(attn_in, d_proj).astype(bf16)
-    d_attnin = reduce_rows(back_dense(d_proj, w_in[:, : 3 * query_width]))
-    d_shift1 = jnp.sum(d_attnin, 1)
-    d_scale1 = jnp.sum(d_attnin * normed_a, 1)
-    d_start = (
-        d_middle + norm_back(d_attnin * (1.0 + part(1)), normed_a, inv_std_a)
-    ).astype(bf16)
-    d_mod_own = jnp.concatenate([d_shift1, d_scale1, d_gate1, d_shift2, d_scale2, d_gate2], 1)
+    d_start, sums_a = start_back_stage(d_proj, w_qkv, start, d_middle, scale1.reshape(1, width))
+    d_mod_own = jnp.concatenate(
+        [sums_a[0], sums_a[1], sums_m[2], sums_m[0], sums_m[1], sums_f[2]]
+    ).reshape(1, 6 * width)
     d_modul = lax.dynamic_slice_in_dim(
         share_rows(d_mod_own.astype(bf16)), my_mp * ada_width, ada_width, 1
     )
     g_ada = weight_grad(signal, d_modul).astype(bf16)
 
     slot_grad = to_slots(
-        jnp.concatenate([g_qkv, g_up, g_ada], 1),
-        jnp.concatenate([g_outp, g_down], 0),
-        slot_of_block,
-        slot_of_block.shape[0],
+        [g_qkv, g_up, g_ada], [g_outp, g_down], slot_of_block, slot_of_block.shape[0]
     )
     red_blocks = reduce_blocks(slot_grad)
 
     d_fmod_all, d_signal = exchange(
-        [(d_fmod, "gather"), (by_columns(back_dense(d_modul, w_in[:, ada_column:])), "scatter")],
+        [(d_fmod, "gather"), (by_columns(back_dense(d_modul, w_ada)), "scatter")],
         EVERY,
         5,
     )
@@ -1040,15 +1365,15 @@
     d_second = d_cond.astype(bf16)
     g_second = weight_grad(first_s, d_second)
     g_class = jnp.einsum("sc,sd->cd", onehot.astype(f32), d_cond, precision=exact_precision_flag)
-    small = jnp.concatenate(
-        [weight_grad(own_patches, d_start), jnp.einsum("...i,...j->ij", d_out, head_in, preferred_element_type=f32)], 0
-    )
-    slice_part = jnp.concatenate(
-        [total_of(flat_q), total_of(flat_v), total_of(d_hidden), total_of(d_modul)]
-    )
-    side_part = jnp.concatenate(
-        [total_of(d_start), total_of(own_attn), total_of(own_branch), total_of(d_out), loss_part[None]]
-    )
+
+    def interleave(p, r):
+        parts = [x.reshape(x.shape[:-1] + (4, 4)) for x in (p, r)]
+        return jnp.concatenate(parts, -1).reshape(p.shape[:-1] + (32,))
+
+    d_out = interleave(d_pred, d_raw)
+    small = jnp.concatenate([weight_grad(own_patches[0], d_start), weight_grad(d_out, head_in)], 0)
+    slice_part = jnp.concatenate([total_of(flat_q), total_of(flat_v), up_sum[0], total_of(d_modul)])
+    side_part = jnp.concatenate([sums_a[2], sums_m[3], sums_f[3], total_of(d_out), loss_part[None]])
     bias_part = jnp.concatenate([slice_part, side_part])
     rows = -(-bias_part.shape[0] // 1024) * 8
     bias_part = jnp.pad(bias_part, (0, rows * 128 - bias_part.shape[0])).reshape(rows, 128)

time: 957 us -> 827 us (0.86)
  waiting for transfers between devices: 161 us -> 0 us
  Pallas kernels: 484 us -> 632 us
  matrix products: 102 us -> 56.8 us
  other arithmetic: 67.4 us -> 37.9 us
  local copies, waits for them, and re-layouts: 95.4 us -> 70.5 us
  between operations: 26 us -> 10.2 us
    pallas_call x0 -> x4, Pallas kernels: none -> 149 us  [stage(): pl.pallas_call(body, in_specs=[vmem] * n_in, out_specs=[vmem] * len(out_s...]
    reduce_scatter x4 -> x0, waiting for transfers between devices: 89.4 us -> none  [reduce_rows(): lax.psum_scatter(x.astype(bf16), 'mp', scatter_dimension=0, tiled=True)]
    all_gather x3 -> x0, waiting for transfers between devices: 71.1 us -> none  [share_rows(): return lax.all_gather(x, 'mp', axis=0, tiled=True)]
    dot_general x8 -> x3, matrix products: 33.6 us -> 7.31 us  [back_dense(): jnp.einsum('...j,ij->...i', gradient, weight, preferred_element_type=jnp....]
    dot_general x11 -> x7, matrix products: 28.1 us -> 12.1 us  [dense(): return jnp.dot(operand, weight, preferred_element_type=jnp.float32)]
    concatenate x4 -> x1, local copies, waits for them, and re-layouts: 15.8 us -> 0.02 us  [per_device(): jnp.concatenate([sums_a[0], sums_a[1], sums_m[2], sums_m[0], sums_m[1], s...]
    reduce_sum x8 -> x2, other arithmetic: 12.1 us -> 1.92 us  [the longest x1 1.24 us: per_device(): loss_part = jnp.sum(loss_part)]
    reduce_sum x7 -> x4, other arithmetic: 10.7 us -> 0.99 us  [total_of(): jnp.sum(inputs.astype(jnp.float32), axis=tuple(range(inputs.ndim - 1)))]
  transfers between devices with their start and end apart: 7 -> 0, of which waited for: 7 -> 0; matrix products, arithmetic and copies ran while one was open for 4% -> 0% of each run, Pallas kernels for 0% -> 0%
where the time goes in v2:
time: 827 us; the launch traced here: 819 us
  Pallas kernels  632 us (76%)
  local copies, waits for them, and re-layouts  70.5 us (9%)
  matrix products  56.8 us (7%)
  other arithmetic  37.9 us (5%)
  blocking collectives  11.4 us (1%)
  between operations  10.2 us (1%)
    pallas_call x4, Pallas kernels, stage(): pl.pallas_call(body, in_specs=[vmem] * n_in, out_specs=[vmem] * len(out_s...  149 us
    pallas_call x1, Pallas kernels, reduce_blocks(): pl.pallas_call(reduce_body, in_specs=[pl.BlockSpec(memory_space=pltpu.VME...  147 us
    pallas_call x1, Pallas kernels, gather_blocks(): pl.pallas_call(gather_body, in_specs=[pl.BlockSpec(memory_space=pl.ANY)],...  132 us
    pallas_call x1, Pallas kernels, shampoo(): pl.pallas_call(shampoo_body, grid=(count,), in_specs=[pl.BlockSpec(memory...  102 us
    pallas_call x7, Pallas kernels, exchange(): pl.pallas_call(body, in_specs=[vmem] * len(arrays), out_specs=[vmem] * le...  76.9 us
    dot_general x10, matrix products, weight_grad(): jnp.einsum('...i,...j->ij', operand, gradient, preferred_element_type=jnp...  26.2 us
    unnamed x152, local copies, waits for them, and re-layouts  23.1 us

profile of v2, /device:TPU:0, one launch (start us, length us, event | category | flops | bytes accessed | tf_op | source)
XLA Modules:
  0.0 818.7 jit_solution(1229913394225110417)
XLA Ops:
  19.6 11.6 %exchange_2.1 = (f32[8,4,3]{2,1,0:T(4,128)S(1)}, bf16[8,144,48]{2,1,0:T(8,128)(2,1)S(1)}) custom-call(f32[4,3]{1,0:T(4,128)S(1)} %pad_maximum_fusion.14.refs_0_, bf16[144,48]{1,0:T(8,128)(2,1)S(1)} %pad_maximum_fusion.5.refs_1_), custom_call_target="tpu_custom_call" | custom-call | tf_op jit(solution)/shard_map/exchange_2/pallas_call | solution.py:520
  33.2 2.7 stack.52
  38.6 8.8 %exchange_3.1 = bf16[8,32,144]{2,1,0:T(8,128)(2,1)S(1)} custom-call(bf16[32,144]{1,0:T(8,128)(2,1)S(1)} %get-tuple-element.151.refs_0_), custom_call_target="tpu_custom_call" | custom-call | tf_op jit(solution)/shard_map/exchange_3/pallas_call | solution.py:520
  49.0 1.9 divide_convert_fusion.4
  51.2 8.9 %exchange_4.1 = (bf16[8,4,144]{2,1,0:T(4,128)(2,1)S(1)}, f32[8,4,2304]{2,1,0:T(4,128)S(1)}) custom-call(bf16[8,4,144]{2,1,0:T(4,128)(2,1)S(1)} %reshape.356.refs_0_, f32[8,4,2304]{2,1,0:T(4,128)S(1)} %reshape.357.refs_1_), custom_call_target="tpu_custom_call" | custom-call | tf_op jit(solution)/shard_map/exchange_4/pallas_call | solution.py:520
  63.4 2.1 copy.211
  65.8 6.6 pack_blocks.1.x_ref
  76.7 131.6 %gather_blocks.1.refs_0_.refs_1_.refs_2_.refs_3_.refs_4_.refs_5_.refs_6_.refs_7_.refs_8_.refs_9_.refs_10_.refs_11_.refs_12_ = bf16[72,656,128]{2,1,0:T(8,128)(2,1)} custom-call(bf16[9,656,128]{2,1,0:T(8,128)(2,1)} %pack_blocks.1.x_ref), custom_call_target="tpu_custom_call" | custom-call | tf_op jit(solution)/shard_map/gather_blocks/pallas_call | solution.py:305
  208.3 4.4 copy-done
  213.6 3.9 assemble.5.refs_1_
  219.1 6.8 assemble.3
  226.0 1.9 copy-done.2
  228.8 5.8 all-gather
  236.7 5.3 fusion.12
  246.3 41.6 %stage_9.1 = (f32[256,1152]{1,0:T(8,128)}, f32[256,1152]{1,0:T(8,128)}, f32[4,256,1152]{2,1,0:T(8,128)}, bf16[4,256,1152]{2,1,0:T(8,128)(2,1)}, bf16[4,256,1152]{2,1,0:T(8,128)(2,1)}) custom-call(bf16[4,256,288]{2,1,0:T(8,128)(2,1)} %copy.221.refs_0_, bf16[288,1152]{1,0:T(8,128)(2,1)} %copy-done.5, bf16[1152,1152]{1,0:T(8,128)(2,1)} %copy-done.3, ...), custom_call_target="tpu_custom_call" | custom-call | tf_op jit(solution)/shard_map/stage_9/pallas_call | solution.py:780
  287.9 45.4 %stage_10.1 = (f32[256,1152]{1,0:T(8,128)}, bf16[256,1152]{1,0:T(8,128)(2,1)}, bf16[256,16]{1,0:T(8,128)(2,1)}, bf16[256,16]{1,0:T(8,128)(2,1)}, f32[4,1152]{1,0...) custom-call(bf16[4,256,1152]{2,1,0:T(8,128)(2,1)} %get-tuple-element, ...), custom_call_target="tpu_custom_call" | custom-call | tf_op jit(solution)/shard_map/stage_10/pallas_call | solution.py:780
  334.6 38.8 %stage_11.1 = (f32[256,1152]{1,0:T(8,128)}, f32[4,1152]{1,0:T(4,128)}, bf16[4,256,288]{2,1,0:T(8,128)(2,1)}, bf16[4,256,1152]{2,1,0:T(8,128)(2,1)}) custom-call(bf16[4,256,1152]{2,1,0:T(8,128)(2,1)} %get-tuple-element.70.refs_0_, bf16[1152,1152]{1,0:T(8,128)(2,1)} %copy-done.3, bf16[288,1152]{1,0:T(8,128)(2,1)} %copy-done.5, ...), custom_call_target="tpu_custom_call" | custom-call | tf_op jit(solution)/shard_map/stage_11/pallas_call | solution.py:780
  373.5 5.2 fusion.refs_1_
  379.8 2.9 fusion.5.refs_3_
  383.0 4.8 fusion.1.refs_4_
  390.1 3.5 multiply_reduce_fusion.1
  400.8 2.3 pad_maximum_fusion.refs_0_
  403.1 23.0 %stage_12.1 = (bf16[256,1152]{1,0:T(8,128)(2,1)}, f32[3,1152]{1,0:T(4,128)}) custom-call(bf16[4,256,864]{2,1,0:T(8,128)(2,1)} %pad_maximum_fusion.refs_0_, bf16[1152,864]{1,0:T(8,128)(2,1)} %copy-done.8, f32[256,1152]{1,0:T(8,128)} %dynamic-slice_bitcast_fusion.refs_3_.refs_2_, f32[256,1152]{1,0:T(8,128)} %get-tuple-element.74.refs_3_, ...), custom_call_target="tpu_custom_call" | custom-call | tf_op jit(solution)/shard_map/stage_12/pallas_call | solution.py:780
  426.2 6.5 bitcast_convert_fusion
  433.1 2.9 copy.243.refs_0_
  436.0 5.6 all-gather.1
  441.7 3.3 fusion.46
  448.1 12.5 %exchange_5.1 = (bf16[32,1,2304]{2,1,0:T(2,128)(2,1)S(1)}, f32[32,4,144]{2,1,0:T(4,128)S(1)}) custom-call(bf16[1,2304]{1,0:T(2,128)(2,1)S(1)} %bitcast.211, f32[8,4,144]{2,1,0:T(4,128)S(1)} %bitcast.210), custom_call_target="tpu_custom_call" | custom-call | tf_op jit(solution)/shard_map/exchange_5/pallas_call | solution.py:520
  460.7 2.0 convert_reduce_fusion.3
  463.3 2.0 fusion.29
  465.9 1.8 reshape.377
  468.8 21.7 %exchange_6.1 = (f32[8,32,144]{2,1,0:T(8,128)S(1)}, f32[8,48,144]{2,1,0:T(8,128)S(1)}, f32[8,56,128]{2,1,0:T(8,128)S(1)}) custom-call(f32[8,32,144]{2,1,0:T(8,128)S(1)} %bitcast.206, f32[8,48,144]{2,1,0:T(8,128)S(1)} %bitcast.203, f32[56,128]{1,0:T(8,128)S(1)} %pad_bitcast_fusion.refs_2_), custom_call_target="tpu_custom_call" | custom-call | tf_op jit(solution)/shard_map/exchange_6/pallas_call | solution.py:520
  500.5 5.0 exchange_7.1
  509.6 2.0 fusion.35
  512.7 2.5 concatenate.69
  515.2 2.3 multiply_reduce_fusion.5
  521.9 3.2 convolution_convert_fusion
  525.1 6.3 copy.244.refs_2_
  531.5 2.2 copy-done.1
  533.6 1.7 copy-done.6
  535.4 1.7 copy-done.7
  537.1 8.0 to_slots.1.x_ref
  545.2 146.6 %reduce_blocks.1.g_ref = f32[9,656,128]{2,1,0:T(8,128)} custom-call(bf16[72,656,128]{2,1,0:T(8,128)(2,1)} %to_slots.1.x_ref), custom_call_target="tpu_custom_call" | custom-call | tf_op jit(solution)/shard_map/reduce_blocks/pallas_call | solution.py:452
  691.9 3.4 multiply_reduce_fusion.3
  695.9 8.4 %exchange_8.1 = f32[32,2,145]{2,1,0:T(2,128)S(1)} custom-call(f32[2,145]{1,0:T(2,128)S(1)} %concatenate.71.refs_0_), custom_call_target="tpu_custom_call" | custom-call | tf_op jit(solution)/shard_map/exchange_8/pallas_call | solution.py:520
  707.4 5.0 fusion.74
  712.4 3.1 fusion.72
  715.5 101.6 %shampoo.1 = (f32[9,288,288]{2,1,0:T(8,128)}, f32[9,2,288,288]{3,2,1,0:T(8,128)}, f32[9,288,288]{2,1,0:T(8,128)}, bf16[9,288,288]{2,1,0:T(8,128)(2,1)}) custom-call(f32[1]{0:T(128)} %bitcast.62.clip_ref, f32[9,656,128]{2,1,0:T(8,128)} %reduce_blocks.1.g_ref, f32[9,2,288,288]{3,2,1,0:T(8,128)} %bitcast.252, f32[9,288,288]{2,1,0:T(8,128)} %bitcast.222), custom_call_target="tpu_custom_call" | custom-call | flops 56757583872 | bytes 25380864 | tf_op jit(solution)/shard_map/shampoo/pallas_call | solution.py:1091
  (304 shorter events, 76.9 us)
Async XLA Ops:
  19.4 31.5 %copy-start.31 = (bf16[144,2336]{1,0:T(8,128)(2,1)}, bf16[144,2336]{1,0:T(8,128)(2,1)S(1)}, u32[]{:S(2)}) copy-start(bf16[144,2336]{1,0:T(8,128)(2,1)S(1)} %convert_element_type.197) | copy-start | bytes 2018308
  36.9 23.7 %copy-start.57 = (bf16[32,128]{1,0:T(8,128)(2,1)}, bf16[32,128]{1,0:T(8,128)(2,1)S(1)}, u32[]{:S(2)}) copy-start(bf16[32,128]{1,0:T(8,128)(2,1)S(1)} %get-tuple-element.146) | copy-start | bytes 24580
  36.9 23.7 %copy-start.58 = (bf16[32,128]{1,0:T(8,128)(2,1)}, bf16[32,128]{1,0:T(8,128)(2,1)S(1)}, u32[]{:S(2)}) copy-start(bf16[32,128]{1,0:T(8,128)(2,1)S(1)} %get-tuple-element.147) | copy-start | bytes 24580
  47.7 3.2 copy-start.37
  60.3 165.7 %copy-start.47 = (bf16[4,1152]{1,0:T(4,128)(2,1)}, bf16[4,1152]{1,0:T(4,128)(2,1)S(1)}, u32[]{:S(2)}) copy-start(bf16[4,1152]{1,0:T(4,128)(2,1)S(1)} %reshape.358) | copy-start | bytes 27652
  73.4 2.2 copy-start.16
  76.7 131.6 %copy-start.12 = (s32[72]{0:T(128)S(1)}, s32[72]{0:T(128)}, u32[]{:S(2)}) copy-start(s32[72]{0:T(128)} %ids.7) | copy-start | bytes 868
  208.3 4.4 copy-start
  213.6 4.0 copy-start.5
  225.9 2.9 copy-start.3
  225.9 10.7 %copy-start.8 = (bf16[1152,864]{1,0:T(8,128)(2,1)}, bf16[1152,864]{1,0:T(8,128)(2,1)S(1)}, u32[]{:S(2)}) copy-start(bf16[1152,864]{1,0:T(8,128)(2,1)S(1)} %get-tuple-element.63.refs_1_) | copy-start | bytes 5971972
  245.1 42.8 %copy-start.41 = (bf16[4,4,72,256]{3,2,1,0:T(8,128)(2,1)}, bf16[4,4,72,256]{3,2,1,0:T(8,128)(2,1)S(1)}, u32[]{:S(2)}) copy-start(bf16[4,4,72,256]{3,2,1,0:T(8,128)(2,1)S(1)} %fusion.16) | copy-start | bytes 1769476
  334.6 38.8 %copy-start.32 = (bf16[4,256,1152]{2,1,0:T(8,128)(2,1)S(1)}, bf16[4,256,1152]{2,1,0:T(8,128)(2,1)}, u32[]{:S(2)}) copy-start(bf16[4,256,1152]{2,1,0:T(8,128)(2,1)} %get-tuple-element.70.refs_0_) | copy-start | bytes 7077892
  334.6 38.8 %copy-start.66 = (bf16[4,256,1152]{2,1,0:T(8,128)(2,1)S(1)}, bf16[4,256,1152]{2,1,0:T(8,128)(2,1)}, u32[]{:S(2)}) copy-start(bf16[4,256,1152]{2,1,0:T(8,128)(2,1)} %get-tuple-element.89) | copy-start | bytes 7077892
  373.5 5.3 copy-start.36
  373.5 5.5 copy-start.61
  373.5 5.6 copy-start.52
  373.5 5.7 copy-start.51
  373.5 5.8 copy-start.39
  379.8 3.0 copy-start.33
  379.8 3.3 copy-start.65
  383.0 4.8 copy-start.14
  390.1 3.6 copy-start.15
  397.8 3.0 copy-start.29
  403.1 23.0 %copy-start.20 = (bf16[4,256,864]{2,1,0:T(8,128)(2,1)S(1)}, bf16[4,256,864]{2,1,0:T(8,128)(2,1)}, u32[]{:S(2)}) copy-start(bf16[4,256,864]{2,1,0:T(8,128)(2,1)} %pad_maximum_fusion.refs_0_) | copy-start | bytes 5308420
  426.2 6.6 copy-start.40
  426.2 6.8 copy-start.60
  441.7 5.3 copy-start.44
  465.3 46.3 %copy-start.38 = (bf16[32,1152]{1,0:T(8,128)(2,1)S(1)}, bf16[32,1152]{1,0:T(8,128)(2,1)}, u32[]{:S(2)}) copy-start(bf16[32,1152]{1,0:T(8,128)(2,1)} %copy-done.37) | copy-start | bytes 221188
  465.3 27.3 %copy-start.49 = (f32[2304]{0:T(1024)}, f32[2304]{0:T(1024)S(1)}, u32[]{:S(2)}) copy-start(f32[2304]{0:T(1024)S(1)} %convert_reduce_fusion.2) | copy-start | bytes 27652
  492.6 19.0 %copy-start.43 = (f32[32,144]{1,0:T(8,128)S(1)}, f32[32,144]{1,0:T(8,128)}, u32[]{:S(2)}) copy-start(f32[32,144]{1,0:T(8,128)} %copy-done.42) | copy-start | bytes 55300
  515.2 6.7 copy-start.45
  515.2 6.7 copy-start.48
  531.5 2.2 copy-start.1
  691.7 14.1 %copy-start.56 = (f32[8096]{0:T(1024)S(1)}, f32[8096]{0:T(1024)}, u32[]{:S(2)}) copy-start(f32[8096]{0:T(1024)} %constant_dynamic-update-slice_fusion.6) | copy-start | bytes 97156
  691.8 14.2 %copy-start.50 = (f32[2304]{0:T(1024)S(1)}, f32[2304]{0:T(1024)}, u32[]{:S(2)}) copy-start(f32[2304]{0:T(1024)} %copy-done.49) | copy-start | bytes 27652
  691.8 14.2 %copy-start.53 = (f32[1,3456]{1,0:T(1,128)S(1)}, f32[1,3456]{1,0:T(1,128)}, u32[]{:S(2)}) copy-start(f32[1,3456]{1,0:T(1,128)} %param.30) | copy-start | bytes 41476
  691.8 14.2 %copy-start.62 = (f32[1,3456]{1,0:T(1,128)S(1)}, f32[1,3456]{1,0:T(1,128)}, u32[]{:S(2)}) copy-start(f32[1,3456]{1,0:T(1,128)} %param.37) | copy-start | bytes 41476
  691.8 14.2 %copy-start.63 = (f32[1,3456]{1,0:T(1,128)S(1)}, f32[1,3456]{1,0:T(1,128)}, u32[]{:S(2)}) copy-start(f32[1,3456]{1,0:T(1,128)} %param.36) | copy-start | bytes 41476
  691.8 14.9 %copy-start.46 = (f32[8096]{0:T(1024)S(1)}, f32[8096]{0:T(1024)}, u32[]{:S(2)}) copy-start(f32[8096]{0:T(1024)} %param.31) | copy-start | bytes 97156
  691.8 14.9 %copy-start.54 = (f32[8096]{0:T(1024)S(1)}, f32[8096]{0:T(1024)}, u32[]{:S(2)}) copy-start(f32[8096]{0:T(1024)} %param.39) | copy-start | bytes 97156
  691.8 14.9 %copy-start.55 = (f32[8096]{0:T(1024)S(1)}, f32[8096]{0:T(1024)}, u32[]{:S(2)}) copy-start(f32[8096]{0:T(1024)} %param.38) | copy-start | bytes 97156
  691.8 15.5 %copy-start.17 = (f32[2425,144]{0,1:T(8,128)S(1)}, f32[2425,144]{0,1:T(8,128)}, u32[]{:S(2)}) copy-start(f32[2425,144]{0,1:T(8,128)} %concatenate.69) | copy-start | bytes 4190404
  691.9 15.5 %copy-start.22 = (f32[2425,144]{0,1:T(8,128)S(1)}, f32[2425,144]{0,1:T(8,128)}, u32[]{:S(2)}) copy-start(f32[2425,144]{0,1:T(8,128)} %param.28) | copy-start | bytes 4190404
  707.4 5.0 copy-start.19
  707.4 5.0 copy-start.24
  707.4 5.0 copy-start.34
  707.4 5.0 copy-start.35
  (19 other events, 23.8 us)

commit v3 on v2

--- a/solution.py
+++ b/solution.py
@@ -194,272 +194,6 @@
 def grid_place():
     me = lax.axis_index("dp")
     return me // COLUMNS, me % COLUMNS
-
-
-def greet_neighbours(z, y):
-    barrier = pltpu.get_barrier_semaphore()
-    signal_to(barrier, {"dp": z * COLUMNS + 1 - y})
-
-    @pl.when(z < LAYERS - 1)
-    def _():
-        signal_to(barrier, {"dp": (z + 1) * COLUMNS + y})
-
-    @pl.when(z > 0)
-    def _():
-        signal_to(barrier, {"dp": (z - 1) * COLUMNS + y})
-
-    pl.semaphore_wait(barrier, jnp.where((z > 0) & (z < LAYERS - 1), 3, 2))
-
-
-def gather_body(x_ref, out_ref, local_sem, up_sem, down_sem, side_sem, recv_sem):
-    count = x_ref.shape[0]
-    z, y = grid_place()
-    greet_neighbours(z, y)
-    peer = {"dp": z * COLUMNS + 1 - y}
-    above = {"dp": jnp.minimum(z + 1, LAYERS - 1) * COLUMNS + y}
-    below = {"dp": jnp.maximum(z - 1, 0) * COLUMNS + y}
-
-    def block(layer, column, k):
-        return out_ref.at[(layer * COLUMNS + column) * count + k]
-
-    def move(source, layer, k, send, place):
-        return remote(
-            source, block(layer, y, k), send.at[layer, k], recv_sem.at[layer, y, k], place
-        )
-
-    def arrival(layer, column, k):
-        here = block(layer, column, k)
-        return remote(here, here, side_sem.at[0, 0], recv_sem.at[layer, column, k], peer)
-
-    def send_own(k, _):
-        own = x_ref.at[k]
-
-        @pl.when(z < LAYERS - 1)
-        def _():
-            move(own, z, k, up_sem, above).start()
-
-        @pl.when(z > 0)
-        def _():
-            move(own, z, k, down_sem, below).start()
-
-        move(own, z, k, side_sem, peer).start()
-        pltpu.make_async_copy(own, block(z, y, k), local_sem.at[k]).start()
-        return 0
-
-    lax.fori_loop(0, count, send_own, 0)
-
-    for hop in range(1, LAYERS):
-
-        def pass_on(k, _):
-            @pl.when(z >= hop)
-            def _():
-                layer = z - hop
-                arrival(layer, y, k).wait_recv()
-
-                @pl.when(z < LAYERS - 1)
-                def _():
-                    move(block(layer, y, k), layer, k, up_sem, above).start()
-
-                move(block(layer, y, k), layer, k, side_sem, peer).start()
-
-            @pl.when(z + hop < LAYERS)
-            def _():
-                layer = z + hop
-                arrival(layer, y, k).wait_recv()
-
-                @pl.when(z > 0)
-                def _():
-                    move(block(layer, y, k), layer, k, down_sem, below).start()
-
-                move(block(layer, y, k), layer, k, side_sem, peer).start()
-
-            return 0
-
-        lax.fori_loop(0, count, pass_on, 0)
-
-    def finish(k, _):
-        pltpu.make_async_copy(x_ref.at[k], block(z, y, k), local_sem.at[k]).wait()
-        for layer in range(LAYERS):
-            arrival(layer, 1 - y, k).wait_recv()
-            move(block(layer, y, k), layer, k, side_sem, peer).wait_send()
-
-            @pl.when((z < LAYERS - 1) & (layer <= z))
-            def _():
-                move(block(layer, y, k), layer, k, up_sem, above).wait_send()
-
-            @pl.when((z > 0) & (layer >= z))
-            def _():
-                move(block(layer, y, k), layer, k, down_sem, below).wait_send()
-
-        return 0
-
-    lax.fori_loop(0, count, finish, 0)
-
-
-def gather_blocks(packed):
-    ways = lax.axis_size("dp")
-    if ways != COLUMNS * LAYERS:
-        return lax.all_gather(packed, "dp", axis=0, tiled=True)
-    count = packed.shape[0]
-    dma = pltpu.SemaphoreType.DMA
-    return pl.pallas_call(
-        gather_body,
-        in_specs=[pl.BlockSpec(memory_space=pl.ANY)],
-        out_specs=pl.BlockSpec(memory_space=pl.ANY),
-        out_shape=jax.ShapeDtypeStruct((count * ways,) + packed.shape[1:], packed.dtype),
-        scratch_shapes=[
-            dma((count,)),
-            dma((LAYERS, count)),
-            dma((LAYERS, count)),
-            dma((LAYERS, count)),
-            dma((LAYERS, COLUMNS, count)),
-        ],
-        compiler_params=pltpu.CompilerParams(collective_id=0, has_side_effects=True),
-        name="gather_blocks",
-    )(packed)
-
-
-def reduce_body(
-    x_ref, out_ref, side_buf, up_buf, down_buf, side_send, line_send, side_recv, up_recv, down_recv
-):
-    count = out_ref.shape[0]
-    z, y = grid_place()
-    greet_neighbours(z, y)
-    peer = {"dp": z * COLUMNS + 1 - y}
-    above = {"dp": jnp.minimum(z + 1, LAYERS - 1) * COLUMNS + y}
-    below = {"dp": jnp.maximum(z - 1, 0) * COLUMNS + y}
-
-    def across(layer, k):
-        return remote(
-            x_ref.at[(layer * COLUMNS + 1 - y) * count + k],
-            side_buf.at[layer, k],
-            side_send.at[layer, k],
-            side_recv.at[layer, k],
-            peer,
-        )
-
-    def upward(layer, k):
-        return remote(
-            side_buf.at[layer, k], up_buf.at[layer, k], line_send.at[layer, k], up_recv.at[layer, k], above
-        )
-
-    def downward(layer, k):
-        return remote(
-            side_buf.at[layer, k], down_buf.at[layer, k], line_send.at[layer, k], down_recv.at[layer, k], below
-        )
-
-    def pair_sum(layer, k):
-        across(layer, k).wait_recv()
-        own = x_ref[(layer * COLUMNS + y) * count + k].astype(jnp.float32)
-        return own + side_buf[layer, k].astype(jnp.float32)
-
-    for hop in range(LAYERS - 1, -1, -1):
-
-        def start(k, _):
-            @pl.when(z + hop < LAYERS)
-            def _():
-                across(z + hop, k).start()
-
-            if hop > 0:
-
-                @pl.when(z >= hop)
-                def _():
-                    across(z - hop, k).start()
-
-            return 0
-
-        lax.fori_loop(0, count, start, 0)
-
-    for hop in range(LAYERS - 1, 0, -1):
-
-        def step(k, _):
-            @pl.when(z + hop < LAYERS)
-            def _():
-                layer = z + hop
-                total = pair_sum(layer, k)
-
-                @pl.when(z > 0)
-                def _():
-                    upward(layer, k).wait_recv()
-                    side_buf[layer, k] = (total + up_buf[layer, k].astype(jnp.float32)).astype(
-                        jnp.bfloat16
-                    )
-
-                @pl.when(z == 0)
-                def _():
-                    side_buf[layer, k] = total.astype(jnp.bfloat16)
-
-                upward(layer, k).start()
-
-            @pl.when(z >= hop)
-            def _():
-                layer = z - hop
-                total = pair_sum(layer, k)
-
-                @pl.when(z < LAYERS - 1)
-                def _():
-                    downward(layer, k).wait_recv()
-                    side_buf[layer, k] = (total + down_buf[layer, k].astype(jnp.float32)).astype(
-                        jnp.bfloat16
-                    )
-
-                @pl.when(z == LAYERS - 1)
-                def _():
-                    side_buf[layer, k] = total.astype(jnp.bfloat16)
-
-                downward(layer, k).start()
-
-            return 0
-
-        lax.fori_loop(0, count, step, 0)
-
-    def last(k, _):
-        out_ref[k] = pair_sum(z, k)
-
-        @pl.when(z > 0)
-        def _():
-            upward(z, k).wait_recv()
-            out_ref[k] += up_buf[z, k].astype(jnp.float32)
-
-        @pl.when(z < LAYERS - 1)
-        def _():
-            downward(z, k).wait_recv()
-            out_ref[k] += down_buf[z, k].astype(jnp.float32)
-
-        for layer in range(LAYERS):
-            across(layer, k).wait_send()
-
-            @pl.when(layer > z)
-            def _():
-                upward(layer, k).wait_send()
-
-            @pl.when(layer < z)
-            def _():
-                downward(layer, k).wait_send()
-
-        return 0
-
-    lax.fori_loop(0, count, last, 0)
-
-
-def reduce_blocks(slots):
-    ways = lax.axis_size("dp")
-    if ways != COLUMNS * LAYERS:
-        return lax.psum_scatter(slots, "dp", scatter_dimension=0, tiled=True).astype(jnp.float32)
-    count = slots.shape[0] // ways
-    dma = pltpu.SemaphoreType.DMA
-    landing = pltpu.VMEM((LAYERS, count) + slots.shape[1:], jnp.bfloat16)
-    return pl.pallas_call(
-        reduce_body,
-        in_specs=[pl.BlockSpec(memory_space=pltpu.VMEM)],
-        out_specs=pl.BlockSpec(memory_space=pltpu.VMEM),
-        out_shape=jax.ShapeDtypeStruct((count,) + slots.shape[1:], jnp.float32),
-        scratch_shapes=[landing] * 3 + [dma((LAYERS, count))] * 5,
-        compiler_params=pltpu.CompilerParams(
-            collective_id=1, has_side_effects=True, vmem_limit_bytes=52 * 2**20
-        ),
-        name="reduce_blocks",
-    )(slots)
 
 
 EVERY = ("dp", "mp")
@@ -562,14 +296,17 @@
     )(slots, *([blocks] * cols))
 
 
-def to_slots(inner, outer, slots, total):
+def to_slots(inner, signal, d_modul, lower, slots, total):
     side = BLOCK_SIDE
     ri, widths = inner[0].shape[0] // side, [g.shape[1] // side for g in inner]
-    ci, co = sum(widths), outer[0].shape[1] // side
-    heights = [g.shape[0] // side for g in outer]
+    wide = d_modul.shape[1] // side
+    ci, co = sum(widths) + wide, lower[0].shape[1] // side
+    heights = [g.shape[0] // side for g in lower]
     ro = sum(heights)
     steps = ri + ro
-    n = len(inner) + len(outer)
+    n = len(inner) + 2 + len(lower)
+    batch = signal.shape[0]
+    signal = signal.reshape(batch, ri, side).transpose(1, 0, 2)
 
     def body(ids, *refs):
         sources, (out, buf, sem) = refs[:n], refs[-3:]
@@ -601,9 +338,10 @@
             for source, width in zip(sources, widths):
                 send(source, width, s * ci + first, first)
                 first += width
+            send(outer(refs[len(inner)][0], refs[len(inner) + 1][...]).astype(jnp.bfloat16), wide, s * ci + first, first)
 
         base = ri
-        for source, height in zip(sources[len(inner) :], heights):
+        for source, height in zip(sources[len(inner) + 2 :], heights):
 
             @pl.when(jnp.logical_and(s >= base, s < base + height))
             def _():
@@ -622,6 +360,10 @@
         aliases = {1 + n: 0}
     specs = [
         pl.BlockSpec((side, w * side), lambda s, ids: (jnp.minimum(s, ri - 1), 0)) for w in widths
+    ]
+    specs += [
+        pl.BlockSpec((1, batch, side), lambda s, ids: (jnp.minimum(s, ri - 1), 0, 0)),
+        pl.BlockSpec(d_modul.shape, lambda s, ids: (0, 0)),
     ]
     base = ri
     for height in heights:
@@ -651,7 +393,7 @@
         ),
         input_output_aliases=aliases,
         name="to_slots",
-    )(slots, *inner, *outer, *extra)
+    )(slots, *inner, signal, d_modul, *lower, *extra)
 
 
 CHUNK = 64
@@ -980,6 +722,690 @@
     )
 
 
+CROSS_LATE = 1
+
+
+class Push:
+    def __init__(self, source, landing, send, receive, n, me, place, row=None):
+        self.source, self.landing, self.send, self.receive = source, landing, send, receive
+        self.n, self.me, self.place, self.row = n, me, place, row
+
+    def _copy(self, i, sender, to):
+        source = self.source if self.row is None else self.source.at[self.row(to)]
+        return remote(
+            source, self.landing.at[sender], self.send.at[i], self.receive.at[sender], self.place(to)
+        )
+
+    def start(self):
+        def one(i, _):
+            self._copy(i, self.me, lax.rem(self.me + i, self.n)).start()
+            return 0
+
+        lax.fori_loop(1, self.n, one, 0)
+        own = self.source[...] if self.row is None else self.source[self.row(self.me)]
+        self.landing[self.me] = own
+
+    def wait(self):
+        def one(i, _):
+            to = lax.rem(self.me + i, self.n)
+            copy = self._copy(i, to, to)
+            copy.wait_recv()
+            copy.wait_send()
+            return 0
+
+        lax.fori_loop(1, self.n, one, 0)
+
+
+def head_body(
+    x_ref, tf_ref, facts_ref, shared_ref, w1_ref, w2_ref, class_ref, fada_ref, b1_ref, b2_ref,
+    out_ref, tf_all, facts_all, shared_all, first_t_ref, first_s_all, cond_ref, signal_ref,
+    signal_all, mod_ref,
+    packed, tf_land, first_s, signal_own, mod_own, mod_land, local_sem, up_sem, down_sem, side_sem,
+    up_other, down_other, recv_sem, send, receive,
+):
+    count, ways, f32, bf16 = x_ref.shape[0], LAYERS * COLUMNS, jnp.float32, jnp.bfloat16
+    batch, cols = tf_ref.shape[0], shared_ref.shape[0]
+    late = count - CROSS_LATE
+    z, y = grid_place()
+    me = lax.axis_index("dp")
+
+    def place(i):
+        return {"dp": i}
+
+    barrier = pltpu.get_barrier_semaphore()
+
+    def greet(i, _):
+        signal_to(barrier, place(lax.rem(me + i, ways)))
+        return 0
+
+    lax.fori_loop(1, ways, greet, 0)
+    pl.semaphore_wait(barrier, ways - 1)
+
+    def push(j, source, landing, row=None):
+        return Push(source, landing, send.at[j], receive.at[j], ways, me, place, row)
+
+    first = [
+        push(0, tf_ref, tf_land),
+        push(1, facts_ref, facts_all),
+        push(2, shared_ref, shared_all),
+    ]
+    for p in first:
+        p.start()
+
+    peer = {"dp": z * COLUMNS + 1 - y}
+    above = {"dp": jnp.minimum(z + 1, LAYERS - 1) * COLUMNS + y}
+    below = {"dp": jnp.maximum(z - 1, 0) * COLUMNS + y}
+
+    def block(layer, column, k):
+        return out_ref.at[(layer * COLUMNS + column) * count + k]
+
+    def move(source, layer, k, sem, to):
+        return remote(source, block(layer, y, k), sem.at[layer, k], recv_sem.at[layer, y, k], to)
+
+    def move_other(layer, k, sem, to):
+        here = block(layer, 1 - y, k)
+        return remote(here, here, sem.at[layer, k - late], recv_sem.at[layer, 1 - y, k], to)
+
+    def arrival(layer, column, k):
+        here = block(layer, column, k)
+        return remote(here, here, side_sem.at[0, 0], recv_sem.at[layer, column, k], peer)
+
+    def send_own(i, _):
+        k = count - 1 - i
+        store_packed(packed, (k,), x_ref[k].astype(bf16))
+        own = packed.at[k]
+        move(own, z, k, side_sem, peer).start()
+
+        @pl.when(z < LAYERS - 1)
+        def _():
+            move(own, z, k, up_sem, above).start()
+
+        @pl.when(z > 0)
+        def _():
+            move(own, z, k, down_sem, below).start()
+
+        pltpu.make_async_copy(own, block(z, y, k), local_sem.at[k]).start()
+        return 0
+
+    lax.fori_loop(0, count, send_own, 0)
+
+    for p in first:
+        p.wait()
+    for i in range(ways):
+        tf_all[i * batch : (i + 1) * batch] = tf_land[i]
+    first_t = times(tf_all[...].astype(bf16), w1_ref[...]) + b1_ref[...]
+    first_t_ref[...] = first_t
+    first_s[...] = swish_unit(first_t).astype(bf16)
+    second = push(3, first_s, first_s_all)
+    second.start()
+
+    for k in range(late, count):
+        arrival(z, 1 - y, k).wait_recv()
+
+        @pl.when(z < LAYERS - 1)
+        def _():
+            move_other(z, k, up_other, above).start()
+
+        @pl.when(z > 0)
+        def _():
+            move_other(z, k, down_other, below).start()
+
+    def run_hop(hop):
+        def pass_on(i, _):
+            k = count - 1 - i
+
+            @pl.when(z >= hop)
+            def _():
+                layer = z - hop
+                arrival(layer, y, k).wait_recv()
+
+                @pl.when(z < LAYERS - 1)
+                def _():
+                    move(block(layer, y, k), layer, k, up_sem, above).start()
+
+                @pl.when(k < late)
+                def _():
+                    move(block(layer, y, k), layer, k, side_sem, peer).start()
+
+            @pl.when(z + hop < LAYERS)
+            def _():
+                layer = z + hop
+                arrival(layer, y, k).wait_recv()
+
+                @pl.when(z > 0)
+                def _():
+                    move(block(layer, y, k), layer, k, down_sem, below).start()
+
+                @pl.when(k < late)
+                def _():
+                    move(block(layer, y, k), layer, k, side_sem, peer).start()
+
+            return 0
+
+        lax.fori_loop(0, count, pass_on, 0)
+        for k in range(late, count):
+
+            @pl.when(z >= hop)
+            def _():
+                layer = z - hop
+                arrival(layer, 1 - y, k).wait_recv()
+
+                @pl.when(z < LAYERS - 1)
+                def _():
+                    move_other(layer, k, up_other, above).start()
+
+            @pl.when(z + hop < LAYERS)
+            def _():
+                layer = z + hop
+                arrival(layer, 1 - y, k).wait_recv()
+
+                @pl.when(z > 0)
+                def _():
+                    move_other(layer, k, down_other, below).start()
+
+    run_hop(1)
+    second.wait()
+    cond = b2_ref[...]
+    for i in range(ways):
+        cond = cond + times(first_s_all[i], w2_ref[i * cols : (i + 1) * cols])
+        row = lax.broadcasted_iota(jnp.int32, (batch, class_ref.shape[0]), 1)
+        hot = (row == facts_all[i][:, 0:1].astype(jnp.int32)).astype(bf16)
+        cond_ref[i * batch : (i + 1) * batch] = times(hot, class_ref[...])
+    cond = cond + cond_ref[...]
+    cond_ref[...] = cond
+    signal = swish_unit(cond).astype(bf16)
+    signal_ref[...] = signal
+    mod = times(signal, fada_ref[...])
+    signal = signal.astype(f32)
+    for i in range(ways):
+        signal_own[i] = signal[i * batch : (i + 1) * batch]
+        mod_own[i] = mod[i * batch : (i + 1) * batch]
+    third = [
+        push(4, signal_own, signal_all, lambda to: to),
+        push(5, mod_own, mod_land, lambda to: to),
+    ]
+    for p in third:
+        p.start()
+    run_hop(2)
+    for p in third:
+        p.wait()
+    mod_ref[...] = jnp.sum(mod_land[...], axis=0)
+    run_hop(3)
+
+    def finish(k, _):
+        pltpu.make_async_copy(packed.at[k], block(z, y, k), local_sem.at[k]).wait()
+        for layer in range(LAYERS):
+
+            @pl.when(k < late)
+            def _():
+                arrival(layer, 1 - y, k).wait_recv()
+
+            @pl.when((k < late) | (layer == z))
+            def _():
+                move(block(layer, y, k), layer, k, side_sem, peer).wait_send()
+
+            @pl.when((z < LAYERS - 1) & (layer <= z))
+            def _():
+                move(block(layer, y, k), layer, k, up_sem, above).wait_send()
+
+            @pl.when((z > 0) & (layer >= z))
+            def _():
+                move(block(layer, y, k), layer, k, down_sem, below).wait_send()
+
+        return 0
+
+    lax.fori_loop(0, count, finish, 0)
+    for k in range(late, count):
+        for layer in range(LAYERS):
+
+            @pl.when((z < LAYERS - 1) & (layer <= z))
+            def _():
+                move_other(layer, k, up_other, above).wait_send()
+
+            @pl.when((z > 0) & (layer >= z))
+            def _():
+                move_other(layer, k, down_other, below).wait_send()
+
+
+def head(blocks, time_freq, facts, shared, w1, w2, w_class, w_fada, b1, b2):
+    ways, f32, bf16 = LAYERS * COLUMNS, jnp.float32, jnp.bfloat16
+    count, side = blocks.shape[0], BLOCK_SIDE
+    batch, cols, rows = time_freq.shape[0], shared.shape[0], time_freq.shape[0] * ways
+    fada = w_fada.shape[1]
+    dma = pltpu.SemaphoreType.DMA
+    vmem, anywhere = pl.BlockSpec(memory_space=pltpu.VMEM), pl.BlockSpec(memory_space=pl.ANY)
+    shape = jax.ShapeDtypeStruct
+    return pl.pallas_call(
+        head_body,
+        in_specs=[vmem] * 10,
+        out_specs=[anywhere] + [vmem] * 9,
+        out_shape=[
+            shape((count * ways, PACK_ROWS, LANES // 2), bf16),
+            shape((rows, time_freq.shape[1]), f32),
+            shape((ways,) + facts.shape, f32),
+            shape((ways,) + shared.shape, bf16),
+            shape((rows, cols), f32),
+            shape((ways, rows, cols), bf16),
+            shape((rows, cols), f32),
+            shape((rows, cols), bf16),
+            shape((ways, batch, cols), f32),
+            shape((batch, fada), f32),
+        ],
+        scratch_shapes=[
+            pltpu.VMEM((count, PACK_ROWS, LANES // 2), bf16),
+            pltpu.VMEM((ways,) + time_freq.shape, f32),
+            pltpu.VMEM((rows, cols), bf16),
+            pltpu.VMEM((ways, batch, cols), f32),
+            pltpu.VMEM((ways, batch, fada), f32),
+            pltpu.VMEM((ways, batch, fada), f32),
+            dma((count,)),
+            dma((LAYERS, count)),
+            dma((LAYERS, count)),
+            dma((LAYERS, count)),
+            dma((LAYERS, CROSS_LATE)),
+            dma((LAYERS, CROSS_LATE)),
+            dma((LAYERS, COLUMNS, count)),
+            dma((6, ways)),
+            dma((6, ways)),
+        ],
+        compiler_params=pltpu.CompilerParams(
+            collective_id=0, has_side_effects=True, vmem_limit_bytes=48 * 2**20
+        ),
+        name="head",
+    )(blocks, time_freq, facts, shared, w1, w2, w_class, w_fada, b1, b2)
+
+
+def outer(a, b):
+    return lax.dot_general(a, b, (((0,), (0,)), ((), ())), preferred_element_type=jnp.float32)
+
+
+def tail_body(
+    x_ref, fmod_ref, dsig_ref, small_ref, bias_ref, fada_ref, w2_ref, cond_ref, first_t_ref,
+    signal_ref, first_s_ref, tf_ref, facts_ref,
+    out_ref, g_cond_ref, g_head_ref, slice_ref, side_ref, mod_sum_ref, last_all,
+    side_buf, up_buf, down_buf, other_buf, up_other, down_other, fmod_land, dsig_land, small_land,
+    bias_land, dsig_all, first_own, first_land, small_own, small_mp, side_own, side_mp, fmod_all, last_own,
+    hot_buf,
+    side_send, line_send, side_recv, up_recv, down_recv, other_send, other_up, other_down,
+    send_all, recv_all, send_dp, recv_dp, send_mp, recv_mp,
+):
+    f32, bf16 = jnp.float32, jnp.bfloat16
+    count, ways, mp = out_ref.shape[0], LAYERS * COLUMNS, lax.axis_size("mp")
+    batch, cols = dsig_ref.shape[1], dsig_ref.shape[2]
+    everyone = ways * mp
+    late = count - CROSS_LATE
+    z, y = grid_place()
+    my_dp, my_mp = lax.axis_index("dp"), lax.axis_index("mp")
+    me = my_dp * mp + my_mp
+
+    def place_all(i):
+        return {"dp": i // mp, "mp": lax.rem(i, mp)}
+
+    barrier = pltpu.get_barrier_semaphore()
+
+    def greet(i, _):
+        signal_to(barrier, place_all(lax.rem(me + i, everyone)))
+        return 0
+
+    lax.fori_loop(1, everyone, greet, 0)
+    pl.semaphore_wait(barrier, everyone - 1)
+
+    def push_all(j, source, landing, row=None):
+        return Push(source, landing, send_all.at[j], recv_all.at[j], everyone, me, place_all, row)
+
+    def push_dp(j, source, landing, row=None):
+        return Push(
+            source, landing, send_dp.at[j], recv_dp.at[j], ways, my_dp, lambda i: {"dp": i}, row
+        )
+
+    def push_mp(j, source, landing):
+        return Push(source, landing, send_mp.at[j], recv_mp.at[j], mp, my_mp, lambda i: {"mp": i})
+
+    first = [
+        push_all(0, fmod_ref, fmod_land),
+        push_all(1, dsig_ref, dsig_land, lambda to: to // mp),
+    ]
+    second = [push_dp(0, small_ref, small_land, lambda to: to), push_dp(1, bias_ref, bias_land)]
+    for p in first + second:
+        p.start()
+
+    peer = {"dp": z * COLUMNS + 1 - y}
+    above = {"dp": jnp.minimum(z + 1, LAYERS - 1) * COLUMNS + y}
+    below = {"dp": jnp.maximum(z - 1, 0) * COLUMNS + y}
+
+    def slot(layer, column, k):
+        return (layer * COLUMNS + column) * count + k
+
+    def across(layer, k):
+        return remote(
+            x_ref.at[slot(layer, 1 - y, k)],
+            side_buf.at[layer, k],
+            side_send.at[layer, k],
+            side_recv.at[layer, k],
+            peer,
+        )
+
+    def cross_late(k):
+        return remote(
+            other_buf.at[z, k - late],
+            side_buf.at[z, k],
+            side_send.at[z, k],
+            side_recv.at[z, k],
+            peer,
+        )
+
+    def upward(layer, k):
+        return remote(
+            side_buf.at[layer, k], up_buf.at[layer, k], line_send.at[layer, k], up_recv.at[layer, k], above
+        )
+
+    def downward(layer, k):
+        return remote(
+            side_buf.at[layer, k], down_buf.at[layer, k], line_send.at[layer, k], down_recv.at[layer, k], below
+        )
+
+    def upward_other(layer, k):
+        j = k - late
+        return remote(
+            other_buf.at[layer, j], up_other.at[layer, j], other_send.at[layer, j], other_up.at[layer, j], above
+        )
+
+    def downward_other(layer, k):
+        j = k - late
+        return remote(
+            other_buf.at[layer, j], down_other.at[layer, j], other_send.at[layer, j], other_down.at[layer, j], below
+        )
+
+    def own_part(layer, k):
+        return x_ref[slot(layer, y, k)].astype(f32)
+
+    def pair_sum(layer, k):
+        across(layer, k).wait_recv()
+        return own_part(layer, k) + side_buf[layer, k].astype(f32)
+
+    for hop in range(LAYERS - 1, -1, -1):
+
+        def begin(k, _):
+            @pl.when(z + hop < LAYERS)
+            def _():
+                across(z + hop, k).start()
+
+            if hop > 0:
+
+                @pl.when(z >= hop)
+                def _():
+                    across(z - hop, k).start()
+
+            return 0
+
+        lax.fori_loop(0, late, begin, 0)
+
+    def along(total, stage_ref, layer, k, copy, landed, begins):
+        @pl.when(jnp.logical_not(begins))
+        def _():
+            copy(layer, k).wait_recv()
+            stage_ref[...] = (total + landed[...].astype(f32)).astype(bf16)
+
+        @pl.when(begins)
+        def _():
+            stage_ref[...] = total.astype(bf16)
+
+        copy(layer, k).start()
+
+    bottom, top = z == 0, z == LAYERS - 1
+
+    def run_hop(hop):
+        for k in range(late, count):
+            j = k - late
+
+            @pl.when(z + hop < LAYERS)
+            def _():
+                layer = z + hop
+                along(
+                    own_part(layer, k), side_buf.at[layer, k], layer, k, upward, up_buf.at[layer, k], bottom
+                )
+                along(
+                    x_ref[slot(layer, 1 - y, k)].astype(f32),
+                    other_buf.at[layer, j], layer, k, upward_other, up_other.at[layer, j], bottom,
+                )
+
+            @pl.when(z >= hop)
+            def _():
+                layer = z - hop
+                along(
+                    own_part(layer, k), side_buf.at[layer, k], layer, k, downward, down_buf.at[layer, k], top
+                )
+                along(
+                    x_ref[slot(layer, 1 - y, k)].astype(f32),
+                    other_buf.at[layer, j], layer, k, downward_other, down_other.at[layer, j], top,
+                )
+
+        def step(k, _):
+            @pl.when(z + hop < LAYERS)
+            def _():
+                layer = z + hop
+                along(
+                    pair_sum(layer, k), side_buf.at[layer, k], layer, k, upward, up_buf.at[layer, k], bottom
+                )
+
+            @pl.when(z >= hop)
+            def _():
+                layer = z - hop
+                along(
+                    pair_sum(layer, k), side_buf.at[layer, k], layer, k, downward, down_buf.at[layer, k], top
+                )
+
+            return 0
+
+        lax.fori_loop(0, late, step, 0)
+
+    run_hop(3)
+
+    for p in first:
+        p.wait()
+    for i in range(everyone):
+        fmod_all[i : i + 1] = fmod_land[i]
+    for i in range(ways):
+        dsig_all[i * batch : (i + 1) * batch] = jnp.sum(dsig_land[i * mp : (i + 1) * mp], axis=0)
+    d_fmod = fmod_all[...].astype(bf16)
+    d_signal = dsig_all[...] + times_flipped(d_fmod, fada_ref[...])
+    d_cond = d_signal * swish_slope(cond_ref[...])
+    d_second = d_cond.astype(bf16)
+    back = times_flipped(d_second, w2_ref[...])
+    for i in range(ways):
+        first_own[i] = back[:, i * cols : (i + 1) * cols]
+    for p in second:
+        p.wait()
+    third = push_dp(2, first_own, first_land, lambda to: to)
+
+    def square(x):
+        return jnp.sum(jnp.sum(x * x, axis=1, keepdims=True), axis=0, keepdims=True)
+
+    third.start()
+    shared_squares = jnp.zeros((1, 1), f32)
+    g_fada = outer(signal_ref[...], d_fmod)
+    g_head_ref[:, : g_fada.shape[1]] = g_fada
+    shared_squares += square(g_fada)
+    mod_sum = column_sum(fmod_all[...])
+    mod_sum_ref[...] = mod_sum
+    t2_row = PATCH_VALUES + FREQ
+    class_row = t2_row + MODEL_WIDTH
+    for i in range(ways):
+        g = outer(first_s_ref[i], d_second)
+        g_cond_ref[t2_row + i * cols : t2_row + (i + 1) * cols] = g
+        shared_squares += square(g)
+    for i in range(ways):
+        row = lax.broadcasted_iota(jnp.int32, (batch, hot_buf.shape[1]), 1)
+        hot = (row == facts_ref[i][:, 0:1].astype(jnp.int32)).astype(f32)
+        hot_buf[i * batch : (i + 1) * batch] = hot
+    hot = hot_buf[...].astype(bf16)
+    high = d_cond.astype(bf16)
+    rest = d_cond - high.astype(f32)
+    mid = rest.astype(bf16)
+    low = (rest - mid.astype(f32)).astype(bf16)
+    g_class = outer(hot, high) + outer(hot, mid) + outer(hot, low)
+    g_cond_ref[class_row:] = g_class[:CLASSES]
+    shared_squares += square(g_class)
+    run_hop(2)
+    third.wait()
+    d_first = (jnp.sum(first_land[...], axis=0) * swish_slope(first_t_ref[...])).astype(bf16)
+    g_first = outer(tf_ref[...].astype(bf16), d_first)
+    g_cond_ref[PATCH_VALUES:t2_row] = g_first
+    shared_squares += square(g_first)
+    small_own[...] = jnp.sum(small_land[...], axis=0)
+    bias = jnp.sum(bias_land[...], axis=0)
+    slice_rows = slice_ref.shape[0]
+    slice_ref[...] = bias[:slice_rows]
+    slice_squares = square(bias[:slice_rows])
+    side_own[...] = bias[slice_rows:]
+    fourth = [push_mp(0, small_own, small_mp), push_mp(1, side_own, side_mp)]
+    for p in fourth:
+        p.start()
+    run_hop(1)
+    for p in fourth:
+        p.wait()
+    small = jnp.sum(small_mp[...], axis=0)
+    g_cond_ref[:PATCH_VALUES] = small[:PATCH_VALUES]
+    g_head_ref[:, g_head_ref.shape[1] - (small.shape[0] - PATCH_VALUES) :] = small[PATCH_VALUES:].T
+    shared_squares += square(small)
+    side = jnp.sum(side_mp[...], axis=0)
+    side_ref[...] = side
+    every_squares = square(side[: side.shape[0] - 8]) + square(mod_sum)
+    column_sums = [column_sum(d_first.astype(f32)), column_sum(d_second.astype(f32))]
+    for s in column_sums:
+        shared_squares += square(s)
+    squares = shared_squares / mp + slice_squares / ways + every_squares / (ways * mp)
+
+    for k in range(late, count):
+        j = k - late
+        other_buf[z, j] = x_ref[slot(z, 1 - y, k)]
+
+        @pl.when(z > 0)
+        def _():
+            upward_other(z, k).wait_recv()
+            other_buf[z, j] = (other_buf[z, j].astype(f32) + up_other[z, j].astype(f32)).astype(bf16)
+
+        @pl.when(z < LAYERS - 1)
+        def _():
+            downward_other(z, k).wait_recv()
+            other_buf[z, j] = (other_buf[z, j].astype(f32) + down_other[z, j].astype(f32)).astype(bf16)
+
+        cross_late(k).start()
+
+    last_own[...] = jnp.zeros_like(last_own)
+
+    def final(k, _):
+        out_ref[k] = pair_sum(z, k)
+
+        @pl.when(z > 0)
+        def _():
+            upward(z, k).wait_recv()
+            out_ref[k] += up_buf[z, k].astype(f32)
+
+        @pl.when(z < LAYERS - 1)
+        def _():
+            downward(z, k).wait_recv()
+            out_ref[k] += down_buf[z, k].astype(f32)
+
+        total = out_ref[k]
+        last_own[2:3, :128] += column_sum(total * total)
+        return 0
+
+    lax.fori_loop(0, count, final, 0)
+    squares += jnp.sum(last_own[2:3, :128], axis=1, keepdims=True)
+    last_own[0:1, :cols] = column_sums[0]
+    last_own[1:2, :cols] = column_sums[1]
+    last_own[2:3, :128] = jnp.broadcast_to(squares, (1, 128))
+    fifth = push_all(2, last_own, last_all)
+    fifth.start()
+
+    def sent(k, _):
+        for layer in range(LAYERS):
+
+            @pl.when(k < late)
+            def _():
+                across(layer, k).wait_send()
+
+            @pl.when(layer > z)
+            def _():
+                upward(layer, k).wait_send()
+
+            @pl.when(layer < z)
+            def _():
+                downward(layer, k).wait_send()
+
+        return 0
+
+    lax.fori_loop(0, count, sent, 0)
+    for k in range(late, count):
+        cross_late(k).wait_send()
+        for layer in range(LAYERS):
+
+            @pl.when(layer > z)
+            def _():
+                upward_other(layer, k).wait_send()
+
+            @pl.when(layer < z)
+            def _():
+                downward_other(layer, k).wait_send()
+
+    fifth.wait()
+
+
+def tail(slots, d_fmod, d_signal, small, bias, w_fada, w2, cond, first_t, signal, first_s, tf, facts, slice_rows):
+    ways, mp, f32, bf16 = LAYERS * COLUMNS, lax.axis_size("mp"), jnp.float32, jnp.bfloat16
+    count, packed = slots.shape[0] // ways, slots.shape[1:]
+    batch, cols = d_signal.shape[1:]
+    rows, fada = batch * ways, w_fada.shape[1]
+    side_rows = bias.shape[0] - slice_rows
+    dma, vmem = pltpu.SemaphoreType.DMA, pl.BlockSpec(memory_space=pltpu.VMEM)
+    shape, scratch = jax.ShapeDtypeStruct, pltpu.VMEM
+    landing = scratch((LAYERS, count) + packed, bf16)
+    few = scratch((LAYERS, CROSS_LATE) + packed, bf16)
+    out_shape = [
+        shape((count,) + packed, f32),
+        shape((PATCH_VALUES + FREQ + MODEL_WIDTH + CLASSES, cols), f32),
+        shape((cols, fada + small.shape[1] - PATCH_VALUES), f32),
+        shape((slice_rows, 128), f32),
+        shape((side_rows, 128), f32),
+        shape((1, fada), f32),
+        shape((ways * mp, 8, LANES), f32),
+    ]
+    return pl.pallas_call(
+        tail_body,
+        in_specs=[vmem] * 13,
+        out_specs=[vmem] * len(out_shape),
+        out_shape=out_shape,
+        scratch_shapes=[landing] * 3
+        + [few] * 3
+        + [
+            scratch((ways * mp, 1, fada), f32),
+            scratch((ways * mp, batch, cols), f32),
+            scratch(small.shape, f32),
+            scratch((ways,) + bias.shape, f32),
+            scratch((rows, cols), f32),
+            scratch((ways, rows, cols), f32),
+            scratch((ways, rows, cols), f32),
+            scratch(small.shape[1:], f32),
+            scratch((mp,) + small.shape[1:], f32),
+            scratch((side_rows, 128), f32),
+            scratch((mp, side_rows, 128), f32),
+            scratch((rows, fada), f32),
+            scratch((8, LANES), f32),
+            scratch((rows, 1024), f32),
+        ]
+        + [dma((LAYERS, count))] * 5
+        + [dma((LAYERS, CROSS_LATE))] * 3
+        + [dma((3, ways * mp))] * 2
+        + [dma((3, ways))] * 2
+        + [dma((2, mp))] * 2,
+        compiler_params=pltpu.CompilerParams(
+            collective_id=1, has_side_effects=True, vmem_limit_bytes=58 * 2**20
+        ),
+        name="tail",
+    )(slots, d_fmod, d_signal, small, bias, w_fada, w2, cond, first_t, signal, first_s, tf, facts)
+
+
 def halves(x):
     high = x.astype(jnp.bfloat16)
     return high, (x - high.astype(jnp.float32)).astype(jnp.bfloat16)
@@ -1048,10 +1474,6 @@
 
 def shampoo_body(clip_ref, g_ref, stat_ref, old_ref, clipped_ref, new_stat_ref, new_ref, low_ref):
     side = BLOCK_SIDE
-    g_main, g_tail = unpack(g_ref[0] * clip_ref[0])
-    clipped_ref[0, :, :LANES] = g_main
-    clipped_ref[0, :, LANES:] = g_tail
-    g = jnp.concatenate([g_main, g_tail], axis=1)
 
     def unit(width, offset):
         row = lax.broadcasted_iota(jnp.int32, (side, width), 0)
@@ -1059,41 +1481,48 @@
         return (row == col).astype(jnp.float32)
 
     eye_main, eye_tail = unit(LANES, 0), unit(TAIL, LANES)
-    flipped = g.T
-    g_right = (right_form(g[:, :LANES]), right_form(g[:, LANES:]))
-    f_right = (right_form(flipped[:, :LANES]), right_form(flipped[:, LANES:]))
-    g_left = left_form(g[:, :LANES], g[:, LANES:])
-    f_left = left_form(flipped[:, :LANES], flipped[:, LANES:])
-    pairs = []
-    for k, (left, right) in enumerate(((g_left, f_right), (f_left, g_right))):
-        main, tail = symmetric_product(left, *right)
-        main = 0.5 * stat_ref[0, k, :, :LANES] + 0.5 * main
-        tail = 0.5 * stat_ref[0, k, :, LANES:] + 0.5 * tail
-        new_stat_ref[0, k, :, :LANES] = main
-        new_stat_ref[0, k, :, LANES:] = tail
-        pairs.append((main, tail))
-    left_root, right_root = inverse_roots(pairs, eye_main, eye_tail)
-    root_left = left_form(*left_root)
-    half = left_form(product(root_left, g_right[0]), product(root_left, g_right[1]))
-    for part, (a, b) in zip(right_root, ((0, LANES), (LANES, side))):
-        direction = product(half, right_form(part))
-        old = old_ref[0, :, a:b]
-        new = old - shampoo_rate * (direction + decay_rate * old)
-        new_ref[0, :, a:b] = new
-        low_ref[0, :, a:b] = new.astype(jnp.bfloat16)
+    pairs, g_rights = [], []
+    for j in range(g_ref.shape[0]):
+        g_main, g_tail = unpack(g_ref[j] * clip_ref[0])
+        clipped_ref[j, :, :LANES] = g_main
+        clipped_ref[j, :, LANES:] = g_tail
+        flipped = jnp.concatenate([g_main, g_tail], axis=1).T
+        g_right = (right_form(g_main), right_form(g_tail))
+        f_right = (right_form(flipped[:, :LANES]), right_form(flipped[:, LANES:]))
+        g_left = left_form(g_main, g_tail)
+        f_left = left_form(flipped[:, :LANES], flipped[:, LANES:])
+        g_rights.append(g_right)
+        for k, (left, right) in enumerate(((g_left, f_right), (f_left, g_right))):
+            main, tail = symmetric_product(left, *right)
+            main = 0.5 * stat_ref[j, k, :, :LANES] + 0.5 * main
+            tail = 0.5 * stat_ref[j, k, :, LANES:] + 0.5 * tail
+            new_stat_ref[j, k, :, :LANES] = main
+            new_stat_ref[j, k, :, LANES:] = tail
+            pairs.append((main, tail))
+    roots = inverse_roots(pairs, eye_main, eye_tail)
+    for j, g_right in enumerate(g_rights):
+        root_left = left_form(*roots[2 * j])
+        half = left_form(product(root_left, g_right[0]), product(root_left, g_right[1]))
+        for part, (a, b) in zip(roots[2 * j + 1], ((0, LANES), (LANES, side))):
+            direction = product(half, right_form(part))
+            old = old_ref[j, :, a:b]
+            new = old - shampoo_rate * (direction + decay_rate * old)
+            new_ref[j, :, a:b] = new
+            low_ref[j, :, a:b] = new.astype(jnp.bfloat16)
 
 
 def shampoo(clip_factor, gradients, stats, old_blocks):
     count, side = gradients.shape[0], BLOCK_SIDE
-    one = pl.BlockSpec((1, side, side), lambda i: (i, 0, 0))
-    two = pl.BlockSpec((1, 2, side, side), lambda i: (i, 0, 0, 0))
+    group = next(g for g in (3, 2, 1) if count % g == 0)
+    one = pl.BlockSpec((group, side, side), lambda i: (i, 0, 0))
+    two = pl.BlockSpec((group, 2, side, side), lambda i: (i, 0, 0, 0))
     block = jax.ShapeDtypeStruct((count, side, side), jnp.float32)
     return pl.pallas_call(
         shampoo_body,
-        grid=(count,),
+        grid=(count // group,),
         in_specs=[
             pl.BlockSpec(memory_space=pltpu.SMEM),
-            pl.BlockSpec((1, PACK_ROWS, LANES // 2), lambda i: (i, 0, 0)),
+            pl.BlockSpec((group, PACK_ROWS, LANES // 2), lambda i: (i, 0, 0)),
             two,
             one,
         ],
@@ -1104,7 +1533,7 @@
             block,
             jax.ShapeDtypeStruct((count, side, side), jnp.bfloat16),
         ],
-        compiler_params=pltpu.CompilerParams(vmem_limit_bytes=56 * 2**20),
+        compiler_params=pltpu.CompilerParams(vmem_limit_bytes=60 * 2**20),
         cost_estimate=pl.CostEstimate(
             flops=count * 44 * 6 * side**3, bytes_accessed=count * 34 * side * side, transcendentals=0
         ),
@@ -1178,42 +1607,51 @@
     def share_rows(x):
         return lax.all_gather(x, "mp", axis=0, tiled=True)
 
-    blocks = gather_blocks(pack_blocks(slotted_block_weights[0]))
-
+    tuned = dp == COLUMNS * LAYERS
     cond_low, head_low = cond_tables.astype(bf16), head_tables.astype(bf16)
-    facts, shared = exchange(
-        [
-            (jnp.stack([timesteps.astype(f32), labels.astype(f32), loss_weights], 1), "gather"),
-            (jnp.concatenate([cond_low[:PATCH_VALUES].T, head_low[:, 2 * width :]], 1), "gather"),
-        ],
-        "dp",
-        2,
-    )
-    facts, shared = facts.reshape(samples, 3), shared.reshape(width, -1)
-    all_steps, all_labels = facts[:, 0].astype(jnp.int32), facts[:, 1].astype(jnp.int32)
-    weight_total = jnp.sum(facts[:, 2])
+    w_first, w_second = cond_low[PATCH_VALUES:t2_row], cond_low[t2_row:class_row]
+    w_class = jnp.pad(cond_low[class_row:], ((0, 1024 - CLASSES), (0, 0)))
+    w_fada = head_low[:, : 2 * width]
+    b_first = my_cols(side_bias[width : 2 * width])
+    b_second = my_cols(side_bias[2 * width : 3 * width])
+    time_freq = time_features(timesteps, FREQ).astype(bf16).astype(f32)
+    facts = jnp.pad(jnp.stack([labels.astype(f32), loss_weights], 1), ((0, 0), (0, 126)))
+    shared = jnp.concatenate([cond_low[:PATCH_VALUES].T, head_low[:, 2 * width :]], 1)
+    if tuned:
+        (
+            blocks, time_freq, facts, shared, first_t, first_s, cond_vec, signal_cols, signal, final_mod,
+        ) = head(
+            slotted_block_weights[0], time_freq, facts, shared, w_first, w_second, w_class, w_fada,
+            b_first[None], b_second[None],
+        )
+    else:
+        blocks = lax.all_gather(pack_blocks(slotted_block_weights[0]), "dp", axis=0, tiled=True)
+        time_freq, facts, shared = exchange(
+            [(time_freq, "gather"), (facts, "gather"), (shared, "gather")], "dp", 2
+        )
+        time_freq = time_freq.reshape(samples, FREQ)
+        first_t = dense(time_freq.astype(bf16), w_first) + b_first
+        (first_s,) = exchange([(swish_unit(first_t).astype(bf16), "gather")], "dp", 3)
+        labels_all = facts[:, :, 0].reshape(samples, 1).astype(jnp.int32)
+        onehot = labels_all == jnp.arange(1024, dtype=jnp.int32)[None, :]
+        cond_vec = (
+            dense(all_columns(first_s), w_second) + b_second + dense(onehot.astype(bf16), w_class)
+        )
+        signal_cols = swish_unit(cond_vec).astype(bf16)
+        signal, final_mod = exchange(
+            [
+                (signal_cols.astype(f32).reshape(dp, batch, cols), "scatter"),
+                (dense(signal_cols, w_fada).reshape(dp, batch, 2 * width), "scatter"),
+            ],
+            "dp",
+            4,
+        )
+        final_mod = jnp.sum(final_mod, 0)
+    weight_total = jnp.sum(facts[:, :, 1])
+    shared = shared.reshape(width, -1)
     w_patch, w_head = shared[:, :PATCH_VALUES].T, shared[:, PATCH_VALUES:]
-    time_freq = time_features(all_steps, FREQ).astype(bf16)
-    onehot = all_labels[:, None] == jnp.arange(CLASSES, dtype=jnp.int32)[None, :]
-    first_t = dense(time_freq, cond_low[PATCH_VALUES:t2_row]) + my_cols(side_bias[width : 2 * width])
-    (first_s,) = exchange([(swish_unit(first_t).astype(bf16), "gather")], "dp", 3)
-    first_s = all_columns(first_s)
-    cond_vec = (
-        dense(first_s, cond_low[t2_row:class_row])
-        + my_cols(side_bias[2 * width : 3 * width])
-        + dense(onehot.astype(bf16), cond_low[class_row:])
-    )
-    signal_cols = swish_unit(cond_vec).astype(bf16)
-    signal, final_mod = exchange(
-        [
-            (signal_cols.reshape(dp, batch, cols), "scatter"),
-            (dense(signal_cols, head_low[:, : 2 * width]).reshape(dp, batch, 2 * width), "scatter"),
-        ],
-        "dp",
-        4,
-    )
-    signal = all_columns(signal)
-    final_mod = own(jnp.sum(final_mod, 0) + side_bias[5 * width : 7 * width])
+    signal = all_columns(signal).astype(bf16)
+    final_mod = own(final_mod + side_bias[5 * width : 7 * width])
 
     w_qkv, w_up, w_ada = assemble(
         blocks,
@@ -1297,7 +1735,7 @@
 
     w_pred, w_raw = halves_of(w_head)
     own_weight = own(loss_weights)
-    facts = [own(upper_log), own(lower_log), own(mean_gap), own_weight, own_weight / weight_total]
+    loss_facts = [own(upper_log), own(lower_log), own(mean_gap), own_weight, own_weight / weight_total]
     d_final, head_in, d_pred, d_raw, sums_f, loss_part, d_hidden, up_sum, d_branch = loss_stage(
         active,
         w_down,
@@ -1308,7 +1746,7 @@
         w_pred,
         w_raw,
         jnp.stack(halves_of(side_bias[7 * width :])),
-        jnp.broadcast_to(jnp.stack(facts), (5, 16)),
+        jnp.broadcast_to(jnp.stack(loss_facts), (5, 16)),
     )
     loss_part = jnp.sum(loss_part)
     d_fmod = sums_f[:2].reshape(1, 2 * width).astype(bf16)
@@ -1345,73 +1783,102 @@
     d_modul = lax.dynamic_slice_in_dim(
         share_rows(d_mod_own.astype(bf16)), my_mp * ada_width, ada_width, 1
     )
-    g_ada = weight_grad(signal, d_modul).astype(bf16)
 
     slot_grad = to_slots(
-        [g_qkv, g_up, g_ada], [g_outp, g_down], slot_of_block, slot_of_block.shape[0]
-    )
-    red_blocks = reduce_blocks(slot_grad)
-
-    d_fmod_all, d_signal = exchange(
-        [(d_fmod, "gather"), (by_columns(back_dense(d_modul, w_ada)), "scatter")],
-        EVERY,
-        5,
-    )
-    d_fmod_all = d_fmod_all.reshape(samples, 2 * width)
-    g_fada = weight_grad(signal_cols, d_fmod_all)
-    d_signal = jnp.sum(d_signal.reshape(dp, mp, batch, cols), 1).reshape(samples, cols)
-    d_signal = d_signal + back_dense(d_fmod_all, head_low[:, : 2 * width])
-    d_cond = d_signal * swish_slope(cond_vec)
-    d_second = d_cond.astype(bf16)
-    g_second = weight_grad(first_s, d_second)
-    g_class = jnp.einsum("sc,sd->cd", onehot.astype(f32), d_cond, precision=exact_precision_flag)
+        [g_qkv, g_up], signal, d_modul, [g_outp, g_down], slot_of_block, slot_of_block.shape[0]
+    )
+    d_signal = by_columns(back_dense(d_modul, w_ada))
 
     def interleave(p, r):
         parts = [x.reshape(x.shape[:-1] + (4, 4)) for x in (p, r)]
         return jnp.concatenate(parts, -1).reshape(p.shape[:-1] + (32,))
 
+    def lanes(x, rows):
+        return jnp.pad(x, (0, rows * 128 - x.shape[0])).reshape(rows, 128)
+
     d_out = interleave(d_pred, d_raw)
-    small = jnp.concatenate([weight_grad(own_patches[0], d_start), weight_grad(d_out, head_in)], 0)
+    small = by_columns(
+        jnp.concatenate([weight_grad(own_patches[0], d_start), weight_grad(d_out, head_in)], 0)
+    )
     slice_part = jnp.concatenate([total_of(flat_q), total_of(flat_v), up_sum[0], total_of(d_modul)])
-    side_part = jnp.concatenate([sums_a[2], sums_m[3], sums_f[3], total_of(d_out), loss_part[None]])
-    bias_part = jnp.concatenate([slice_part, side_part])
-    rows = -(-bias_part.shape[0] // 1024) * 8
-    bias_part = jnp.pad(bias_part, (0, rows * 128 - bias_part.shape[0])).reshape(rows, 128)
-    d_first, small, bias_part = exchange(
+    side_part = jnp.concatenate([sums_a[2], sums_m[3], sums_f[3], total_of(d_out)])
+    slice_rows, side_rows = (-(-x.shape[0] // 1024) * 8 for x in (slice_part, side_part))
+    bias_part = jnp.concatenate(
+        [lanes(slice_part, slice_rows), lanes(side_part, side_rows), lanes(loss_part[None], 8)], 0
+    )
+    if tuned:
+        red_blocks, red_cond, red_head, red_slice, side_sum, side_mod, last = tail(
+            slot_grad, d_fmod.astype(f32), d_signal, small, bias_part, w_fada, w_second, cond_vec,
+            first_t, signal_cols, first_s, time_freq, facts, slice_rows,
+        )
+    else:
+        red_blocks = lax.psum_scatter(slot_grad, "dp", scatter_dimension=0, tiled=True).astype(f32)
+        d_fmod_all, d_signal = exchange(
+            [(d_fmod.astype(f32), "gather"), (d_signal, "scatter")], EVERY, 5
+        )
+        d_fmod_all = d_fmod_all.reshape(samples, 2 * width).astype(bf16)
+        d_signal = jnp.sum(d_signal.reshape(dp, mp, batch, cols), 1).reshape(samples, cols)
+        d_signal = d_signal + back_dense(d_fmod_all, w_fada)
+        d_cond = d_signal * swish_slope(cond_vec)
+        d_second = d_cond.astype(bf16)
+        d_first, small, bias_part = exchange(
+            [
+                (by_columns(back_dense(d_second, w_second)), "scatter"),
+                (small, "scatter"),
+                (bias_part, "gather"),
+            ],
+            "dp",
+            6,
+        )
+        d_first = (jnp.sum(d_first, 0) * swish_slope(first_t)).astype(bf16)
+        bias_part = jnp.sum(bias_part, 0)
+        red_slice = bias_part[:slice_rows]
+        small, side_sum = exchange(
+            [(jnp.sum(small, 0), "gather"), (bias_part[slice_rows:], "gather")], "mp", 7
+        )
+        small, side_sum = jnp.sum(small, 0), jnp.sum(side_sum, 0)
+        side_mod = total_of(d_fmod_all)
+        g_class = jnp.einsum(
+            "sc,sd->cd", onehot[:, :CLASSES].astype(f32), d_cond, precision=exact_precision_flag
+        )
+        red_cond = jnp.concatenate(
+            [
+                small[:PATCH_VALUES],
+                weight_grad(time_freq.astype(bf16), d_first),
+                weight_grad(all_columns(first_s), d_second),
+                g_class,
+            ],
+            0,
+        )
+        red_head = jnp.concatenate([weight_grad(signal_cols, d_fmod_all), small[PATCH_VALUES:].T], 1)
+        side_cols = jnp.stack([total_of(d_first), total_of(d_second)])
+        local_squares = (
+            jnp.sum(red_blocks * red_blocks)
+            + (
+                jnp.sum(red_cond * red_cond)
+                + jnp.sum(red_head * red_head)
+                + jnp.sum(side_cols * side_cols)
+            )
+            / mp
+            + jnp.sum(red_slice * red_slice) / dp
+            + (jnp.sum(side_sum[:-8] * side_sum[:-8]) + jnp.sum(side_mod * side_mod)) / (dp * mp)
+        )
+        last = jnp.pad(side_cols, ((0, 6), (0, LANES - cols)))
+        last = jnp.where(jnp.arange(8)[:, None] == 2, local_squares, last)
+        (last,) = exchange([(last, "gather")], EVERY, 8)
+    grad_norm = jnp.sqrt(jnp.sum(last[:, 2, 0]))
+    loss_sum = side_sum[side_rows, 0]
+    side_sum = side_sum[:side_rows].reshape(-1)[: side_part.shape[0]]
+    red_slice = red_slice.reshape(-1)[: slice_part.shape[0]]
+    side_cols = last[:, :2, :cols].reshape(dp, mp, 2, cols)[:, 0].transpose(1, 0, 2).reshape(2 * width)
+    red_side = jnp.concatenate(
         [
-            (by_columns(back_dense(d_second, cond_low[t2_row:class_row])), "scatter"),
-            (by_columns(small), "scatter"),
-            (bias_part, "gather"),
-        ],
-        "dp",
-        6,
-    )
-    d_first = (jnp.sum(d_first, 0) * swish_slope(first_t)).astype(bf16)
-    g_first = weight_grad(time_freq, d_first)
-    bias_part = jnp.sum(bias_part, 0).reshape(-1)
-    red_slice = bias_part[: slice_part.shape[0]]
-    side_rows = bias_part[slice_part.shape[0] // 128 * 128 :].reshape(-1, 128)
-    small, side_rows = exchange([(jnp.sum(small, 0), "gather"), (side_rows, "gather")], "mp", 7)
-    small, side_sum = jnp.sum(small, 0), jnp.sum(side_rows, 0).reshape(-1)
-    loss_sum = side_sum[side_part.shape[0] - 1]
-    side_sum = side_sum[: side_part.shape[0] - 1]
-    side_mod = total_of(d_fmod_all)
-    red_cond = jnp.concatenate([small[:PATCH_VALUES], g_first, g_second, g_class], 0)
-    red_head = jnp.concatenate([g_fada, small[PATCH_VALUES:].T], 1)
-    side_cols = jnp.stack([total_of(d_first), total_of(d_second)])
-
-    local_squares = (
-        jnp.sum(red_blocks * red_blocks)
-        + (jnp.sum(red_cond * red_cond) + jnp.sum(red_head * red_head) + jnp.sum(side_cols * side_cols)) / mp
-        + jnp.sum(red_slice * red_slice) / dp
-        + (jnp.sum(side_sum * side_sum) + jnp.sum(side_mod * side_mod)) / (dp * mp)
-    )
-    last = jnp.concatenate([side_cols, jnp.broadcast_to(local_squares, (2, 1))], 1)
-    (last,) = exchange([(last, "gather")], EVERY, 8)
-    grad_norm = jnp.sqrt(jnp.sum(last[:, 0, cols]))
-    side_cols = last[:, :, :cols].reshape(dp, mp, 2, cols)[:, 0].transpose(1, 0, 2).reshape(2 * width)
-    red_side = jnp.concatenate(
-        [side_sum[:width], side_cols, side_sum[width : 3 * width], side_mod, side_sum[3 * width :]]
+            side_sum[:width],
+            side_cols,
+            side_sum[width : 3 * width],
+            side_mod.reshape(2 * width),
+            side_sum[3 * width :],
+        ]
     )
     clip_factor = 1.0 / jnp.maximum(grad_norm, 1.0)
     clipped, new_stats, new_blocks, new_low = shampoo(

time: 827 us -> 775 us (0.937)
  Pallas kernels: 632 us -> 587 us
  matrix products: 56.8 us -> 39.3 us
  local copies, waits for them, and re-layouts: 70.5 us -> 85.7 us
    pallas_call x11 -> x3, Pallas kernels: 463 us -> 418 us  [the longest x1 191 us: tail(): pl.pallas_call(tail_body, in_specs=[vmem] * 13, out_specs=[vmem] * len(ou...]
    unnamed x152, local copies, waits for them, and re-layouts: 23.1 us -> 38.3 us
    reduce_sum x16 -> x2, other arithmetic: 14.2 us -> 2.22 us  [the longest x1 1.54 us: per_device(): grad_norm = jnp.sqrt(jnp.sum(last[:, 2, 0]))]
    dot_general x10 -> x6, matrix products: 26.2 us -> 20 us  [weight_grad(): jnp.einsum('...i,...j->ij', operand, gradient, preferred_element_type=jnp...]
where the time goes in v3:
time: 775 us; the launch traced here: 766 us
  Pallas kernels  587 us (76%)
  local copies, waits for them, and re-layouts  85.7 us (11%)
  matrix products  39.3 us (5%)
  other arithmetic  37.4 us (5%)
  blocking collectives  11.4 us (1%)
    pallas_call x1, Pallas kernels, tail(): pl.pallas_call(tail_body, in_specs=[vmem] * 13, out_specs=[vmem] * len(ou...  191 us
    pallas_call x4, Pallas kernels, stage(): pl.pallas_call(body, in_specs=[vmem] * n_in, out_specs=[vmem] * len(out_s...  149 us
    pallas_call x1, Pallas kernels, head(): pl.pallas_call(head_body, in_specs=[vmem] * 10, out_specs=[anywhere] + [v...  139 us
    pallas_call x1, Pallas kernels, shampoo(): pl.pallas_call(shampoo_body, grid=(count // group,), in_specs=[pl.BlockSp...  87.7 us
    unnamed x152, local copies, waits for them, and re-layouts  38.3 us
    dot_general x6, matrix products, weight_grad(): jnp.einsum('...i,...j->ij', operand, gradient, preferred_element_type=jnp...  20 us

profile of v3, /device:TPU:0, one launch (start us, length us, event | category | flops | bytes accessed | tf_op | source)
XLA Modules:
  0.0 766.3 jit_solution(14426219695270704685)
XLA Ops:
  9.2 1.4 slice_reduce_fusion.7
  14.1 1.4 fusion.48
  23.1 2.1 copy.285
  26.1 3.0 copy.288
  29.1 1.8 convert_element_type.197
  31.4 3.1 copy.318
  34.5 3.0 copy.319
  37.5 139.4 %head.1 = (bf16[72,656,128]{2,1,0:T(8,128)(2,1)}, f32[32,256]{1,0:T(8,128)S(1)}, f32[8,4,128]{2,1,0:T(4,128)S(1)}, bf16[8,144,48]{2,1,0:T(8,128)(2,1)S(1)}, f32[...) custom-call(f32[9,288,288]{2,1,0:T(8,128)} %bitcast.191, ...), custom_call_target="tpu_custom_call" | custom-call | tf_op jit(solution)/shard_map/head/pallas_call | solution.py:978
  181.3 2.7 stack.39
  188.3 4.4 copy-done
  193.6 3.9 assemble.5.refs_1_
  197.6 1.5 copy-done.3
  199.1 6.8 assemble.3
  206.0 2.0 copy-done.1
  208.8 5.7 all-gather
  215.2 1.7 reshape.372
  221.2 1.7 fusion.52
  223.5 1.5 dynamic-slice_bitcast_fusion.refs_3_.refs_2_
  225.4 3.0 fusion.13
  232.7 41.7 %stage_9.1 = (f32[256,1152]{1,0:T(8,128)}, f32[256,1152]{1,0:T(8,128)}, f32[4,256,1152]{2,1,0:T(8,128)}, bf16[4,256,1152]{2,1,0:T(8,128)(2,1)}, bf16[4,256,1152]{2,1,0:T(8,128)(2,1)}) custom-call(bf16[4,256,288]{2,1,0:T(8,128)(2,1)} %copy.294.refs_0_, bf16[288,1152]{1,0:T(8,128)(2,1)} %copy-done.5, bf16[1152,1152]{1,0:T(8,128)(2,1)} %copy-done.2, ...), custom_call_target="tpu_custom_call" | custom-call | tf_op jit(solution)/shard_map/stage_9/pallas_call | solution.py:522
  274.4 45.5 %stage_10.1 = (f32[256,1152]{1,0:T(8,128)}, bf16[256,1152]{1,0:T(8,128)(2,1)}, bf16[256,16]{1,0:T(8,128)(2,1)}, bf16[256,16]{1,0:T(8,128)(2,1)}, f32[4,1152]{1,0...) custom-call(bf16[4,256,1152]{2,1,0:T(8,128)(2,1)} %get-tuple-element, ...), custom_call_target="tpu_custom_call" | custom-call | tf_op jit(solution)/shard_map/stage_10/pallas_call | solution.py:522
  321.2 39.0 %stage_11.1 = (f32[256,1152]{1,0:T(8,128)}, f32[4,1152]{1,0:T(4,128)}, bf16[4,256,288]{2,1,0:T(8,128)(2,1)}, bf16[4,256,1152]{2,1,0:T(8,128)(2,1)}) custom-call(bf16[4,256,1152]{2,1,0:T(8,128)(2,1)} %get-tuple-element.76.refs_0_, bf16[1152,1152]{1,0:T(8,128)(2,1)} %copy-done.2, bf16[288,1152]{1,0:T(8,128)(2,1)} %copy-done.5, ...), custom_call_target="tpu_custom_call" | custom-call | tf_op jit(solution)/shard_map/stage_11/pallas_call | solution.py:522
  360.2 4.8 fusion.refs_1_
  369.5 2.9 fusion.5.refs_4_
  372.8 4.8 fusion.1.refs_5_
  377.6 1.7 convert_reduce_fusion
  381.5 3.7 multiply_reduce_fusion.1
  386.4 1.6 fusion.18
  387.9 1.7 convert_reduce_fusion.1
  391.8 1.4 copy.305
  393.2 2.1 pad_maximum_fusion.refs_0_
  395.3 23.0 %stage_12.1 = (bf16[256,1152]{1,0:T(8,128)(2,1)}, f32[3,1152]{1,0:T(4,128)}) custom-call(bf16[4,256,864]{2,1,0:T(8,128)(2,1)} %pad_maximum_fusion.refs_0_, bf16[1152,864]{1,0:T(8,128)(2,1)} %copy-done.9, f32[256,1152]{1,0:T(8,128)} %dynamic-slice_bitcast_fusion.refs_3_.refs_2_, f32[256,1152]{1,0:T(8,128)} %get-tuple-element.81.refs_3_, ...), custom_call_target="tpu_custom_call" | custom-call | tf_op jit(solution)/shard_map/stage_12/pallas_call | solution.py:522
  418.4 6.4 bitcast_convert_fusion
  426.0 2.9 copy.313.refs_0_
  428.9 5.7 all-gather.1
  434.7 3.3 fusion.53
  440.7 1.7 copy-done.7
  442.4 1.7 copy-done.8
  444.2 8.2 %to_slots.1.x_ref = bf16[72,656,128]{2,1,0:T(8,128)(2,1)} custom-call(s32[72]{0:T(128)S(1)} %copy-done.18, bf16[1152,864]{1,0:T(8,128)(2,1)S(1)} %copy.313.refs_0_, bf16[1152,1152]{1,0:T(8,128)(2,1)S(1)} %copy-done.7, bf16[4,4,288]{2,1,0:T(4,128)(2,1)S(1)} %bitcast.180, bf16[4,1728]{1,0:T(4,128)(2,1)S(1)} %get-tuple-element.275.refs_3_, ...), custom_call_target="tpu_custom_call" | custom-call | bytes 23887872 | tf_op jit(solution)/shard_map/to_slots/pallas_call | solution.py:377
  452.5 191.1 %tail.1 = (f32[9,656,128]{2,1,0:T(8,128)}, f32[2425,144]{1,0:T(8,128)}, f32[144,2336]{1,0:T(8,128)}, f32[32,128]{1,0:T(8,128)}, f32[40,128]{1,0:T(8,128)}, /*index=5*/f32[1,2304]{1,0:T(1,128)}, f32[32,8,256]{2,1,0:T(8,128)}) custom-call(bf16[72,656,128]{2,1,0:T(8,128)(2,1)} %to_slots.1.x_ref, f32[1,2304]{1,0:T(1,128)} %bitcast.213, f32[8,4,144]{2,1,0:T(4,128)} %bitcast.208, ...), custom_call_target="tpu_custom_call" | custom-call | tf_op jit(solution)/shard_map/tail/pallas_call | solution.py:1374
  644.8 1.5 slice_reduce_fusion
  653.2 8.1 %fusion.45 = (bf16[2425,144]{1,0:T(8,128)(2,1)}, f32[2425,144]{1,0:T(8,128)}, f32[2425,144]{1,0:T(8,128)}, f32[2425,144]{1,0:T(8,128)}) fusion(f32[2425,144]{1,0:T(8,128)S(1)} %copy-done.23, f32[2425,144]{1,0:T(8,128)} %get-tuple-element.105, f32[]{:T(128)} %div.113, f32[2425,144]{1,0:T(8,128)} %copy.319, f32[2425,144]{1,0:T(8,128)} %copy.318), kind=kLoop, calls=%fused_computation.152 | loop fusion | flops 5587200 | bytes 10476004 | tf_op jit(solution)/shard_map/convert_element_type | solution.py:1904
  661.4 2.2 copy.326
  663.6 2.9 copy.325
  666.5 3.1 copy.324
  669.6 1.9 copy.323
  671.4 5.7 fusion.43
  677.1 87.7 %shampoo.1 = (f32[9,288,288]{2,1,0:T(8,128)}, f32[9,2,288,288]{3,2,1,0:T(8,128)}, f32[9,288,288]{2,1,0:T(8,128)}, bf16[9,288,288]{2,1,0:T(8,128)(2,1)}) custom-call(f32[1]{0:T(128)} %bitcast.56.clip_ref, f32[9,656,128]{2,1,0:T(8,128)} %get-tuple-element.100.g_ref, f32[9,2,288,288]{3,2,1,0:T(8,128)} %bitcast.216, f32[9,288,288]{2,1,0:T(8,128)} %bitcast.192), custom_call_target="tpu_custom_call" | custom-call | flops 56757583872 | bytes 25380864 | tf_op jit(solution)/shard_map/shampoo/pallas_call | solution.py:1520
  (272 shorter events, 62.5 us)
Async XLA Ops:
  22.2 15.2 %copy-start.4 = (bf16[144,2304]{1,0:T(8,128)(2,1)}, bf16[144,2304]{1,0:T(8,128)(2,1)S(1)}, u32[]{:S(2)}) copy-start(bf16[144,2304]{1,0:T(8,128)(2,1)S(1)} %slice.260.fada_ref) | copy-start | bytes 1990660
  31.3 6.2 copy-start.6
  37.5 150.8 %copy-start.18 = (s32[72]{0:T(128)S(1)}, s32[72]{0:T(128)}, u32[]{:S(2)}) copy-start(s32[72]{0:T(128)} %ids.7) | copy-start | bytes 868
  179.3 14.3 %copy-start.10 = (bf16[8,144,48]{2,1,0:T(8,128)(2,1)}, bf16[8,144,48]{2,1,0:T(8,128)(2,1)S(1)}, u32[]{:S(2)}) copy-start(bf16[8,144,48]{2,1,0:T(8,128)(2,1)S(1)} %get-tuple-element.65) | copy-start | bytes 331780
  179.3 14.3 %copy-start.12 = (bf16[8,32,144]{2,1,0:T(8,128)(2,1)}, bf16[8,32,144]{2,1,0:T(8,128)(2,1)S(1)}, u32[]{:S(2)}) copy-start(bf16[8,32,144]{2,1,0:T(8,128)(2,1)S(1)} %get-tuple-element.96.first_s_ref) | copy-start | bytes 221188
  179.3 14.3 %copy-start.13 = (f32[8,4,128]{2,1,0:T(4,128)}, f32[8,4,128]{2,1,0:T(4,128)S(1)}, u32[]{:S(2)}) copy-start(f32[8,4,128]{2,1,0:T(4,128)S(1)} %get-tuple-element.75.facts_ref) | copy-start | bytes 49156
  188.3 4.4 copy-start
  193.6 4.0 copy-start.5
  199.1 8.9 %copy-start.39 = (bf16[4,1152]{1,0:T(4,128)(2,1)S(1)}, bf16[4,1152]{1,0:T(4,128)(2,1)}, u32[]{:S(2)}) copy-start(bf16[4,1152]{1,0:T(4,128)(2,1)} %convert_element_type.203) | copy-start | bytes 27652
  199.1 8.9 %copy-start.40 = (f32[1728]{0:T(1024)S(1)}, f32[1728]{0:T(1024)}, u32[]{:S(2)}) copy-start(f32[1728]{0:T(1024)} %slice_reduce_fusion.2) | copy-start | bytes 20740
  206.0 19.0 %copy-start.9 = (bf16[1152,864]{1,0:T(8,128)(2,1)}, bf16[1152,864]{1,0:T(8,128)(2,1)S(1)}, u32[]{:S(2)}) copy-start(bf16[1152,864]{1,0:T(8,128)(2,1)S(1)} %get-tuple-element.69.refs_1_) | copy-start | bytes 5971972
  208.0 13.2 %copy-start.11 = (bf16[8,144,48]{2,1,0:T(8,128)(2,1)S(1)}, bf16[8,144,48]{2,1,0:T(8,128)(2,1)}, u32[]{:S(2)}) copy-start(bf16[8,144,48]{2,1,0:T(8,128)(2,1)} %copy-done.10) | copy-start | bytes 331780
  208.0 13.2 %copy-start.27 = (f32[16,16,1152]{2,1,0:T(8,128)S(1)}, f32[16,16,1152]{2,1,0:T(8,128)}, u32[]{:S(2)}) copy-start(f32[16,16,1152]{2,1,0:T(8,128)} %pad_maximum_fusion.1) | copy-start | bytes 3538948
  221.2 3.9 copy-start.49
  221.2 3.9 copy-start.51
  231.5 42.9 %copy-start.34 = (bf16[4,4,72,256]{3,2,1,0:T(8,128)(2,1)}, bf16[4,4,72,256]{3,2,1,0:T(8,128)(2,1)S(1)}, u32[]{:S(2)}) copy-start(bf16[4,4,72,256]{3,2,1,0:T(8,128)(2,1)S(1)} %fusion.16) | copy-start | bytes 1769476
  321.1 39.0 %copy-start.28 = (bf16[4,256,1152]{2,1,0:T(8,128)(2,1)S(1)}, bf16[4,256,1152]{2,1,0:T(8,128)(2,1)}, u32[]{:S(2)}) copy-start(bf16[4,256,1152]{2,1,0:T(8,128)(2,1)} %get-tuple-element.76.refs_0_) | copy-start | bytes 7077892
  321.1 39.0 %copy-start.65 = (bf16[4,256,1152]{2,1,0:T(8,128)(2,1)S(1)}, bf16[4,256,1152]{2,1,0:T(8,128)(2,1)}, u32[]{:S(2)}) copy-start(bf16[4,256,1152]{2,1,0:T(8,128)(2,1)} %get-tuple-element.80) | copy-start | bytes 7077892
  360.1 4.8 copy-start.31
  360.2 6.4 copy-start.48
  360.2 6.4 copy-start.37
  360.2 6.5 copy-start.36
  360.2 6.6 copy-start.32
  360.2 7.5 copy-start.60
  360.2 8.1 %copy-start.46 = (f32[4,1152]{1,0:T(4,128)S(1)}, f32[4,1152]{1,0:T(4,128)}, u32[]{:S(2)}) copy-start(f32[4,1152]{1,0:T(4,128)} %get-tuple-element.84) | copy-start | bytes 55300
  369.5 3.3 copy-start.64
  372.8 4.8 copy-start.20
  381.5 3.7 copy-start.21
  395.3 23.0 %copy-start.25 = (bf16[4,256,864]{2,1,0:T(8,128)(2,1)S(1)}, bf16[4,256,864]{2,1,0:T(8,128)(2,1)}, u32[]{:S(2)}) copy-start(bf16[4,256,864]{2,1,0:T(8,128)(2,1)} %pad_maximum_fusion.refs_0_) | copy-start | bytes 5308420
  395.3 23.0 %copy-start.50 = (f32[4,1152]{1,0:T(4,128)S(1)}, f32[4,1152]{1,0:T(4,128)}, u32[]{:S(2)}) copy-start(f32[4,1152]{1,0:T(4,128)} %copy-done.49) | copy-start | bytes 55300
  395.3 23.0 %copy-start.52 = (f32[4,1152]{1,0:T(4,128)S(1)}, f32[4,1152]{1,0:T(4,128)}, u32[]{:S(2)}) copy-start(f32[4,1152]{1,0:T(4,128)} %copy-done.51) | copy-start | bytes 55300
  395.3 23.1 %copy-start.62 = (f32[4,256]{1,0:T(4,128)S(1)}, f32[4,256]{1,0:T(4,128)}, u32[]{:S(2)}) copy-start(f32[4,256]{1,0:T(4,128)} %copy-done.61) | copy-start | bytes 12292
  418.4 6.5 copy-start.33
  418.4 7.4 copy-start.47
  418.4 7.4 copy-start.44
  418.4 7.4 copy-start.63
  428.8 9.2 %copy-start.45 = (f32[1152]{0:T(1024)S(1)}, f32[1152]{0:T(1024)}, u32[]{:S(2)}) copy-start(f32[1152]{0:T(1024)} %reduce.8) | copy-start | bytes 13828
  428.9 9.2 %copy-start.58 = (f32[288]{0:T(512)S(1)}, f32[288]{0:T(512)}, u32[]{:S(2)}) copy-start(f32[288]{0:T(512)} %reduce_sum.133) | copy-start | bytes 3460
  428.9 9.2 %copy-start.59 = (f32[288]{0:T(512)S(1)}, f32[288]{0:T(512)}, u32[]{:S(2)}) copy-start(f32[288]{0:T(512)} %reduce_sum.131) | copy-start | bytes 3460
  428.9 9.3 %copy-start.53 = (f32[8,128]{1,0:T(8,128)S(1)}, f32[8,128]{1,0:T(8,128)}, u32[]{:S(2)}) copy-start(f32[8,128]{1,0:T(8,128)} %pad_bitcast_fusion.1) | copy-start | bytes 12292
  452.4 194.7 %copy-start.43 = (f32[8096]{0:T(1024)S(1)}, f32[8096]{0:T(1024)}, u32[]{:S(2)}) copy-start(f32[8096]{0:T(1024)} %custom-call) | copy-start | bytes 97156
  452.4 197.6 %copy-start.38 = (f32[1,3456]{1,0:T(1,128)S(1)}, f32[1,3456]{1,0:T(1,128)}, u32[]{:S(2)}) copy-start(f32[1,3456]{1,0:T(1,128)} %param.30) | copy-start | bytes 41476
  452.4 197.5 %copy-start.54 = (f32[1,3456]{1,0:T(1,128)S(1)}, f32[1,3456]{1,0:T(1,128)}, u32[]{:S(2)}) copy-start(f32[1,3456]{1,0:T(1,128)} %param.37) | copy-start | bytes 41476
  452.4 197.5 %copy-start.55 = (f32[1,3456]{1,0:T(1,128)S(1)}, f32[1,3456]{1,0:T(1,128)}, u32[]{:S(2)}) copy-start(f32[1,3456]{1,0:T(1,128)} %param.36) | copy-start | bytes 41476
  452.4 200.1 %copy-start.35 = (f32[8096]{0:T(1024)S(1)}, f32[8096]{0:T(1024)}, u32[]{:S(2)}) copy-start(f32[8096]{0:T(1024)} %param.31) | copy-start | bytes 97156
  452.5 200.1 %copy-start.41 = (f32[8096]{0:T(1024)S(1)}, f32[8096]{0:T(1024)}, u32[]{:S(2)}) copy-start(f32[8096]{0:T(1024)} %param.39) | copy-start | bytes 97156
  452.5 200.1 %copy-start.42 = (f32[8096]{0:T(1024)S(1)}, f32[8096]{0:T(1024)}, u32[]{:S(2)}) copy-start(f32[8096]{0:T(1024)} %param.38) | copy-start | bytes 97156
  452.5 200.7 %copy-start.23 = (f32[2425,144]{1,0:T(8,128)S(1)}, f32[2425,144]{1,0:T(8,128)}, u32[]{:S(2)}) copy-start(f32[2425,144]{1,0:T(8,128)} %copy.288) | copy-start | bytes 4190404
  (18 other events, 35.3 us)

commit v4 on v3

--- a/solution.py
+++ b/solution.py
@@ -128,6 +128,7 @@
 
 
 PACK_ROWS = 656
+SPLIT = 1
 
 
 def pack(x):
@@ -154,6 +155,19 @@
     ref[index + (slice(0, side),)] = a
     ref[index + (slice(side, 2 * side),)] = b
     ref[index + (slice(2 * side, PACK_ROWS),)] = c
+
+
+def store_pieces(ref, first, x):
+    rows = [part for part in pack(x)]
+    size, at, piece = PACK_ROWS // SPLIT, 0, 0
+    for part in rows:
+        done = 0
+        while done < part.shape[0]:
+            step = min(size - at, part.shape[0] - done)
+            ref[first + piece, at : at + step] = part[done : done + step]
+            done, at = done + step, at + step
+            if at == size:
+                piece, at = piece + 1, 0
 
 
 def pack_blocks(blocks):
@@ -722,6 +736,7 @@
     )
 
 
+AHEAD = 4
 CROSS_LATE = 1
 
 
@@ -756,15 +771,23 @@
         lax.fori_loop(1, self.n, one, 0)
 
 
+def in_parts(first, last, step, between):
+    for at, work in between:
+        lax.fori_loop(first, at, step, 0)
+        work()
+        first = at
+    lax.fori_loop(first, last, step, 0)
+
+
 def head_body(
-    x_ref, tf_ref, facts_ref, shared_ref, w1_ref, w2_ref, class_ref, fada_ref, b1_ref, b2_ref,
-    out_ref, tf_all, facts_all, shared_all, first_t_ref, first_s_all, cond_ref, signal_ref,
+    x_ref, tf_ref, facts_ref, shared_ref, tables_ref, fada_ref, b1_ref, b2_ref,
+    out_ref, tf_all, facts_all, shared_all, first_t_ref, first_s_ref, cond_ref, signal_ref,
     signal_all, mod_ref,
-    packed, tf_land, first_s, signal_own, mod_own, mod_land, local_sem, up_sem, down_sem, side_sem,
+    packed, tf_land, hot_buf, first_s, first_s_all, signal_own, mod_own, mod_land, local_sem, up_sem, down_sem, side_sem,
     up_other, down_other, recv_sem, send, receive,
 ):
-    count, ways, f32, bf16 = x_ref.shape[0], LAYERS * COLUMNS, jnp.float32, jnp.bfloat16
-    batch, cols = tf_ref.shape[0], shared_ref.shape[0]
+    count, ways, f32, bf16 = packed.shape[0], LAYERS * COLUMNS, jnp.float32, jnp.bfloat16
+    batch, cols = mod_ref.shape[0], tables_ref.shape[0]
     late = count - CROSS_LATE
     z, y = grid_place()
     me = lax.axis_index("dp")
@@ -811,35 +834,25 @@
         return remote(here, here, side_sem.at[0, 0], recv_sem.at[layer, column, k], peer)
 
     def send_own(i, _):
-        k = count - 1 - i
-        store_packed(packed, (k,), x_ref[k].astype(bf16))
-        own = packed.at[k]
-        move(own, z, k, side_sem, peer).start()
-
-        @pl.when(z < LAYERS - 1)
-        def _():
-            move(own, z, k, up_sem, above).start()
-
-        @pl.when(z > 0)
-        def _():
-            move(own, z, k, down_sem, below).start()
-
-        pltpu.make_async_copy(own, block(z, y, k), local_sem.at[k]).start()
+        base = count - SPLIT * (i + 1)
+        store_pieces(packed, base, x_ref[x_ref.shape[0] - 1 - i].astype(bf16))
+        for j in range(SPLIT - 1, -1, -1):
+            k = base + j
+            own = packed.at[k]
+            move(own, z, k, side_sem, peer).start()
+
+            @pl.when(z < LAYERS - 1)
+            def _():
+                move(own, z, k, up_sem, above).start()
+
+            @pl.when(z > 0)
+            def _():
+                move(own, z, k, down_sem, below).start()
+
+            pltpu.make_async_copy(own, block(z, y, k), local_sem.at[k]).start()
         return 0
 
-    lax.fori_loop(0, count, send_own, 0)
-
-    for p in first:
-        p.wait()
-    for i in range(ways):
-        tf_all[i * batch : (i + 1) * batch] = tf_land[i]
-    first_t = times(tf_all[...].astype(bf16), w1_ref[...]) + b1_ref[...]
-    first_t_ref[...] = first_t
-    first_s[...] = swish_unit(first_t).astype(bf16)
-    second = push(3, first_s, first_s_all)
-    second.start()
-
-    for k in range(late, count):
+    def pass_own(k):
         arrival(z, 1 - y, k).wait_recv()
 
         @pl.when(z < LAYERS - 1)
@@ -903,33 +916,66 @@
                 def _():
                     move_other(layer, k, down_other, below).start()
 
-    run_hop(1)
-    second.wait()
-    cond = b2_ref[...]
-    for i in range(ways):
-        cond = cond + times(first_s_all[i], w2_ref[i * cols : (i + 1) * cols])
-        row = lax.broadcasted_iota(jnp.int32, (batch, class_ref.shape[0]), 1)
-        hot = (row == facts_all[i][:, 0:1].astype(jnp.int32)).astype(bf16)
-        cond_ref[i * batch : (i + 1) * batch] = times(hot, class_ref[...])
-    cond = cond + cond_ref[...]
-    cond_ref[...] = cond
-    signal = swish_unit(cond).astype(bf16)
-    signal_ref[...] = signal
-    mod = times(signal, fada_ref[...])
-    signal = signal.astype(f32)
-    for i in range(ways):
-        signal_own[i] = signal[i * batch : (i + 1) * batch]
-        mod_own[i] = mod[i * batch : (i + 1) * batch]
+    t2_row = PATCH_VALUES + FREQ
+    class_row = t2_row + MODEL_WIDTH
+    second = push(3, first_s, first_s_all)
     third = [
         push(4, signal_own, signal_all, lambda to: to),
         push(5, mod_own, mod_land, lambda to: to),
     ]
-    for p in third:
-        p.start()
+
+    def first_row():
+        for p in first:
+            p.wait()
+        for i in range(ways):
+            tf_all[i * batch : (i + 1) * batch] = tf_land[i][:batch]
+        first_t = times_flipped(tf_all[...].astype(bf16), tables_ref[:, PATCH_VALUES:t2_row]) + b1_ref[...]
+        first_t_ref[...] = first_t
+        first_s[:, :cols] = swish_unit(first_t).astype(bf16)
+        second.start()
+
+    def class_part():
+        for i in range(ways):
+            row = lax.broadcasted_iota(jnp.int32, (batch, CLASSES), 1)
+            hot = (row == facts_all[i][:batch, 0:1].astype(jnp.int32)).astype(f32)
+            hot_buf[i * batch : (i + 1) * batch] = hot
+        cond_ref[...] = (
+            times_flipped(hot_buf[...].astype(bf16), tables_ref[:, class_row:]) + b2_ref[...]
+        )
+
+    def second_row():
+        second.wait()
+        first_s_ref[...] = jnp.concatenate([first_s_all[i][:, :cols] for i in range(ways)], axis=1)
+        cond = cond_ref[...] + times_flipped(first_s_ref[...], tables_ref[:, t2_row:class_row])
+        cond_ref[...] = cond
+        signal = swish_unit(cond).astype(bf16)
+        signal_ref[...] = signal
+        signal = signal.astype(f32)
+        for i in range(ways):
+            signal_own[i, :batch, :cols] = signal[i * batch : (i + 1) * batch]
+        third[0].start()
+
+    def modulation():
+        mod = times(signal_ref[...], fada_ref[...])
+        half = mod.shape[1] // 2
+        for i in range(ways):
+            mod_own[i, :batch] = mod[i * batch : (i + 1) * batch, :half]
+            mod_own[i, batch:] = mod[i * batch : (i + 1) * batch, half:]
+        third[1].start()
+
+    own_count = x_ref.shape[0]
+    third_of = -(-own_count // 3)
+    in_parts(0, own_count, send_own, [(third_of, first_row), (2 * third_of, class_part)])
+    second_row()
+    modulation()
+    for k in range(late, count):
+        pass_own(k)
+    run_hop(1)
     run_hop(2)
     for p in third:
         p.wait()
-    mod_ref[...] = jnp.sum(mod_land[...], axis=0)
+    mod = jnp.sum(mod_land[...], axis=0)
+    mod_ref[...] = jnp.concatenate([mod[:batch], mod[batch:]], axis=1)
     run_hop(3)
 
     def finish(k, _):
@@ -967,37 +1013,43 @@
                 move_other(layer, k, down_other, below).wait_send()
 
 
-def head(blocks, time_freq, facts, shared, w1, w2, w_class, w_fada, b1, b2):
+def head(blocks, time_freq, facts, shared, tables, w_fada, b1, b2):
     ways, f32, bf16 = LAYERS * COLUMNS, jnp.float32, jnp.bfloat16
-    count, side = blocks.shape[0], BLOCK_SIDE
-    batch, cols, rows = time_freq.shape[0], shared.shape[0], time_freq.shape[0] * ways
+    count = blocks.shape[0] * SPLIT
+    batch, cols, rows = time_freq.shape[0], tables.shape[0], time_freq.shape[0] * ways
     fada = w_fada.shape[1]
+    piece = (PACK_ROWS // SPLIT, LANES // 2)
+    time_freq = jnp.pad(time_freq, ((0, 8 - batch), (0, 0)))
+    facts = jnp.pad(facts, ((0, 8 - batch), (0, 0)))
+    shared = jnp.pad(shared.T, ((0, 0), (0, LANES - cols)))
     dma = pltpu.SemaphoreType.DMA
     vmem, anywhere = pl.BlockSpec(memory_space=pltpu.VMEM), pl.BlockSpec(memory_space=pl.ANY)
     shape = jax.ShapeDtypeStruct
-    return pl.pallas_call(
+    out = pl.pallas_call(
         head_body,
-        in_specs=[vmem] * 10,
+        in_specs=[vmem] * 8,
         out_specs=[anywhere] + [vmem] * 9,
         out_shape=[
-            shape((count * ways, PACK_ROWS, LANES // 2), bf16),
+            shape((count * ways,) + piece, bf16),
             shape((rows, time_freq.shape[1]), f32),
             shape((ways,) + facts.shape, f32),
             shape((ways,) + shared.shape, bf16),
             shape((rows, cols), f32),
-            shape((ways, rows, cols), bf16),
+            shape((rows, ways * cols), bf16),
             shape((rows, cols), f32),
             shape((rows, cols), bf16),
-            shape((ways, batch, cols), f32),
+            shape((ways, 8, LANES), f32),
             shape((batch, fada), f32),
         ],
         scratch_shapes=[
-            pltpu.VMEM((count, PACK_ROWS, LANES // 2), bf16),
+            pltpu.VMEM((count,) + piece, bf16),
             pltpu.VMEM((ways,) + time_freq.shape, f32),
-            pltpu.VMEM((rows, cols), bf16),
-            pltpu.VMEM((ways, batch, cols), f32),
-            pltpu.VMEM((ways, batch, fada), f32),
-            pltpu.VMEM((ways, batch, fada), f32),
+            pltpu.VMEM((rows, CLASSES), f32),
+            pltpu.VMEM((rows, LANES), bf16),
+            pltpu.VMEM((ways, rows, LANES), bf16),
+            pltpu.VMEM((ways, 8, LANES), f32),
+            pltpu.VMEM((ways, 2 * batch, fada // 2), f32),
+            pltpu.VMEM((ways, 2 * batch, fada // 2), f32),
             dma((count,)),
             dma((LAYERS, count)),
             dma((LAYERS, count)),
@@ -1012,7 +1064,13 @@
             collective_id=0, has_side_effects=True, vmem_limit_bytes=48 * 2**20
         ),
         name="head",
-    )(blocks, time_freq, facts, shared, w1, w2, w_class, w_fada, b1, b2)
+    )(blocks, time_freq, facts, shared, tables, w_fada, b1, b2)
+    blocks, time_freq, facts, shared, first_t, first_s, cond, signal, signal_all, mod = out
+    blocks = blocks.reshape(-1, PACK_ROWS, LANES // 2)
+    return (
+        blocks, time_freq, facts[:, :batch], shared[:, :, :cols].transpose(0, 2, 1), first_t, first_s, cond, signal,
+        signal_all[:, :batch, :cols], mod,
+    )
 
 
 def outer(a, b):
@@ -1020,18 +1078,18 @@
 
 
 def tail_body(
-    x_ref, fmod_ref, dsig_ref, small_ref, bias_ref, fada_ref, w2_ref, cond_ref, first_t_ref,
+    x_ref, early_ref, small_ref, bias_ref, fada_ref, tables_ref, cond_ref, first_t_ref,
     signal_ref, first_s_ref, tf_ref, facts_ref,
-    out_ref, g_cond_ref, g_head_ref, slice_ref, side_ref, mod_sum_ref, last_all,
-    side_buf, up_buf, down_buf, other_buf, up_other, down_other, fmod_land, dsig_land, small_land,
-    bias_land, dsig_all, first_own, first_land, small_own, small_mp, side_own, side_mp, fmod_all, last_own,
-    hot_buf,
+    out_ref, g_cond_ref, g_head_ref, slice_ref, side_ref, mod_sum_ref, columns_all, last_all,
+    side_buf, up_buf, down_buf, other_buf, up_other, down_other, early_land, small_land,
+    bias_land, dsig_all, first_own, first_land, small_own, small_mp, side_own, side_mp, fmod_all, columns_own,
+    last_own, hot_buf,
     side_send, line_send, side_recv, up_recv, down_recv, other_send, other_up, other_down,
     send_all, recv_all, send_dp, recv_dp, send_mp, recv_mp,
 ):
     f32, bf16 = jnp.float32, jnp.bfloat16
     count, ways, mp = out_ref.shape[0], LAYERS * COLUMNS, lax.axis_size("mp")
-    batch, cols = dsig_ref.shape[1], dsig_ref.shape[2]
+    batch, cols = facts_ref.shape[1], tables_ref.shape[0]
     everyone = ways * mp
     late = count - CROSS_LATE
     z, y = grid_place()
@@ -1061,13 +1119,11 @@
     def push_mp(j, source, landing):
         return Push(source, landing, send_mp.at[j], recv_mp.at[j], mp, my_mp, lambda i: {"mp": i})
 
-    first = [
-        push_all(0, fmod_ref, fmod_land),
-        push_all(1, dsig_ref, dsig_land, lambda to: to // mp),
-    ]
+    first = [push_all(0, early_ref, early_land, lambda to: to // mp)]
     second = [push_dp(0, small_ref, small_land, lambda to: to), push_dp(1, bias_ref, bias_land)]
-    for p in first + second:
-        p.start()
+    third = push_dp(2, first_own, first_land, lambda to: to)
+    fifth = push_dp(3, columns_own, columns_all)
+    fourth = [push_mp(0, small_own, small_mp), push_mp(1, side_own, side_mp)]
 
     peer = {"dp": z * COLUMNS + 1 - y}
     above = {"dp": jnp.minimum(z + 1, LAYERS - 1) * COLUMNS + y}
@@ -1123,22 +1179,26 @@
         across(layer, k).wait_recv()
         return own_part(layer, k) + side_buf[layer, k].astype(f32)
 
-    for hop in range(LAYERS - 1, -1, -1):
-
-        def begin(k, _):
-            @pl.when(z + hop < LAYERS)
-            def _():
-                across(z + hop, k).start()
-
-            if hop > 0:
-
-                @pl.when(z >= hop)
-                def _():
-                    across(z - hop, k).start()
-
-            return 0
-
-        lax.fori_loop(0, late, begin, 0)
+    at_end = (z == 0) | (z == LAYERS - 1)
+
+    def turn(t):
+        part, within = t // late, lax.rem(t, late)
+        end_layer = jnp.where(z == 0, LAYERS - 1 - part, part)
+        pair = t - late
+        near = jnp.where(lax.rem(pair, 2) == 0, z + 1, z - 1)
+        inner_layer = jnp.where(part == 0, jnp.where(z == 1, LAYERS - 1, 0), jnp.where(part == 3, z, near))
+        inner_k = jnp.where((part == 0) | (part == 3), within, pair // 2)
+        return jnp.where(at_end, end_layer, inner_layer), jnp.where(at_end, within, inner_k)
+
+    def issue(t):
+        @pl.when(t < LAYERS * late)
+        def _():
+            across(*turn(t)).start()
+
+    for t in range(AHEAD):
+        issue(jnp.int32(t))
+    for p in first + second:
+        p.start()
 
     def along(total, stage_ref, layer, k, copy, landed, begins):
         @pl.when(jnp.logical_not(begins))
@@ -1154,7 +1214,7 @@
 
     bottom, top = z == 0, z == LAYERS - 1
 
-    def run_hop(hop):
+    def run_late(hop):
         for k in range(late, count):
             j = k - late
 
@@ -1180,101 +1240,134 @@
                     other_buf.at[layer, j], layer, k, downward_other, down_other.at[layer, j], top,
                 )
 
-        def step(k, _):
-            @pl.when(z + hop < LAYERS)
-            def _():
-                layer = z + hop
-                along(
-                    pair_sum(layer, k), side_buf.at[layer, k], layer, k, upward, up_buf.at[layer, k], bottom
-                )
-
-            @pl.when(z >= hop)
-            def _():
-                layer = z - hop
-                along(
-                    pair_sum(layer, k), side_buf.at[layer, k], layer, k, downward, down_buf.at[layer, k], top
-                )
-
-            return 0
-
-        lax.fori_loop(0, late, step, 0)
-
-    run_hop(3)
-
-    for p in first:
-        p.wait()
-    for i in range(everyone):
-        fmod_all[i : i + 1] = fmod_land[i]
-    for i in range(ways):
-        dsig_all[i * batch : (i + 1) * batch] = jnp.sum(dsig_land[i * mp : (i + 1) * mp], axis=0)
-    d_fmod = fmod_all[...].astype(bf16)
-    d_signal = dsig_all[...] + times_flipped(d_fmod, fada_ref[...])
-    d_cond = d_signal * swish_slope(cond_ref[...])
-    d_second = d_cond.astype(bf16)
-    back = times_flipped(d_second, w2_ref[...])
-    for i in range(ways):
-        first_own[i] = back[:, i * cols : (i + 1) * cols]
-    for p in second:
-        p.wait()
-    third = push_dp(2, first_own, first_land, lambda to: to)
+    def step(t, _):
+        issue(t + AHEAD)
+        layer, k = turn(t)
+
+        @pl.when(layer > z)
+        def _():
+            along(
+                pair_sum(layer, k), side_buf.at[layer, k], layer, k, upward, up_buf.at[layer, k], bottom
+            )
+
+        @pl.when(layer < z)
+        def _():
+            along(
+                pair_sum(layer, k), side_buf.at[layer, k], layer, k, downward, down_buf.at[layer, k], top
+            )
+
+        return 0
+
+    t2_row = PATCH_VALUES + FREQ
+    class_row = t2_row + MODEL_WIDTH
+    held = {"shared": jnp.zeros((1, 1), f32)}
 
     def square(x):
         return jnp.sum(jnp.sum(x * x, axis=1, keepdims=True), axis=0, keepdims=True)
 
-    third.start()
-    shared_squares = jnp.zeros((1, 1), f32)
-    g_fada = outer(signal_ref[...], d_fmod)
-    g_head_ref[:, : g_fada.shape[1]] = g_fada
-    shared_squares += square(g_fada)
-    mod_sum = column_sum(fmod_all[...])
-    mod_sum_ref[...] = mod_sum
-    t2_row = PATCH_VALUES + FREQ
-    class_row = t2_row + MODEL_WIDTH
-    for i in range(ways):
-        g = outer(first_s_ref[i], d_second)
-        g_cond_ref[t2_row + i * cols : t2_row + (i + 1) * cols] = g
-        shared_squares += square(g)
-    for i in range(ways):
-        row = lax.broadcasted_iota(jnp.int32, (batch, hot_buf.shape[1]), 1)
-        hot = (row == facts_ref[i][:, 0:1].astype(jnp.int32)).astype(f32)
-        hot_buf[i * batch : (i + 1) * batch] = hot
-    hot = hot_buf[...].astype(bf16)
-    high = d_cond.astype(bf16)
-    rest = d_cond - high.astype(f32)
-    mid = rest.astype(bf16)
-    low = (rest - mid.astype(f32)).astype(bf16)
-    g_class = outer(hot, high) + outer(hot, mid) + outer(hot, low)
-    g_cond_ref[class_row:] = g_class[:CLASSES]
-    shared_squares += square(g_class)
-    run_hop(2)
-    third.wait()
-    d_first = (jnp.sum(first_land[...], axis=0) * swish_slope(first_t_ref[...])).astype(bf16)
-    g_first = outer(tf_ref[...].astype(bf16), d_first)
-    g_cond_ref[PATCH_VALUES:t2_row] = g_first
-    shared_squares += square(g_first)
-    small_own[...] = jnp.sum(small_land[...], axis=0)
-    bias = jnp.sum(bias_land[...], axis=0)
-    slice_rows = slice_ref.shape[0]
-    slice_ref[...] = bias[:slice_rows]
-    slice_squares = square(bias[:slice_rows])
-    side_own[...] = bias[slice_rows:]
-    fourth = [push_mp(0, small_own, small_mp), push_mp(1, side_own, side_mp)]
-    for p in fourth:
-        p.start()
-    run_hop(1)
-    for p in fourth:
-        p.wait()
-    small = jnp.sum(small_mp[...], axis=0)
-    g_cond_ref[:PATCH_VALUES] = small[:PATCH_VALUES]
-    g_head_ref[:, g_head_ref.shape[1] - (small.shape[0] - PATCH_VALUES) :] = small[PATCH_VALUES:].T
-    shared_squares += square(small)
-    side = jnp.sum(side_mp[...], axis=0)
-    side_ref[...] = side
-    every_squares = square(side[: side.shape[0] - 8]) + square(mod_sum)
-    column_sums = [column_sum(d_first.astype(f32)), column_sum(d_second.astype(f32))]
-    for s in column_sums:
-        shared_squares += square(s)
-    squares = shared_squares / mp + slice_squares / ways + every_squares / (ways * mp)
+    def add_shared(x):
+        held["shared"] = held["shared"] + square(x)
+
+    def signal_back():
+        for p in first:
+            p.wait()
+        lines = fmod_all.shape[1] // 128
+        for i in range(everyone):
+            here = early_land[i].astype(f32)
+            for j in range(lines):
+                fmod_all[i : i + 1, j * 128 : (j + 1) * 128] = here[j : j + 1]
+        for i in range(ways):
+            here = early_land[i * mp].astype(f32)[24:]
+            for j in range(1, mp):
+                here = here + early_land[i * mp + j].astype(f32)[24:]
+            dsig_all[i * batch : (i + 1) * batch, :128] = here[:batch]
+            dsig_all[i * batch : (i + 1) * batch, 128:] = here[batch:]
+        d_signal = dsig_all[:, :cols] + times_flipped(fmod_all[...].astype(bf16), fada_ref[...])
+        held["d_cond"] = d_signal * swish_slope(cond_ref[...])
+        held["d_second"] = held["d_cond"].astype(bf16)
+
+    def second_back():
+        back = times(held["d_second"], tables_ref[:, t2_row:class_row])
+        for i in range(ways):
+            first_own[i, :, :cols] = back[:, i * cols : (i + 1) * cols].astype(bf16)
+        third.start()
+
+    def bias_sums():
+        for p in second:
+            p.wait()
+        small_own[...] = jnp.sum(small_land[...].astype(f32), axis=0)
+        bias = jnp.sum(bias_land[...].astype(f32), axis=0)
+        slice_rows = slice_ref.shape[0]
+        slice_ref[...] = bias[:slice_rows]
+        held["slice"] = square(bias[:slice_rows])
+        side_own[...] = bias[slice_rows:]
+        for p in fourth:
+            p.start()
+
+    def fada_gradient():
+        g_fada = outer(signal_ref[...], fmod_all[...].astype(bf16))
+        g_head_ref[:, : g_fada.shape[1]] = g_fada
+        add_shared(g_fada)
+        held["mod"] = column_sum(fmod_all[...])
+        mod_sum_ref[...] = held["mod"]
+
+    def second_gradient():
+        held["g_second"] = outer(held["d_second"], first_s_ref[...])
+        add_shared(held["g_second"])
+
+    def class_gradient():
+        for i in range(ways):
+            row = lax.broadcasted_iota(jnp.int32, (batch, CLASSES), 1)
+            hot = (row == facts_ref[i][:, 0:1].astype(jnp.int32)).astype(f32)
+            hot_buf[i * batch : (i + 1) * batch] = hot
+        hot = hot_buf[...].astype(bf16)
+        high = held["d_cond"].astype(bf16)
+        rest = held["d_cond"] - high.astype(f32)
+        mid = rest.astype(bf16)
+        low = (rest - mid.astype(f32)).astype(bf16)
+        held["g_class"] = outer(high, hot) + outer(mid, hot) + outer(low, hot)
+        add_shared(held["g_class"])
+
+    def first_gradient():
+        third.wait()
+        d_first = (jnp.sum(first_land[...].astype(f32), axis=0)[:, :cols] * swish_slope(first_t_ref[...])).astype(bf16)
+        held["g_first"] = outer(d_first, tf_ref[...].astype(bf16))
+        add_shared(held["g_first"])
+        held["columns"] = [column_sum(d_first.astype(f32)), column_sum(held["d_second"].astype(f32))]
+        for i, s in enumerate(held["columns"]):
+            add_shared(s)
+            columns_own[i : i + 1, :cols] = s
+        fifth.start()
+
+    def totals():
+        for p in fourth:
+            p.wait()
+        small = jnp.sum(small_mp[...], axis=0)[:, :cols]
+        add_shared(small)
+        small = small.T
+        g_head_ref[:, fmod_all.shape[1] :] = small[:, PATCH_VALUES:]
+        g_cond_ref[...] = jnp.concatenate(
+            [small[:, :PATCH_VALUES], held["g_first"], held["g_second"], held["g_class"]], axis=1
+        )
+        side = jnp.sum(side_mp[...], axis=0)
+        side_ref[...] = side
+        held["every"] = square(side[: side.shape[0] - 8]) + square(held["mod"])
+
+    steps = (LAYERS - 1) * late
+    places = [
+        (0, lambda: run_late(3)),
+        (3, lambda: run_late(2)),
+        (12, lambda: run_late(1)),
+        (22, signal_back),
+        (25, second_back),
+        (30, bias_sums),
+        (35, fada_gradient),
+        (40, second_gradient),
+        (45, class_gradient),
+        (57, first_gradient),
+        (63, totals),
+    ]
+    in_parts(0, steps, step, [(-(-t * steps // 72), work) for t, work in places])
 
     for k in range(late, count):
         j = k - late
@@ -1295,6 +1388,7 @@
     last_own[...] = jnp.zeros_like(last_own)
 
     def final(k, _):
+        issue(steps + k + AHEAD)
         out_ref[k] = pair_sum(z, k)
 
         @pl.when(z > 0)
@@ -1308,16 +1402,15 @@
             out_ref[k] += down_buf[z, k].astype(f32)
 
         total = out_ref[k]
-        last_own[2:3, :128] += column_sum(total * total)
+        last_own[...] += column_sum(total * total)
         return 0
 
     lax.fori_loop(0, count, final, 0)
-    squares += jnp.sum(last_own[2:3, :128], axis=1, keepdims=True)
-    last_own[0:1, :cols] = column_sums[0]
-    last_own[1:2, :cols] = column_sums[1]
-    last_own[2:3, :128] = jnp.broadcast_to(squares, (1, 128))
-    fifth = push_all(2, last_own, last_all)
-    fifth.start()
+    squares = held["shared"] / mp + held["slice"] / ways + held["every"] / (ways * mp)
+    squares += jnp.sum(last_own[...], axis=1, keepdims=True)
+    last_own[...] = jnp.broadcast_to(squares, (1, 128))
+    sixth = push_all(1, last_own, last_all)
+    sixth.start()
 
     def sent(k, _):
         for layer in range(LAYERS):
@@ -1350,60 +1443,73 @@
                 downward_other(layer, k).wait_send()
 
     fifth.wait()
-
-
-def tail(slots, d_fmod, d_signal, small, bias, w_fada, w2, cond, first_t, signal, first_s, tf, facts, slice_rows):
+    sixth.wait()
+
+
+def tail(slots, d_fmod, d_signal, small, bias, w_fada, tables, cond, first_t, signal, first_s, tf, facts, slice_rows):
     ways, mp, f32, bf16 = LAYERS * COLUMNS, lax.axis_size("mp"), jnp.float32, jnp.bfloat16
-    count, packed = slots.shape[0] // ways, slots.shape[1:]
+    piece = (PACK_ROWS // SPLIT, LANES // 2)
+    slots = slots.reshape((-1,) + piece)
+    count = slots.shape[0] // ways
     batch, cols = d_signal.shape[1:]
     rows, fada = batch * ways, w_fada.shape[1]
     side_rows = bias.shape[0] - slice_rows
+    wide = ((0, 0), (0, 0), (0, LANES - cols))
+    d_signal = jnp.pad(d_signal, wide).reshape(ways, batch, 2, 128).transpose(0, 2, 1, 3)
+    d_fmod = jnp.pad(d_fmod.reshape(fada // 128, 128), ((0, 24 - fada // 128), (0, 0)))
+    early = jnp.concatenate(
+        [jnp.broadcast_to(d_fmod, (ways, 24, 128)), d_signal.reshape(ways, 2 * batch, 128)], 1
+    ).astype(bf16)
+    small = jnp.pad(small, wide).astype(bf16)
+    bias = bias.astype(bf16)
     dma, vmem = pltpu.SemaphoreType.DMA, pl.BlockSpec(memory_space=pltpu.VMEM)
     shape, scratch = jax.ShapeDtypeStruct, pltpu.VMEM
-    landing = scratch((LAYERS, count) + packed, bf16)
-    few = scratch((LAYERS, CROSS_LATE) + packed, bf16)
+    landing = scratch((LAYERS, count) + piece, bf16)
+    few = scratch((LAYERS, CROSS_LATE) + piece, bf16)
     out_shape = [
-        shape((count,) + packed, f32),
-        shape((PATCH_VALUES + FREQ + MODEL_WIDTH + CLASSES, cols), f32),
+        shape((count,) + piece, f32),
+        shape(tables.shape, f32),
         shape((cols, fada + small.shape[1] - PATCH_VALUES), f32),
         shape((slice_rows, 128), f32),
         shape((side_rows, 128), f32),
         shape((1, fada), f32),
-        shape((ways * mp, 8, LANES), f32),
+        shape((ways, 8, LANES), f32),
+        shape((ways * mp, 1, 128), f32),
     ]
-    return pl.pallas_call(
+    out = pl.pallas_call(
         tail_body,
-        in_specs=[vmem] * 13,
+        in_specs=[vmem] * 12,
         out_specs=[vmem] * len(out_shape),
         out_shape=out_shape,
         scratch_shapes=[landing] * 3
         + [few] * 3
         + [
-            scratch((ways * mp, 1, fada), f32),
-            scratch((ways * mp, batch, cols), f32),
-            scratch(small.shape, f32),
-            scratch((ways,) + bias.shape, f32),
-            scratch((rows, cols), f32),
-            scratch((ways, rows, cols), f32),
-            scratch((ways, rows, cols), f32),
+            scratch((ways * mp,) + early.shape[1:], bf16),
+            scratch(small.shape, bf16),
+            scratch((ways,) + bias.shape, bf16),
+            scratch((rows, LANES), f32),
+            scratch((ways, rows, LANES), bf16),
+            scratch((ways, rows, LANES), bf16),
             scratch(small.shape[1:], f32),
             scratch((mp,) + small.shape[1:], f32),
             scratch((side_rows, 128), f32),
             scratch((mp, side_rows, 128), f32),
             scratch((rows, fada), f32),
             scratch((8, LANES), f32),
-            scratch((rows, 1024), f32),
+            scratch((1, 128), f32),
+            scratch((rows, CLASSES), f32),
         ]
         + [dma((LAYERS, count))] * 5
         + [dma((LAYERS, CROSS_LATE))] * 3
-        + [dma((3, ways * mp))] * 2
-        + [dma((3, ways))] * 2
+        + [dma((2, ways * mp))] * 2
+        + [dma((4, ways))] * 2
         + [dma((2, mp))] * 2,
         compiler_params=pltpu.CompilerParams(
             collective_id=1, has_side_effects=True, vmem_limit_bytes=58 * 2**20
         ),
         name="tail",
-    )(slots, d_fmod, d_signal, small, bias, w_fada, w2, cond, first_t, signal, first_s, tf, facts)
+    )(slots, early, small, bias, w_fada, tables, cond, first_t, signal, first_s, tf, facts)
+    return [out[0].reshape(-1, PACK_ROWS, LANES // 2)] + list(out[1:])
 
 
 def halves(x):
@@ -1608,23 +1714,22 @@
         return lax.all_gather(x, "mp", axis=0, tiled=True)
 
     tuned = dp == COLUMNS * LAYERS
-    cond_low, head_low = cond_tables.astype(bf16), head_tables.astype(bf16)
-    w_first, w_second = cond_low[PATCH_VALUES:t2_row], cond_low[t2_row:class_row]
-    w_class = jnp.pad(cond_low[class_row:], ((0, 1024 - CLASSES), (0, 0)))
+    tables, head_low = cond_tables.T.astype(bf16), head_tables.astype(bf16)
     w_fada = head_low[:, : 2 * width]
     b_first = my_cols(side_bias[width : 2 * width])
     b_second = my_cols(side_bias[2 * width : 3 * width])
     time_freq = time_features(timesteps, FREQ).astype(bf16).astype(f32)
     facts = jnp.pad(jnp.stack([labels.astype(f32), loss_weights], 1), ((0, 0), (0, 126)))
-    shared = jnp.concatenate([cond_low[:PATCH_VALUES].T, head_low[:, 2 * width :]], 1)
+    shared = jnp.concatenate([tables[:, :PATCH_VALUES], head_low[:, 2 * width :]], 1)
     if tuned:
         (
             blocks, time_freq, facts, shared, first_t, first_s, cond_vec, signal_cols, signal, final_mod,
         ) = head(
-            slotted_block_weights[0], time_freq, facts, shared, w_first, w_second, w_class, w_fada,
-            b_first[None], b_second[None],
+            slotted_block_weights[0], time_freq, facts, shared, tables, w_fada, b_first[None],
+            b_second[None],
         )
     else:
+        w_first, w_second = tables[:, PATCH_VALUES:t2_row].T, tables[:, t2_row:class_row].T
         blocks = lax.all_gather(pack_blocks(slotted_block_weights[0]), "dp", axis=0, tiled=True)
         time_freq, facts, shared = exchange(
             [(time_freq, "gather"), (facts, "gather"), (shared, "gather")], "dp", 2
@@ -1633,9 +1738,10 @@
         first_t = dense(time_freq.astype(bf16), w_first) + b_first
         (first_s,) = exchange([(swish_unit(first_t).astype(bf16), "gather")], "dp", 3)
         labels_all = facts[:, :, 0].reshape(samples, 1).astype(jnp.int32)
-        onehot = labels_all == jnp.arange(1024, dtype=jnp.int32)[None, :]
+        onehot = labels_all == jnp.arange(CLASSES, dtype=jnp.int32)[None, :]
+        first_s = all_columns(first_s)
         cond_vec = (
-            dense(all_columns(first_s), w_second) + b_second + dense(onehot.astype(bf16), w_class)
+            dense(first_s, w_second) + b_second + dense(onehot.astype(bf16), tables[:, class_row:].T)
         )
         signal_cols = swish_unit(cond_vec).astype(bf16)
         signal, final_mod = exchange(
@@ -1793,6 +1899,11 @@
         parts = [x.reshape(x.shape[:-1] + (4, 4)) for x in (p, r)]
         return jnp.concatenate(parts, -1).reshape(p.shape[:-1] + (32,))
 
+    def thirds(x):
+        high = x.astype(bf16).astype(f32)
+        mid = (x - high).astype(bf16).astype(f32)
+        return [high, mid, x - high - mid]
+
     def lanes(x, rows):
         return jnp.pad(x, (0, rows * 128 - x.shape[0])).reshape(rows, 128)
 
@@ -1804,11 +1915,11 @@
     side_part = jnp.concatenate([sums_a[2], sums_m[3], sums_f[3], total_of(d_out)])
     slice_rows, side_rows = (-(-x.shape[0] // 1024) * 8 for x in (slice_part, side_part))
     bias_part = jnp.concatenate(
-        [lanes(slice_part, slice_rows), lanes(side_part, side_rows), lanes(loss_part[None], 8)], 0
+        [lanes(slice_part, slice_rows), lanes(side_part, side_rows), lanes(jnp.stack(thirds(loss_part)), 8)], 0
     )
     if tuned:
-        red_blocks, red_cond, red_head, red_slice, side_sum, side_mod, last = tail(
-            slot_grad, d_fmod.astype(f32), d_signal, small, bias_part, w_fada, w_second, cond_vec,
+        red_blocks, red_cond, red_head, red_slice, side_sum, side_mod, columns, last = tail(
+            slot_grad, d_fmod.astype(f32), d_signal, small, bias_part, w_fada, tables, cond_vec,
             first_t, signal_cols, first_s, time_freq, facts, slice_rows,
         )
     else:
@@ -1839,17 +1950,17 @@
         small, side_sum = jnp.sum(small, 0), jnp.sum(side_sum, 0)
         side_mod = total_of(d_fmod_all)
         g_class = jnp.einsum(
-            "sc,sd->cd", onehot[:, :CLASSES].astype(f32), d_cond, precision=exact_precision_flag
+            "sc,sd->cd", onehot.astype(f32), d_cond, precision=exact_precision_flag
         )
         red_cond = jnp.concatenate(
             [
                 small[:PATCH_VALUES],
                 weight_grad(time_freq.astype(bf16), d_first),
-                weight_grad(all_columns(first_s), d_second),
+                weight_grad(first_s, d_second),
                 g_class,
             ],
             0,
-        )
+        ).T
         red_head = jnp.concatenate([weight_grad(signal_cols, d_fmod_all), small[PATCH_VALUES:].T], 1)
         side_cols = jnp.stack([total_of(d_first), total_of(d_second)])
         local_squares = (
@@ -1866,11 +1977,12 @@
         last = jnp.pad(side_cols, ((0, 6), (0, LANES - cols)))
         last = jnp.where(jnp.arange(8)[:, None] == 2, local_squares, last)
         (last,) = exchange([(last, "gather")], EVERY, 8)
-    grad_norm = jnp.sqrt(jnp.sum(last[:, 2, 0]))
-    loss_sum = side_sum[side_rows, 0]
+        columns, last = last.reshape(dp, mp, 8, LANES)[:, 0], last[:, 2:3]
+    grad_norm = jnp.sqrt(jnp.sum(last[:, 0, 0]))
+    loss_sum = jnp.sum(side_sum[side_rows, :3])
     side_sum = side_sum[:side_rows].reshape(-1)[: side_part.shape[0]]
     red_slice = red_slice.reshape(-1)[: slice_part.shape[0]]
-    side_cols = last[:, :2, :cols].reshape(dp, mp, 2, cols)[:, 0].transpose(1, 0, 2).reshape(2 * width)
+    side_cols = columns[:, :2, :cols].transpose(1, 0, 2).reshape(2 * width)
     red_side = jnp.concatenate(
         [
             side_sum[:width],
@@ -1884,7 +1996,10 @@
     clipped, new_stats, new_blocks, new_low = shampoo(
         clip_factor, red_blocks, statistics[0], slotted_block_weights[0]
     )
-    cond_one, cond_two, new_cond = adam_update(cond_tables, red_cond * clip_factor, cond_m, cond_v)
+    cond_one, cond_two, new_cond = adam_update(
+        cond_tables.T, red_cond * clip_factor, cond_m.T, cond_v.T
+    )
+    cond_one, cond_two, new_cond = cond_one.T, cond_two.T, new_cond.T
     head_one, head_two, new_head = adam_update(head_tables, red_head * clip_factor, head_m, head_v)
     slice_one, slice_two, new_slice = adam_update(
         slice_bias[0], red_slice * clip_factor, slice_m[0], slice_v[0]

time: 775 us -> 708 us (0.914)
  Pallas kernels: 587 us -> 555 us
  local copies, waits for them, and re-layouts: 85.7 us -> 58.8 us
    pallas_call x2, Pallas kernels: 331 us -> 299 us  [the longest x1 162 us: tail(): pl.pallas_call(tail_body, in_specs=[vmem] * 12, out_specs=[vmem] * len(ou...]
    unnamed x152 -> x122, local copies, waits for them, and re-layouts: 38.3 us -> 20.6 us
where the time goes in v4:
time: 708 us; the launch traced here: 701 us
  Pallas kernels  555 us (78%)
  local copies, waits for them, and re-layouts  58.8 us (8%)
  matrix products  37.7 us (5%)
  other arithmetic  31.5 us (4%)
  blocking collectives  11.3 us (2%)
    pallas_call x1, Pallas kernels, tail(): pl.pallas_call(tail_body, in_specs=[vmem] * 12, out_specs=[vmem] * len(ou...  162 us
    pallas_call x4, Pallas kernels, stage(): pl.pallas_call(body, in_specs=[vmem] * n_in, out_specs=[vmem] * len(out_s...  149 us
    pallas_call x1, Pallas kernels, head(): pl.pallas_call(head_body, in_specs=[vmem] * 8, out_specs=[anywhere] + [vm...  137 us
    pallas_call x1, Pallas kernels, shampoo(): pl.pallas_call(shampoo_body, grid=(count // group,), in_specs=[pl.BlockSp...  87.7 us
    unnamed x122, local copies, waits for them, and re-layouts  20.6 us
    dot_general x6, matrix products, weight_grad(): jnp.einsum('...i,...j->ij', operand, gradient, preferred_element_type=jnp...  19.4 us

profile of v4, /device:TPU:0, one launch (start us, length us, event | category | flops | bytes accessed | tf_op | source)
XLA Modules:
  0.0 701.0 jit_solution(16751062924101725312)
XLA Ops:
  0.7 1.2 dynamic_slice.45
  9.2 1.4 slice_reduce_fusion.7
  10.6 1.4 slice.220.refs_5_
  18.5 1.3 pad_maximum_fusion.1
  21.5 2.1 copy.227
  23.9 2.1 copy-done.7
  26.0 137.0 %head.1 = (bf16[72,656,128]{2,1,0:T(8,128)(2,1)}, f32[32,256]{1,0:T(8,128)S(1)}, f32[8,8,128]{2,1,0:T(8,128)S(1)}, bf16[8,48,256]{2,1,0:T(8,128)(2,1)S(1)}, f32[...) custom-call(f32[9,288,288]{2,1,0:T(8,128)S(1)} %bitcast.211, ...), custom_call_target="tpu_custom_call" | custom-call | tf_op jit(solution)/shard_map/head/pallas_call | solution.py:1028
  168.2 2.7 stack.55
  175.1 4.4 copy-done
  180.4 3.9 assemble.5.refs_1_
  184.4 1.5 copy-done.3
  185.9 6.8 assemble.3
  192.8 2.0 copy-done.1
  195.6 5.7 all-gather
  204.2 1.3 pad_maximum_fusion.5
  207.9 1.6 dynamic-slice_bitcast_fusion.refs_3_.refs_2_
  209.8 3.0 fusion.12
  216.0 1.2 copy.235.refs_0_
  217.1 41.5 %stage_9.1 = (f32[256,1152]{1,0:T(8,128)}, f32[256,1152]{1,0:T(8,128)}, f32[4,256,1152]{2,1,0:T(8,128)}, bf16[4,256,1152]{2,1,0:T(8,128)(2,1)}, bf16[4,256,1152]{2,1,0:T(8,128)(2,1)}) custom-call(bf16[4,256,288]{2,1,0:T(8,128)(2,1)} %copy.235.refs_0_, bf16[288,1152]{1,0:T(8,128)(2,1)} %copy-done.6, bf16[1152,1152]{1,0:T(8,128)(2,1)} %copy-done.2, ...), custom_call_target="tpu_custom_call" | custom-call | tf_op jit(solution)/shard_map/stage_9/pallas_call | solution.py:536
  258.6 45.4 %stage_10.1 = (f32[256,1152]{1,0:T(8,128)}, bf16[256,1152]{1,0:T(8,128)(2,1)}, bf16[256,16]{1,0:T(8,128)(2,1)}, bf16[256,16]{1,0:T(8,128)(2,1)}, f32[4,1152]{1,0...) custom-call(bf16[4,256,1152]{2,1,0:T(8,128)(2,1)} %get-tuple-element, ...), custom_call_target="tpu_custom_call" | custom-call | tf_op jit(solution)/shard_map/stage_10/pallas_call | solution.py:536
  304.0 1.2 reduce_sum.146
  306.6 39.0 %stage_11.1 = (f32[256,1152]{1,0:T(8,128)}, f32[4,1152]{1,0:T(4,128)}, bf16[4,256,288]{2,1,0:T(8,128)(2,1)}, bf16[4,256,1152]{2,1,0:T(8,128)(2,1)}) custom-call(bf16[4,256,1152]{2,1,0:T(8,128)(2,1)} %get-tuple-element.77.refs_0_, bf16[1152,1152]{1,0:T(8,128)(2,1)} %copy-done.2, bf16[288,1152]{1,0:T(8,128)(2,1)} %copy-done.6, ...), custom_call_target="tpu_custom_call" | custom-call | tf_op jit(solution)/shard_map/stage_11/pallas_call | solution.py:536
  345.7 4.8 fusion.refs_1_
  351.6 2.9 fusion.5.refs_4_
  354.8 4.8 fusion.1.refs_5_
  359.6 1.7 bitcast_reduce_fusion
  361.5 1.4 copy.247
  362.9 3.7 multiply_reduce_fusion.1
  366.6 1.1 multiply_convert_fusion
  367.8 1.6 fusion.21
  369.4 1.5 bitcast_reduce_fusion.1
  371.0 1.4 copy.246
  372.4 1.4 copy.245
  373.8 2.1 pad_maximum_fusion.refs_0_
  375.9 23.0 %stage_12.1 = (bf16[256,1152]{1,0:T(8,128)(2,1)}, f32[3,1152]{1,0:T(4,128)}) custom-call(bf16[4,256,864]{2,1,0:T(8,128)(2,1)} %pad_maximum_fusion.refs_0_, bf16[1152,864]{1,0:T(8,128)(2,1)} %copy-done.10, f32[256,1152]{1,0:T(8,128)} %dynamic-slice_bitcast_fusion.refs_3_.refs_2_, f32[256,1152]{1,0:T(8,128)} %get-tuple-element.82.refs_3_, ...), custom_call_target="tpu_custom_call" | custom-call | tf_op jit(solution)/shard_map/stage_12/pallas_call | solution.py:536
  399.0 6.5 bitcast_convert_fusion
  405.9 2.9 copy.253.refs_0_
  408.7 5.6 all-gather.1
  415.3 3.3 convolution_convert_fusion.2
  420.4 1.7 copy-done.8
  422.2 1.7 copy-done.9
  423.9 8.3 %to_slots.1.x_ref = bf16[72,656,128]{2,1,0:T(8,128)(2,1)} custom-call(s32[72]{0:T(128)S(1)} %copy-done.16, bf16[1152,864]{1,0:T(8,128)(2,1)S(1)} %copy.253.refs_0_, bf16[1152,1152]{1,0:T(8,128)(2,1)S(1)} %copy-done.8, bf16[4,4,288]{2,1,0:T(4,128)(2,1)S(1)} %bitcast.214, bf16[4,1728]{1,0:T(4,128)(2,1)S(1)} %bitcast.213, bf16[288,1152]{1,0:T(8,128)(2,1)S(1)} %fusion.5.refs_4_, ...), custom_call_target="tpu_custom_call" | custom-call | bytes 23887872 | tf_op jit(solution)/shard_map/to_slots/pallas_call | solution.py:391
  432.3 161.9 %tail.1 = (f32[9,656,128]{2,1,0:T(8,128)}, f32[144,2425]{1,0:T(8,128)}, f32[144,2336]{1,0:T(8,128)}, f32[32,128]{1,0:T(8,128)}, f32[40,128]{1,0:T(8,128)}, /*ind...) custom-call(bf16[72,656,128]{2,1,0:T(8,128)(2,1)} %to_slots.1.x_ref, ...), custom_call_target="tpu_custom_call" | custom-call | tf_op jit(solution)/shard_map/tail/pallas_call | solution.py:1479
  594.2 1.3 slice_reduce_fusion.8
  596.2 1.4 slice_reduce_fusion
  603.6 5.2 fusion.67
  608.9 3.1 fusion.65
  611.9 87.7 %shampoo.1 = (f32[9,288,288]{2,1,0:T(8,128)}, f32[9,2,288,288]{3,2,1,0:T(8,128)}, f32[9,288,288]{2,1,0:T(8,128)}, bf16[9,288,288]{2,1,0:T(8,128)(2,1)}) custom-call(f32[1]{0:T(128)} %bitcast.60.clip_ref, f32[9,656,128]{2,1,0:T(8,128)} %get-tuple-element.101.g_ref, f32[9,2,288,288]{3,2,1,0:T(8,128)} %bitcast.246, f32[9,288,288]{2,1,0:T(8,128)} %bitcast.210), custom_call_target="tpu_custom_call" | custom-call | flops 56757583872 | bytes 25380864 | tf_op jit(solution)/shard_map/shampoo/pallas_call | solution.py:1626
  (248 shorter events, 44.6 us)
Async XLA Ops:
  17.0 2.8 copy-start.22
  18.5 1.8 copy-start.24
  19.8 4.0 copy-start.4
  20.4 142.7 %copy-start.5 = (bf16[144,2304]{1,0:T(8,128)(2,1)}, bf16[144,2304]{1,0:T(8,128)(2,1)S(1)}, u32[]{:S(2)}) copy-start(bf16[144,2304]{1,0:T(8,128)(2,1)S(1)} %slice.257.fada_ref) | copy-start | bytes 1990660
  23.9 2.1 copy-start.7
  166.2 9.0 %copy-start.16 = (s32[72]{0:T(128)S(1)}, s32[72]{0:T(128)}, u32[]{:S(2)}) copy-start(s32[72]{0:T(128)} %ids.7) | copy-start | bytes 868
  175.1 4.4 copy-start
  180.4 4.0 copy-start.6
  192.8 2.0 copy-start.1
  192.8 2.9 copy-start.2
  192.8 16.7 %copy-start.10 = (bf16[1152,864]{1,0:T(8,128)(2,1)}, bf16[1152,864]{1,0:T(8,128)(2,1)S(1)}, u32[]{:S(2)}) copy-start(bf16[1152,864]{1,0:T(8,128)(2,1)S(1)} %get-tuple-element.70.refs_1_) | copy-start | bytes 5971972
  194.8 11.5 %copy-start.26 = (f32[16,16,1152]{2,1,0:T(8,128)S(1)}, f32[16,16,1152]{2,1,0:T(8,128)}, u32[]{:S(2)}) copy-start(f32[16,16,1152]{2,1,0:T(8,128)} %pad_maximum_fusion.1) | copy-start | bytes 3538948
  206.3 3.2 copy-start.48
  207.3 2.5 copy-start.20
  209.8 3.1 copy-start.52
  213.2 2.6 copy-start.28
  213.9 2.0 copy-start.17
  216.0 42.6 %copy-start.37 = (bf16[4,4,72,256]{3,2,1,0:T(8,128)(2,1)}, bf16[4,4,72,256]{3,2,1,0:T(8,128)(2,1)S(1)}, u32[]{:S(2)}) copy-start(bf16[4,4,72,256]{3,2,1,0:T(8,128)(2,1)S(1)} %fusion.19) | copy-start | bytes 1769476
  306.6 39.0 %copy-start.27 = (bf16[4,256,1152]{2,1,0:T(8,128)(2,1)S(1)}, bf16[4,256,1152]{2,1,0:T(8,128)(2,1)}, u32[]{:S(2)}) copy-start(bf16[4,256,1152]{2,1,0:T(8,128)(2,1)} %get-tuple-element.77.refs_0_) | copy-start | bytes 7077892
  306.6 39.0 %copy-start.55 = (bf16[4,256,1152]{2,1,0:T(8,128)(2,1)S(1)}, bf16[4,256,1152]{2,1,0:T(8,128)(2,1)}, u32[]{:S(2)}) copy-start(bf16[4,256,1152]{2,1,0:T(8,128)(2,1)} %get-tuple-element.81) | copy-start | bytes 7077892
  345.6 4.8 copy-start.34
  345.6 5.2 copy-start.53
  345.6 5.2 copy-start.40
  345.6 5.3 copy-start.39
  345.6 5.4 copy-start.35
  345.6 5.8 copy-start.46
  345.6 5.8 copy-start.45
  351.5 3.0 copy-start.29
  351.6 3.3 copy-start.54
  354.8 4.8 copy-start.18
  362.9 3.7 copy-start.19
  375.9 23.0 %copy-start.21 = (bf16[4,256,864]{2,1,0:T(8,128)(2,1)S(1)}, bf16[4,256,864]{2,1,0:T(8,128)(2,1)}, u32[]{:S(2)}) copy-start(bf16[4,256,864]{2,1,0:T(8,128)(2,1)} %pad_maximum_fusion.refs_0_) | copy-start | bytes 5308420
  375.9 23.0 %copy-start.49 = (f32[4,1152]{1,0:T(4,128)S(1)}, f32[4,1152]{1,0:T(4,128)}, u32[]{:S(2)}) copy-start(f32[4,1152]{1,0:T(4,128)} %copy-done.48) | copy-start | bytes 55300
  399.0 6.5 copy-start.47
  399.0 6.5 copy-start.36
  432.2 163.3 %copy-start.44 = (f32[8096]{0:T(1024)S(1)}, f32[8096]{0:T(1024)}, u32[]{:S(2)}) copy-start(f32[8096]{0:T(1024)} %custom-call) | copy-start | bytes 97156
  432.2 169.9 %copy-start.41 = (f32[1,3456]{1,0:T(1,128)S(1)}, f32[1,3456]{1,0:T(1,128)}, u32[]{:S(2)}) copy-start(f32[1,3456]{1,0:T(1,128)} %param.30) | copy-start | bytes 41476
  432.2 169.9 %copy-start.50 = (f32[1,3456]{1,0:T(1,128)S(1)}, f32[1,3456]{1,0:T(1,128)}, u32[]{:S(2)}) copy-start(f32[1,3456]{1,0:T(1,128)} %param.37) | copy-start | bytes 41476
  432.3 169.9 %copy-start.51 = (f32[1,3456]{1,0:T(1,128)S(1)}, f32[1,3456]{1,0:T(1,128)}, u32[]{:S(2)}) copy-start(f32[1,3456]{1,0:T(1,128)} %param.36) | copy-start | bytes 41476
  432.3 170.6 %copy-start.38 = (f32[8096]{0:T(1024)S(1)}, f32[8096]{0:T(1024)}, u32[]{:S(2)}) copy-start(f32[8096]{0:T(1024)} %param.31) | copy-start | bytes 97156
  432.3 170.6 %copy-start.42 = (f32[8096]{0:T(1024)S(1)}, f32[8096]{0:T(1024)}, u32[]{:S(2)}) copy-start(f32[8096]{0:T(1024)} %param.39) | copy-start | bytes 97156
  432.3 170.6 %copy-start.43 = (f32[8096]{0:T(1024)S(1)}, f32[8096]{0:T(1024)}, u32[]{:S(2)}) copy-start(f32[8096]{0:T(1024)} %param.38) | copy-start | bytes 97156
  432.3 171.2 %copy-start.23 = (f32[2425,144]{0,1:T(8,128)S(1)}, f32[2425,144]{0,1:T(8,128)}, u32[]{:S(2)}) copy-start(f32[2425,144]{0,1:T(8,128)} %param.28) | copy-start | bytes 4190404
  432.3 171.2 %copy-start.30 = (f32[2425,144]{0,1:T(8,128)S(1)}, f32[2425,144]{0,1:T(8,128)}, u32[]{:S(2)}) copy-start(f32[2425,144]{0,1:T(8,128)} %param.33) | copy-start | bytes 4190404
  603.6 5.3 copy-start.25
  603.6 5.3 copy-start.31
  603.6 5.3 copy-start.32
  603.6 5.3 copy-start.33
  (8 other events, 8.1 us)

commit v5 on v4

--- a/solution.py
+++ b/solution.py
@@ -456,7 +456,7 @@
         across = lax.rem(me + 2, 4)
         other = lax.rem(core + 2, 4)
         to_core, to_across = {"mp": core}, {"mp": across}
-        partial, own, after = make(ins, outs, share)
+        partial, own, after, side = make(ins, outs, share)
         barrier = pltpu.get_barrier_semaphore()
         signal_to(barrier, to_core)
         signal_to(barrier, to_across)
@@ -499,6 +499,8 @@
         copy_c.wait_recv()
         for i in range(pieces):
             at = piece(i)
+            if side and not shared:
+                side(i)
             copy_b(i).wait_recv()
             result = own(
                 i * CHUNK, total[at] + c_in[at].astype(jnp.float32) + b_in[at].astype(jnp.float32)
@@ -507,18 +509,23 @@
                 share[me, at] = result
                 share_far(me, i).start()
                 share_near(me, i).start()
+                if side:
+                    side(i)
         if shared:
-            after(me)
+            for i in range(pieces):
+                after(me, i * CHUNK)
             for i in range(pieces):
                 share_near(core, i).wait_recv()
-            after(core)
+                after(core, i * CHUNK)
             for i in range(pieces):
                 share_far(across, i).wait_recv()
                 pass_near(across, i).start()
-            after(across)
-            for i in range(pieces):
-                pass_near(other, i).wait_recv()
-            after(other)
+                after(across, i * CHUNK)
+                if i > 0:
+                    pass_near(other, i - 1).wait_recv()
+                    after(other, (i - 1) * CHUNK)
+            pass_near(other, pieces - 1).wait_recv()
+            after(other, (pieces - 1) * CHUNK)
         copy_a.wait_send()
         copy_c.wait_send()
         for i in range(pieces):
@@ -570,14 +577,13 @@
             normed, _ = norm_rows(middle)
             return (normed * (1.0 + rows_ref[2:3]) + rows_ref[3:4]).astype(jnp.bfloat16)
 
-        def after(group):
-            for at in range(0, n, CHUNK):
-                at = slice(at, at + CHUNK)
-                hidden = times(share[group, at], w_up_ref[...]) + up_ref[...]
-                hidden_ref[group, at] = hidden
-                active_ref[group, at] = tanh_gelu_activation(hidden).astype(jnp.bfloat16)
-
-        return partial, own, after
+        def after(group, at):
+            at = slice(at, at + CHUNK)
+            hidden = times(share[group, at], w_up_ref[...]) + up_ref[...]
+            hidden_ref[group, at] = hidden
+            active_ref[group, at] = tanh_gelu_activation(hidden).astype(jnp.bfloat16)
+
+        return partial, own, after, None
 
     inner = w_up.shape[1]
     return stage(
@@ -638,15 +644,14 @@
             sums_ref[3:4] += column_sum(d_branch.astype(f32))
             return d_branch
 
-        def after(group):
-            for at in range(0, n, CHUNK):
-                at = slice(at, at + CHUNK)
-                d_active = times_flipped(share[group, at], w_ref[...])
-                d_hidden = (d_active * gelu_slope(hidden_ref[group, at])).astype(bf16)
-                d_hidden_ref[group, at] = d_hidden
-                up_sum_ref[...] += column_sum(d_hidden.astype(f32))
-
-        return partial, own, after
+        def after(group, at):
+            at = slice(at, at + CHUNK)
+            d_active = times_flipped(share[group, at], w_ref[...])
+            d_hidden = (d_active * gelu_slope(hidden_ref[group, at])).astype(bf16)
+            d_hidden_ref[group, at] = d_hidden
+            up_sum_ref[...] += column_sum(d_hidden.astype(f32))
+
+        return partial, own, after, None
 
     half = w_pred.shape[1]
     return stage(
@@ -667,12 +672,26 @@
     )
 
 
-def middle_back_stage(d_hidden, w_up, w_o, middle, d_final, attn, rows):
+def gradient_part(out_ref, a_ref, b_ref, i):
+    width = a_ref.shape[2]
+    step = max(width // 512, 1) * 128
+    at = slice(min(i * step, width), width if i == 3 else min((i + 1) * step, width))
+    if at.start < at.stop:
+        tokens = a_ref.shape[0] * a_ref.shape[1]
+        a = a_ref[:, :, at].reshape(tokens, at.stop - at.start)
+        b = b_ref[...].reshape(tokens, b_ref.shape[2])
+        out_ref[at] = outer(a, b).astype(jnp.bfloat16)
+
+
+def middle_back_stage(d_hidden, w_up, w_o, middle, d_final, attn, rows, active, d_branch):
     n, width, f32, bf16 = d_hidden.shape[1], MODEL_WIDTH, jnp.float32, jnp.bfloat16
 
     def make(ins, outs, share):
-        d_hidden_ref, w_up_ref, w_o_ref, middle_ref, d_final_ref, attn_ref, rows_ref = ins
-        d_middle_ref, sums_ref, d_mixed_ref = outs
+        (
+            d_hidden_ref, w_up_ref, w_o_ref, middle_ref, d_final_ref, attn_ref, rows_ref, active_ref,
+            d_branch_ref,
+        ) = ins
+        d_middle_ref, sums_ref, d_mixed_ref, g_down_ref = outs
         sums_ref[...] = jnp.zeros_like(sums_ref)
 
         def partial(group):
@@ -690,26 +709,36 @@
             sums_ref[3:4] += column_sum(d_attn.astype(f32))
             return d_attn
 
-        def after(group):
-            d_mixed_ref[group] = times_flipped(share[group], w_o_ref[...]).astype(bf16)
-
-        return partial, own, after
+        def after(group, at):
+            at = slice(at, at + CHUNK)
+            d_mixed_ref[group, at] = times_flipped(share[group, at], w_o_ref[...]).astype(bf16)
+
+        def side(i):
+            gradient_part(g_down_ref, active_ref, d_branch_ref, i)
+
+        return partial, own, after, side
 
     return stage(
         11,
-        [d_hidden, w_up, w_o, middle, d_final, attn, rows],
-        [((n, width), f32), ((4, width), f32), ((4, n, w_o.shape[0]), bf16)],
+        [d_hidden, w_up, w_o, middle, d_final, attn, rows, active, d_branch],
+        [
+            ((n, width), f32),
+            ((4, width), f32),
+            ((4, n, w_o.shape[0]), bf16),
+            ((active.shape[2], width), bf16),
+        ],
         True,
         make,
     )
 
 
-def start_back_stage(d_proj, w_qkv, start, d_middle, rows):
+def start_back_stage(d_proj, w_qkv, start, d_middle, rows, attn_in, mlp_in, d_hidden, mixed, d_attn):
     n, width, f32, bf16 = d_proj.shape[1], MODEL_WIDTH, jnp.float32, jnp.bfloat16
 
     def make(ins, outs, share):
-        d_proj_ref, w_ref, start_ref, d_middle_ref, rows_ref = ins
-        d_start_ref, sums_ref = outs
+        d_proj_ref, w_ref, start_ref, d_middle_ref, rows_ref = ins[:5]
+        attn_in_ref, mlp_in_ref, d_hidden_ref, mixed_ref, d_attn_ref = ins[5:]
+        d_start_ref, sums_ref, g_qkv_ref, g_up_ref, g_outp_ref = outs
         sums_ref[...] = jnp.zeros_like(sums_ref)
 
         def partial(group):
@@ -725,12 +754,23 @@
             sums_ref[1:2] += column_sum(total * normed)
             sums_ref[2:3] += column_sum(d_start.astype(f32))
 
-        return partial, own, None
+        def side(i):
+            gradient_part(g_up_ref, mlp_in_ref, d_hidden_ref, i)
+            gradient_part(g_qkv_ref, attn_in_ref, d_proj_ref, i)
+            gradient_part(g_outp_ref, mixed_ref, d_attn_ref, i)
+
+        return partial, own, None, side
 
     return stage(
         12,
-        [d_proj, w_qkv, start, d_middle, rows],
-        [((n, width), bf16), ((3, width), f32)],
+        [d_proj, w_qkv, start, d_middle, rows, attn_in, mlp_in, d_hidden, mixed, d_attn],
+        [
+            ((n, width), bf16),
+            ((3, width), f32),
+            ((width, d_proj.shape[2]), bf16),
+            ((width, d_hidden.shape[2]), bf16),
+            ((mixed.shape[2], width), bf16),
+        ],
         False,
         make,
     )
@@ -1081,7 +1121,7 @@
     x_ref, early_ref, small_ref, bias_ref, fada_ref, tables_ref, cond_ref, first_t_ref,
     signal_ref, first_s_ref, tf_ref, facts_ref,
     out_ref, g_cond_ref, g_head_ref, slice_ref, side_ref, mod_sum_ref, columns_all, last_all,
-    side_buf, up_buf, down_buf, other_buf, up_other, down_other, early_land, small_land,
+    side_buf, up_buf, down_buf, other_buf, up_other, down_other, early_land, early_mp, small_land,
     bias_land, dsig_all, first_own, first_land, small_own, small_mp, side_own, side_mp, fmod_all, columns_own,
     last_own, hot_buf,
     side_send, line_send, side_recv, up_recv, down_recv, other_send, other_up, other_down,
@@ -1119,7 +1159,8 @@
     def push_mp(j, source, landing):
         return Push(source, landing, send_mp.at[j], recv_mp.at[j], mp, my_mp, lambda i: {"mp": i})
 
-    first = [push_all(0, early_ref, early_land, lambda to: to // mp)]
+    first = [push_dp(4, early_ref, early_land, lambda to: to)]
+    early_pass = push_mp(2, early_land, early_mp)
     second = [push_dp(0, small_ref, small_land, lambda to: to), push_dp(1, bias_ref, bias_land)]
     third = push_dp(2, first_own, first_land, lambda to: to)
     fifth = push_dp(3, columns_own, columns_all)
@@ -1268,18 +1309,22 @@
     def add_shared(x):
         held["shared"] = held["shared"] + square(x)
 
-    def signal_back():
+    def pass_early():
         for p in first:
             p.wait()
+        early_pass.start()
+
+    def signal_back():
+        early_pass.wait()
         lines = fmod_all.shape[1] // 128
         for i in range(everyone):
-            here = early_land[i].astype(f32)
+            here = early_mp[i % mp, i // mp].astype(f32)
             for j in range(lines):
                 fmod_all[i : i + 1, j * 128 : (j + 1) * 128] = here[j : j + 1]
         for i in range(ways):
-            here = early_land[i * mp].astype(f32)[24:]
+            here = early_mp[0, i].astype(f32)[24:]
             for j in range(1, mp):
-                here = here + early_land[i * mp + j].astype(f32)[24:]
+                here = here + early_mp[j, i].astype(f32)[24:]
             dsig_all[i * batch : (i + 1) * batch, :128] = here[:batch]
             dsig_all[i * batch : (i + 1) * batch, 128:] = here[batch:]
         d_signal = dsig_all[:, :cols] + times_flipped(fmod_all[...].astype(bf16), fada_ref[...])
@@ -1358,10 +1403,11 @@
         (0, lambda: run_late(3)),
         (3, lambda: run_late(2)),
         (12, lambda: run_late(1)),
-        (22, signal_back),
-        (25, second_back),
-        (30, bias_sums),
-        (35, fada_gradient),
+        (20, pass_early),
+        (29, signal_back),
+        (31, second_back),
+        (35, bias_sums),
+        (38, fada_gradient),
         (40, second_gradient),
         (45, class_gradient),
         (57, first_gradient),
@@ -1409,7 +1455,7 @@
     squares = held["shared"] / mp + held["slice"] / ways + held["every"] / (ways * mp)
     squares += jnp.sum(last_own[...], axis=1, keepdims=True)
     last_own[...] = jnp.broadcast_to(squares, (1, 128))
-    sixth = push_all(1, last_own, last_all)
+    sixth = push_all(0, last_own, last_all)
     sixth.start()
 
     def sent(k, _):
@@ -1484,7 +1530,8 @@
         scratch_shapes=[landing] * 3
         + [few] * 3
         + [
-            scratch((ways * mp,) + early.shape[1:], bf16),
+            scratch(early.shape, bf16),
+            scratch((mp,) + early.shape, bf16),
             scratch(small.shape, bf16),
             scratch((ways,) + bias.shape, bf16),
             scratch((rows, LANES), f32),
@@ -1501,9 +1548,9 @@
         ]
         + [dma((LAYERS, count))] * 5
         + [dma((LAYERS, CROSS_LATE))] * 3
-        + [dma((2, ways * mp))] * 2
-        + [dma((4, ways))] * 2
-        + [dma((2, mp))] * 2,
+        + [dma((1, ways * mp))] * 2
+        + [dma((5, ways))] * 2
+        + [dma((3, mp))] * 2,
         compiler_params=pltpu.CompilerParams(
             collective_id=1, has_side_effects=True, vmem_limit_bytes=58 * 2**20
         ),
@@ -1558,7 +1605,7 @@
         more = newton_step < NEWTON - 1
         factors = [((5.0 * eye_main - m) * 0.25, (5.0 * eye_tail - t) * 0.25) for m, t in contracted]
         rights = [(right_form(m), right_form(t)) for m, t in factors]
-        lefts = [left_form(m, t) for m, t in factors]
+        lefts = [left_form(m, t) for m, t in factors] if more else None
         if more:
             powers = [symmetric_product(l, *r) for l, r in zip(lefts, rights)]
         if estimates is None:
@@ -1856,12 +1903,9 @@
     )
     loss_part = jnp.sum(loss_part)
     d_fmod = sums_f[:2].reshape(1, 2 * width).astype(bf16)
-    g_down = weight_grad(active, d_branch).astype(bf16)
-    d_middle, sums_m, d_mixed, d_attn = middle_back_stage(
-        d_hidden, w_up, w_o, middle, d_final, attn, rows_of(scale2, gate1)
-    )
-    g_up = weight_grad(mlp_in, d_hidden).astype(bf16)
-    g_outp = weight_grad(mixed, d_attn).astype(bf16)
+    d_middle, sums_m, d_mixed, g_down, d_attn = middle_back_stage(
+        d_hidden, w_up, w_o, middle, d_final, attn, rows_of(scale2, gate1), active, d_branch
+    )
     d_mixed = heads_of(d_mixed)
     probs = jnp.exp(
         jnp.einsum("slhe,smhe->shlm", queries, keys, preferred_element_type=f32) * score_scale
@@ -1881,8 +1925,9 @@
     flat_q = d_query.reshape(batch, seq_len, query_width)
     flat_v = d_values.reshape(batch, seq_len, query_width)
     d_proj = jnp.concatenate([flat_q, d_keys.reshape(batch, seq_len, query_width), flat_v], 2)
-    g_qkv = weight_grad(attn_in, d_proj).astype(bf16)
-    d_start, sums_a = start_back_stage(d_proj, w_qkv, start, d_middle, scale1.reshape(1, width))
+    d_start, sums_a, g_qkv, g_up, g_outp = start_back_stage(
+        d_proj, w_qkv, start, d_middle, scale1.reshape(1, width), attn_in, mlp_in, d_hidden, mixed, d_attn
+    )
     d_mod_own = jnp.concatenate(
         [sums_a[0], sums_a[1], sums_m[2], sums_m[0], sums_m[1], sums_f[2]]
     ).reshape(1, 6 * width)
@@ -1999,8 +2044,9 @@
     cond_one, cond_two, new_cond = adam_update(
         cond_tables.T, red_cond * clip_factor, cond_m.T, cond_v.T
     )
-    cond_one, cond_two, new_cond = cond_one.T, cond_two.T, new_cond.T
+    cond_short = new_cond.astype(bf16)
     head_one, head_two, new_head = adam_update(head_tables, red_head * clip_factor, head_m, head_v)
+    head_short = new_head.astype(bf16)
     slice_one, slice_two, new_slice = adam_update(
         slice_bias[0], red_slice * clip_factor, slice_m[0], slice_v[0]
     )
@@ -2013,14 +2059,14 @@
         new_stats[None],
         new_blocks[None],
         new_low[None],
-        cond_one,
-        cond_two,
-        new_cond,
-        new_cond.astype(bf16),
+        cond_one.T,
+        cond_two.T,
+        new_cond.T,
+        cond_short.T,
         head_one,
         head_two,
         new_head,
-        new_head.astype(bf16),
+        head_short,
         slice_one[None],
         slice_two[None],
         new_slice[None],

time: 708 us -> 689 us (0.973)
  matrix products: 37.7 us -> 19.7 us
    dot_general x6 -> x2, matrix products: 19.4 us -> 1.45 us  [weight_grad(): jnp.einsum('...i,...j->ij', operand, gradient, preferred_element_type=jnp...]
    unnamed x122 -> x100, local copies, waits for them, and re-layouts: 20.6 us -> 20.2 us
where the time goes in v5:
time: 689 us; the launch traced here: 681 us
  Pallas kernels  554 us (80%)
  local copies, waits for them, and re-layouts  54.9 us (8%)
  other arithmetic  35 us (5%)
  matrix products  19.7 us (3%)
  blocking collectives  11.3 us (2%)
    pallas_call x1, Pallas kernels, tail(): pl.pallas_call(tail_body, in_specs=[vmem] * 12, out_specs=[vmem] * len(ou...  158 us
    pallas_call x4, Pallas kernels, stage(): pl.pallas_call(body, in_specs=[vmem] * n_in, out_specs=[vmem] * len(out_s...  152 us
    pallas_call x1, Pallas kernels, head(): pl.pallas_call(head_body, in_specs=[vmem] * 8, out_specs=[anywhere] + [vm...  137 us
    pallas_call x1, Pallas kernels, shampoo(): pl.pallas_call(shampoo_body, grid=(count // group,), in_specs=[pl.BlockSp...  87.7 us
    unnamed x100, local copies, waits for them, and re-layouts  20.2 us

profile of v5, /device:TPU:0, one launch (start us, length us, event | category | flops | bytes accessed | tf_op | source)
XLA Modules:
  0.0 681.4 jit_solution(9832317124614923473)
XLA Ops:
  0.7 1.2 dynamic_slice.45
  9.2 1.4 slice_reduce_fusion.7
  10.6 1.4 slice.220.refs_5_
  15.6 1.1 add_convert_fusion.1
  18.5 1.3 pad_maximum_fusion.1
  21.6 2.1 copy.177
  24.0 2.1 copy-done.7
  26.1 137.0 %head.1 = (bf16[72,656,128]{2,1,0:T(8,128)(2,1)}, f32[32,256]{1,0:T(8,128)S(1)}, f32[8,8,128]{2,1,0:T(8,128)S(1)}, bf16[8,48,256]{2,1,0:T(8,128)(2,1)S(1)}, f32[...) custom-call(f32[9,288,288]{2,1,0:T(8,128)S(1)} %bitcast.189, ...), custom_call_target="tpu_custom_call" | custom-call | tf_op jit(solution)/shard_map/head/pallas_call | solution.py:1068
  168.3 2.7 stack.55
  175.3 4.4 copy-done
  180.6 3.9 assemble.5.refs_1_
  184.5 1.5 copy-done.3
  186.0 6.8 %assemble.3 = (bf16[1152,864]{1,0:T(8,128)(2,1)S(1)}, bf16[1152,1152]{1,0:T(8,128)(2,1)S(1)}, bf16[1152,1728]{1,0:T(8,128)(2,1)S(1)}) custom-call(s32[72]{0:T(128)S(1)} %copy-done.18, bf16[72,656,128]{2,1,0:T(8,128)(2,1)} %get-tuple-element.72.refs_0_.refs_1_.refs_2_.refs_3_.refs_4_.refs_5_.refs_6_.refs_7_.refs_8_.refs_9_.refs_10_.refs_11_.refs_12_, ...), custom_call_target="tpu_custom_call" | custom-call | bytes 17252352 | tf_op jit(solution)/shard_map/assemble/pallas_call | solution.py:296
  192.9 1.5 copy-done.2
  195.0 5.7 all-gather
  201.5 0.9 dynamic-slice_bitcast_fusion.1
  203.7 1.3 pad_maximum_fusion.5
  205.8 0.9 fusion.69
  207.4 1.1 dynamic-slice_bitcast_fusion.refs_3_.refs_2_
  208.5 2.0 add_convert_fusion.refs_5_
  210.5 2.5 fusion.9
  214.9 1.2 copy-done.19
  216.1 1.0 fusion.15
  217.2 1.2 copy.185.refs_0_.refs_8_
  218.3 39.8 %stage_9.1 = (f32[256,1152]{1,0:T(8,128)}, f32[256,1152]{1,0:T(8,128)}, f32[4,256,1152]{2,1,0:T(8,128)}, bf16[4,256,1152]{2,1,0:T(8,128)(2,1)}, bf16[4,256,1152]{2,1,0:T(8,128)(2,1)}) custom-call(bf16[4,256,288]{2,1,0:T(8,128)(2,1)} %copy.185.refs_0_.refs_8_, bf16[288,1152]{1,0:T(8,128)(2,1)} %copy-done.6, bf16[1152,1152]{1,0:T(8,128)(2,1)} %copy-done.2, ...), custom_call_target="tpu_custom_call" | custom-call | tf_op jit(solution)/shard_map/stage_9/pallas_call | solution.py:543
  258.2 43.2 %stage_10.1 = (f32[256,1152]{1,0:T(8,128)}, bf16[256,1152]{1,0:T(8,128)(2,1)}, bf16[256,16]{1,0:T(8,128)(2,1)}, bf16[256,16]{1,0:T(8,128)(2,1)}, f32[4,1152]{1,0...) custom-call(bf16[4,256,1152]{2,1,0:T(8,128)(2,1)} %get-tuple-element, ...), custom_call_target="tpu_custom_call" | custom-call | tf_op jit(solution)/shard_map/stage_10/pallas_call | solution.py:543
  301.4 1.2 reduce_sum.146
  303.9 41.0 %stage_11.1 = (f32[256,1152]{1,0:T(8,128)}, f32[4,1152]{1,0:T(4,128)}, bf16[4,256,288]{2,1,0:T(8,128)(2,1)}, bf16[1152,1152]{1,0:T(8,128)(2,1)}, bf16[4,256,1152]{2,1,0:T(8,128)(2,1)}) custom-call(bf16[4,256,1152]{2,1,0:T(8,128)(2,1)} %get-tuple-element.81.refs_0_.refs_7_, bf16[1152,1152]{1,0:T(8,128)(2,1)} %copy-done.2, bf16[288,1152]{1,0:T(8,128)(2,1)} %copy-done.6, ...), custom_call_target="tpu_custom_call" | custom-call | tf_op jit(solution)/shard_map/stage_11/pallas_call | solution.py:543
  345.0 1.4 copy.191
  347.2 3.9 bitcast_reduce_fusion
  351.2 1.4 copy.197
  352.7 3.5 multiply_reduce_fusion.1
  356.2 1.1 multiply_convert_fusion
  359.6 2.3 pad_maximum_fusion.refs_0_
  361.9 27.7 %stage_12.1 = (bf16[256,1152]{1,0:T(8,128)(2,1)}, f32[3,1152]{1,0:T(4,128)}, bf16[1152,864]{1,0:T(8,128)(2,1)}, bf16[1152,1152]{1,0:T(8,128)(2,1)}, bf16[288,1152]{1,0:T(8,128)(2,1)}) custom-call(bf16[4,256,864]{2,1,0:T(8,128)(2,1)} %pad_maximum_fusion.refs_0_, bf16[1152,864]{1,0:T(8,128)(2,1)} %copy-done.11, ...), custom_call_target="tpu_custom_call" | custom-call | tf_op jit(solution)/shard_map/stage_12/pallas_call | solution.py:543
  389.6 1.3 convolution_convert_fusion.1
  392.5 5.6 all-gather.1
  399.0 3.5 convolution_convert_fusion.2
  403.3 1.2 reshape.366
  405.2 1.7 copy-done.9
  407.0 1.6 copy-done.10
  408.6 8.3 %to_slots.1.x_ref = bf16[72,656,128]{2,1,0:T(8,128)(2,1)} custom-call(s32[72]{0:T(128)S(1)} %copy-done.18, bf16[1152,864]{1,0:T(8,128)(2,1)S(1)} %copy-done.10, bf16[1152,1152]{1,0:T(8,128)(2,1)S(1)} %copy-done.9, bf16[4,4,288]{2,1,0:T(4,128)(2,1)S(1)} %bitcast.192, bf16[4,1728]{1,0:T(4,128)(2,1)S(1)} %bitcast.191, bf16[288,1152]{1,0:T(8,128)(2,1)S(1)} %copy-done.12, ...), custom_call_target="tpu_custom_call" | custom-call | bytes 23887872 | tf_op jit(solution)/shard_map/to_slots/pallas_call | solution.py:391
  416.9 157.6 %tail.1 = (f32[9,656,128]{2,1,0:T(8,128)}, f32[144,2425]{1,0:T(8,128)}, f32[144,2336]{1,0:T(8,128)}, f32[32,128]{1,0:T(8,128)}, f32[40,128]{1,0:T(8,128)}, /*ind...) custom-call(bf16[72,656,128]{2,1,0:T(8,128)(2,1)} %to_slots.1.x_ref, ...), custom_call_target="tpu_custom_call" | custom-call | tf_op jit(solution)/shard_map/tail/pallas_call | solution.py:1525
  574.6 1.3 slice_reduce_fusion.8
  576.6 1.4 slice_reduce_fusion
  584.0 5.2 convert_bitcast_fusion
  589.2 3.1 fusion.61
  592.3 87.7 %shampoo.1 = (f32[9,288,288]{2,1,0:T(8,128)}, f32[9,2,288,288]{3,2,1,0:T(8,128)}, f32[9,288,288]{2,1,0:T(8,128)}, bf16[9,288,288]{2,1,0:T(8,128)(2,1)}) custom-call(f32[1]{0:T(128)} %bitcast.56.clip_ref, f32[9,656,128]{2,1,0:T(8,128)} %get-tuple-element.109.g_ref, f32[9,2,288,288]{3,2,1,0:T(8,128)} %bitcast.224, f32[9,288,288]{2,1,0:T(8,128)} %bitcast.188), custom_call_target="tpu_custom_call" | custom-call | flops 56757583872 | bytes 25380864 | tf_op jit(solution)/shard_map/shampoo/pallas_call | solution.py:1673
  (222 shorter events, 42.3 us)
Async XLA Ops:
  17.5 2.2 copy-start.22
  18.5 1.9 copy-start.24
  19.8 4.1 copy-start.4
  20.5 142.7 %copy-start.5 = (bf16[144,2304]{1,0:T(8,128)(2,1)}, bf16[144,2304]{1,0:T(8,128)(2,1)S(1)}, u32[]{:S(2)}) copy-start(bf16[144,2304]{1,0:T(8,128)(2,1)S(1)} %slice.257.fada_ref) | copy-start | bytes 1990660
  24.0 2.1 copy-start.7
  163.2 0.6 copy-start.13
  163.8 0.6 copy-start.14
  164.4 0.6 copy-start.15
  165.1 0.6 copy-start.16
  165.7 0.6 copy-start.17
  166.3 9.0 %copy-start.18 = (s32[72]{0:T(128)S(1)}, s32[72]{0:T(128)}, u32[]{:S(2)}) copy-start(s32[72]{0:T(128)} %ids.7) | copy-start | bytes 868
  175.3 4.4 copy-start
  180.6 4.0 copy-start.6
  184.5 1.5 copy-start.3
  192.9 1.5 copy-start.2
  194.4 6.3 copy-start.1
  194.4 16.1 %copy-start.11 = (bf16[1152,864]{1,0:T(8,128)(2,1)}, bf16[1152,864]{1,0:T(8,128)(2,1)S(1)}, u32[]{:S(2)}) copy-start(bf16[1152,864]{1,0:T(8,128)(2,1)S(1)} %get-tuple-element.74.refs_1_) | copy-start | bytes 5971972
  194.4 11.4 %copy-start.26 = (f32[16,16,1152]{2,1,0:T(8,128)S(1)}, f32[16,16,1152]{2,1,0:T(8,128)}, u32[]{:S(2)}) copy-start(f32[16,16,1152]{2,1,0:T(8,128)} %pad_maximum_fusion.1) | copy-start | bytes 3538948
  210.5 2.6 copy-start.21
  210.5 2.6 copy-start.43
  214.1 2.0 copy-start.19
  303.9 42.6 %copy-start.44 = (f32[1,1152]{1,0:T(1,128)S(1)}, f32[1,1152]{1,0:T(1,128)}, u32[]{:S(2)}) copy-start(f32[1,1152]{1,0:T(1,128)} %get-tuple-element.100) | copy-start | bytes 13828
  303.9 42.6 %copy-start.34 = (bf16[256,16]{1,0:T(8,128)(2,1)S(1)}, bf16[256,16]{1,0:T(8,128)(2,1)}, u32[]{:S(2)}) copy-start(bf16[256,16]{1,0:T(8,128)(2,1)} %get-tuple-element.97) | copy-start | bytes 24580
  303.9 42.7 %copy-start.33 = (bf16[256,16]{1,0:T(8,128)(2,1)S(1)}, bf16[256,16]{1,0:T(8,128)(2,1)}, u32[]{:S(2)}) copy-start(bf16[256,16]{1,0:T(8,128)(2,1)} %get-tuple-element.98) | copy-start | bytes 24580
  303.9 42.8 %copy-start.31 = (bf16[256,1152]{1,0:T(8,128)(2,1)S(1)}, bf16[256,1152]{1,0:T(8,128)(2,1)}, u32[]{:S(2)}) copy-start(bf16[256,1152]{1,0:T(8,128)(2,1)} %get-tuple-element.99) | copy-start | bytes 1769476
  345.0 2.2 copy-start.40
  345.0 2.2 copy-start.39
  352.7 3.6 copy-start.20
  399.0 6.3 copy-start.8
  399.0 6.3 copy-start.12
  405.2 1.8 copy-start.9
  407.0 1.6 copy-start.10
  416.8 159.0 %copy-start.38 = (f32[8096]{0:T(1024)S(1)}, f32[8096]{0:T(1024)}, u32[]{:S(2)}) copy-start(f32[8096]{0:T(1024)} %custom-call) | copy-start | bytes 97156
  416.8 165.7 %copy-start.35 = (f32[1,3456]{1,0:T(1,128)S(1)}, f32[1,3456]{1,0:T(1,128)}, u32[]{:S(2)}) copy-start(f32[1,3456]{1,0:T(1,128)} %param.30) | copy-start | bytes 41476
  416.9 165.7 %copy-start.41 = (f32[1,3456]{1,0:T(1,128)S(1)}, f32[1,3456]{1,0:T(1,128)}, u32[]{:S(2)}) copy-start(f32[1,3456]{1,0:T(1,128)} %param.37) | copy-start | bytes 41476
  416.9 165.7 %copy-start.42 = (f32[1,3456]{1,0:T(1,128)S(1)}, f32[1,3456]{1,0:T(1,128)}, u32[]{:S(2)}) copy-start(f32[1,3456]{1,0:T(1,128)} %param.36) | copy-start | bytes 41476
  416.9 166.4 %copy-start.32 = (f32[8096]{0:T(1024)S(1)}, f32[8096]{0:T(1024)}, u32[]{:S(2)}) copy-start(f32[8096]{0:T(1024)} %param.31) | copy-start | bytes 97156
  416.9 166.4 %copy-start.36 = (f32[8096]{0:T(1024)S(1)}, f32[8096]{0:T(1024)}, u32[]{:S(2)}) copy-start(f32[8096]{0:T(1024)} %param.39) | copy-start | bytes 97156
  416.9 166.4 %copy-start.37 = (f32[8096]{0:T(1024)S(1)}, f32[8096]{0:T(1024)}, u32[]{:S(2)}) copy-start(f32[8096]{0:T(1024)} %param.38) | copy-start | bytes 97156
  416.9 167.0 %copy-start.23 = (f32[2425,144]{0,1:T(8,128)S(1)}, f32[2425,144]{0,1:T(8,128)}, u32[]{:S(2)}) copy-start(f32[2425,144]{0,1:T(8,128)} %param.28) | copy-start | bytes 4190404
  416.9 167.0 %copy-start.27 = (f32[2425,144]{0,1:T(8,128)S(1)}, f32[2425,144]{0,1:T(8,128)}, u32[]{:S(2)}) copy-start(f32[2425,144]{0,1:T(8,128)} %param.33) | copy-start | bytes 4190404
  583.9 5.3 copy-start.25
  583.9 5.3 copy-start.28
  583.9 5.3 copy-start.29
  584.0 5.3 copy-start.30

commit v6 on v5

--- a/solution.py
+++ b/solution.py
@@ -617,9 +617,10 @@
             head_in = (normed * fscale + rows_ref[3:4]).astype(bf16)
             head_in_ref[at] = head_in
             upper, lower, gap = facts_ref[0:1], facts_ref[1:2], facts_ref[2:3]
-            weight, share_of = facts_ref[3:4], facts_ref[4:5]
-            error = times(head_in, wp_ref[...]) + bias_ref[0:1] - target_ref[at]
-            fraction = (times(head_in, wr_ref[...]) + bias_ref[1:2] + 1.0) / 2.0
+            weight = facts_ref[3:4]
+            share_of = weight / facts_ref[4:5]
+            error = times_flipped(head_in, wp_ref[...]) + bias_ref[0:1] - target_ref[at]
+            fraction = (times_flipped(head_in, wr_ref[...]) + bias_ref[1:2] + 1.0) / 2.0
             log_var = fraction * upper + (1.0 - fraction) * lower
             gap = gap * error
             ratio = jnp.exp(lower - log_var)
@@ -634,7 +635,7 @@
             ).astype(bf16)
             d_pred_ref[at] = d_pred
             d_raw_ref[at] = d_raw
-            d_head = times_flipped(d_pred, wp_ref[...]) + times_flipped(d_raw, wr_ref[...])
+            d_head = times(d_pred, wp_ref[...]) + times(d_raw, wr_ref[...])
             d_final = norm_rows_back(d_head * fscale, normed, inv_std)
             d_final_ref[at] = d_final
             d_branch = (gate * d_final).astype(bf16)
@@ -653,7 +654,7 @@
 
         return partial, own, after, None
 
-    half = w_pred.shape[1]
+    half = w_pred.shape[0]
     return stage(
         10,
         [active, w_down, hidden, middle, rows, target, w_pred, w_raw, head_bias, facts],
@@ -821,9 +822,9 @@
 
 def head_body(
     x_ref, tf_ref, facts_ref, shared_ref, tables_ref, fada_ref, b1_ref, b2_ref,
-    out_ref, tf_all, facts_all, shared_all, first_t_ref, first_s_ref, cond_ref, signal_ref,
-    signal_all, mod_ref,
-    packed, tf_land, hot_buf, first_s, first_s_all, signal_own, mod_own, mod_land, local_sem, up_sem, down_sem, side_sem,
+    out_ref, tf_all, facts_all, shared_out, first_t_ref, first_s_ref, cond_ref, signal_ref,
+    signal_out, mod_ref,
+    packed, shared_all, signal_all, tf_land, hot_buf, first_s, first_s_all, signal_own, mod_own, mod_land, local_sem, up_sem, down_sem, side_sem,
     up_other, down_other, recv_sem, send, receive,
 ):
     count, ways, f32, bf16 = packed.shape[0], LAYERS * COLUMNS, jnp.float32, jnp.bfloat16
@@ -1016,6 +1017,16 @@
         p.wait()
     mod = jnp.sum(mod_land[...], axis=0)
     mod_ref[...] = jnp.concatenate([mod[:batch], mod[batch:]], axis=1)
+    signal_out[...] = jnp.concatenate(
+        [signal_all[i][:batch, :cols] for i in range(ways)], axis=1
+    ).astype(bf16)
+    rows = jnp.concatenate([shared_all[i].astype(f32)[:, :cols] for i in range(ways)], axis=1)
+    shared_out[:PATCH_VALUES] = rows[:PATCH_VALUES].astype(bf16)
+    for i in range(2):
+        picked = [rows[PATCH_VALUES + 8 * p + 4 * i :][:4] for p in range(4)]
+        shared_out[16 * i + PATCH_VALUES : 16 * i + PATCH_VALUES + 16] = jnp.concatenate(
+            picked, axis=0
+        ).astype(bf16)
     run_hop(3)
 
     def finish(k, _):
@@ -1073,16 +1084,18 @@
             shape((count * ways,) + piece, bf16),
             shape((rows, time_freq.shape[1]), f32),
             shape((ways,) + facts.shape, f32),
-            shape((ways,) + shared.shape, bf16),
+            shape((shared.shape[0], ways * cols), bf16),
             shape((rows, cols), f32),
             shape((rows, ways * cols), bf16),
             shape((rows, cols), f32),
             shape((rows, cols), bf16),
-            shape((ways, 8, LANES), f32),
+            shape((batch, ways * cols), bf16),
             shape((batch, fada), f32),
         ],
         scratch_shapes=[
             pltpu.VMEM((count,) + piece, bf16),
+            pltpu.VMEM((ways,) + shared.shape, bf16),
+            pltpu.VMEM((ways, 8, LANES), f32),
             pltpu.VMEM((ways,) + time_freq.shape, f32),
             pltpu.VMEM((rows, CLASSES), f32),
             pltpu.VMEM((rows, LANES), bf16),
@@ -1108,8 +1121,7 @@
     blocks, time_freq, facts, shared, first_t, first_s, cond, signal, signal_all, mod = out
     blocks = blocks.reshape(-1, PACK_ROWS, LANES // 2)
     return (
-        blocks, time_freq, facts[:, :batch], shared[:, :, :cols].transpose(0, 2, 1), first_t, first_s, cond, signal,
-        signal_all[:, :batch, :cols], mod,
+        blocks, time_freq, facts[:, :batch], shared, first_t, first_s, cond, signal, signal_all, mod,
     )
 
 
@@ -1800,10 +1812,12 @@
             4,
         )
         final_mod = jnp.sum(final_mod, 0)
+        signal = all_columns(signal).astype(bf16)
+        shared = shared.reshape(width, -1).T
+        of_head = shared[PATCH_VALUES:].reshape(4, 2, 4, width).transpose(1, 0, 2, 3)
+        shared = jnp.concatenate([shared[:PATCH_VALUES], of_head.reshape(32, width)], 0)
     weight_total = jnp.sum(facts[:, :, 1])
-    shared = shared.reshape(width, -1)
-    w_patch, w_head = shared[:, :PATCH_VALUES].T, shared[:, PATCH_VALUES:]
-    signal = all_columns(signal).astype(bf16)
+    w_patch, w_pred, w_raw = shared[:PATCH_VALUES], shared[PATCH_VALUES:32], shared[32:]
     final_mod = own(final_mod + side_bias[5 * width : 7 * width])
 
     w_qkv, w_up, w_ada = assemble(
@@ -1886,9 +1900,9 @@
         x = x.reshape(x.shape[:-1] + (4, 8))
         return x[..., :4].reshape(x.shape[:-2] + (16,)), x[..., 4:].reshape(x.shape[:-2] + (16,))
 
-    w_pred, w_raw = halves_of(w_head)
-    own_weight = own(loss_weights)
-    loss_facts = [own(upper_log), own(lower_log), own(mean_gap), own_weight, own_weight / weight_total]
+    own_facts = [own(x) for x in (upper_log, lower_log, mean_gap, loss_weights)]
+    loss_facts = jnp.stack(own_facts + [weight_total[None]])
+    loss_facts = jnp.broadcast_to(loss_facts, (5, 16))
     d_final, head_in, d_pred, d_raw, sums_f, loss_part, d_hidden, up_sum, d_branch = loss_stage(
         active,
         w_down,
@@ -1899,7 +1913,7 @@
         w_pred,
         w_raw,
         jnp.stack(halves_of(side_bias[7 * width :])),
-        jnp.broadcast_to(jnp.stack(loss_facts), (5, 16)),
+        loss_facts,
     )
     loss_part = jnp.sum(loss_part)
     d_fmod = sums_f[:2].reshape(1, 2 * width).astype(bf16)

time: 689 us -> 703 us (1.020)
  Pallas kernels: 554 us -> 572 us
    pallas_call x1, Pallas kernels: 87.7 us -> 106 us  [shampoo(): pl.pallas_call(shampoo_body, grid=(count // group,), in_specs=[pl.BlockSp...]
    unnamed x100 -> x102, local copies, waits for them, and re-layouts: 20.2 us -> 19.6 us
where the time goes in v6:
time: 703 us; the launch traced here: 696 us
  Pallas kernels  572 us (81%)
  local copies, waits for them, and re-layouts  53.3 us (8%)
  other arithmetic  34.9 us (5%)
  matrix products  19.7 us (3%)
  blocking collectives  11.1 us (2%)
    pallas_call x1, Pallas kernels, tail(): pl.pallas_call(tail_body, in_specs=[vmem] * 12, out_specs=[vmem] * len(ou...  158 us
    pallas_call x4, Pallas kernels, stage(): pl.pallas_call(body, in_specs=[vmem] * n_in, out_specs=[vmem] * len(out_s...  152 us
    pallas_call x1, Pallas kernels, head(): pl.pallas_call(head_body, in_specs=[vmem] * 8, out_specs=[anywhere] + [vm...  137 us
    pallas_call x1, Pallas kernels, shampoo(): pl.pallas_call(shampoo_body, grid=(count // group,), in_specs=[pl.BlockSp...  106 us
    unnamed x102, local copies, waits for them, and re-layouts  19.6 us

profile of v6, /device:TPU:0, one launch (start us, length us, event | category | flops | bytes accessed | tf_op | source)
XLA Modules:
  0.0 696.0 jit_solution(17079457378907217583)
XLA Ops:
  0.7 1.2 dynamic_slice.45
  9.2 1.4 slice_reduce_fusion.7
  10.6 1.4 slice.209.refs_5_
  15.6 1.1 add_convert_fusion.1
  18.5 1.3 pad_maximum_fusion.1
  21.5 2.1 copy.155
  24.0 2.1 copy-done.7
  26.1 137.0 %head.1 = (bf16[72,656,128]{2,1,0:T(8,128)(2,1)}, f32[32,256]{1,0:T(8,128)S(1)}, f32[8,8,128]{2,1,0:T(8,128)S(1)}, bf16[48,1152]{1,0:T(8,128)(2,1)S(1)}, f32[32,...) custom-call(f32[9,288,288]{2,1,0:T(8,128)S(1)} %bitcast.176, ...), custom_call_target="tpu_custom_call" | custom-call | tf_op jit(solution)/shard_map/head/pallas_call | solution.py:1079
  166.3 3.3 stack.51
  172.2 4.4 copy-done
  177.5 3.9 assemble.5.refs_1_
  181.5 1.5 copy-done.3
  183.0 6.8 assemble.3
  189.9 1.5 copy-done.2
  192.0 5.7 all-gather
  198.5 0.9 dynamic-slice_bitcast_fusion.1
  200.6 1.4 pad_maximum_fusion.5
  202.8 1.0 fusion.70
  204.4 1.1 dynamic-slice_bitcast_fusion.refs_3_.refs_2_
  205.5 2.0 add_convert_fusion.refs_5_
  207.5 2.5 fusion.9
  212.0 1.2 copy-done.19
  213.2 1.0 fusion.15
  214.2 1.2 copy.161.refs_0_.refs_8_
  215.4 39.9 %stage_9.1 = (f32[256,1152]{1,0:T(8,128)}, f32[256,1152]{1,0:T(8,128)}, f32[4,256,1152]{2,1,0:T(8,128)}, bf16[4,256,1152]{2,1,0:T(8,128)(2,1)}, bf16[4,256,1152]{2,1,0:T(8,128)(2,1)}) custom-call(bf16[4,256,288]{2,1,0:T(8,128)(2,1)} %copy.161.refs_0_.refs_8_, bf16[288,1152]{1,0:T(8,128)(2,1)} %copy-done.6, bf16[1152,1152]{1,0:T(8,128)(2,1)} %copy-done.2, ...), custom_call_target="tpu_custom_call" | custom-call | tf_op jit(solution)/shard_map/stage_9/pallas_call | solution.py:543
  255.3 43.1 %stage_10.1 = (f32[256,1152]{1,0:T(8,128)}, bf16[256,1152]{1,0:T(8,128)(2,1)}, bf16[256,16]{1,0:T(8,128)(2,1)}, bf16[256,16]{1,0:T(8,128)(2,1)}, f32[4,1152]{1,0...) custom-call(bf16[4,256,1152]{2,1,0:T(8,128)(2,1)} %get-tuple-element, ...), custom_call_target="tpu_custom_call" | custom-call | tf_op jit(solution)/shard_map/stage_10/pallas_call | solution.py:543
  298.4 1.3 reduce_sum.146
  301.1 41.1 %stage_11.1 = (f32[256,1152]{1,0:T(8,128)}, f32[4,1152]{1,0:T(4,128)}, bf16[4,256,288]{2,1,0:T(8,128)(2,1)}, bf16[1152,1152]{1,0:T(8,128)(2,1)}, bf16[4,256,1152]{2,1,0:T(8,128)(2,1)}) custom-call(bf16[4,256,1152]{2,1,0:T(8,128)(2,1)} %get-tuple-element.81.refs_0_.refs_7_, bf16[1152,1152]{1,0:T(8,128)(2,1)} %copy-done.2, bf16[288,1152]{1,0:T(8,128)(2,1)} %copy-done.6, ...), custom_call_target="tpu_custom_call" | custom-call | tf_op jit(solution)/shard_map/stage_11/pallas_call | solution.py:543
  342.2 1.4 copy.165
  344.4 3.9 bitcast_reduce_fusion
  348.4 1.4 copy.171
  349.8 3.5 multiply_reduce_fusion.1
  353.4 1.1 multiply_convert_fusion
  356.7 2.1 pad_maximum_fusion.refs_0_
  358.8 27.7 %stage_12.1 = (bf16[256,1152]{1,0:T(8,128)(2,1)}, f32[3,1152]{1,0:T(4,128)}, bf16[1152,864]{1,0:T(8,128)(2,1)}, bf16[1152,1152]{1,0:T(8,128)(2,1)}, bf16[288,1152]{1,0:T(8,128)(2,1)}) custom-call(bf16[4,256,864]{2,1,0:T(8,128)(2,1)} %pad_maximum_fusion.refs_0_, bf16[1152,864]{1,0:T(8,128)(2,1)} %copy-done.11, ...), custom_call_target="tpu_custom_call" | custom-call | tf_op jit(solution)/shard_map/stage_12/pallas_call | solution.py:543
  386.6 1.3 convolution_convert_fusion.1
  389.4 5.4 all-gather.1
  395.6 3.5 convolution_convert_fusion.2
  399.9 1.2 reshape.349
  401.9 1.7 copy-done.9
  403.6 1.6 copy-done.10
  405.2 8.3 %to_slots.1.x_ref = bf16[72,656,128]{2,1,0:T(8,128)(2,1)} custom-call(s32[72]{0:T(128)S(1)} %copy-done.18, bf16[1152,864]{1,0:T(8,128)(2,1)S(1)} %copy-done.10, bf16[1152,1152]{1,0:T(8,128)(2,1)S(1)} %copy-done.9, bf16[4,4,288]{2,1,0:T(4,128)(2,1)S(1)} %bitcast.179, bf16[4,1728]{1,0:T(4,128)(2,1)S(1)} %bitcast.178, bf16[288,1152]{1,0:T(8,128)(2,1)S(1)} %copy-done.12, ...), custom_call_target="tpu_custom_call" | custom-call | bytes 23887872 | tf_op jit(solution)/shard_map/to_slots/pallas_call | solution.py:391
  413.6 157.6 %tail.1 = (f32[9,656,128]{2,1,0:T(8,128)}, f32[144,2425]{1,0:T(8,128)}, f32[144,2336]{1,0:T(8,128)}, f32[32,128]{1,0:T(8,128)}, f32[40,128]{1,0:T(8,128)}, /*ind...) custom-call(bf16[72,656,128]{2,1,0:T(8,128)(2,1)} %to_slots.1.x_ref, ...), custom_call_target="tpu_custom_call" | custom-call | tf_op jit(solution)/shard_map/tail/pallas_call | solution.py:1537
  571.2 1.3 slice_reduce_fusion.8
  573.2 1.4 slice_reduce_fusion
  580.6 5.2 convert_bitcast_fusion
  585.9 3.1 fusion.62
  589.0 105.7 %shampoo.1 = (f32[9,288,288]{2,1,0:T(8,128)}, f32[9,2,288,288]{3,2,1,0:T(8,128)}, f32[9,288,288]{2,1,0:T(8,128)}, bf16[9,288,288]{2,1,0:T(8,128)(2,1)}) custom-call(f32[1]{0:T(128)} %bitcast.52.clip_ref, f32[9,656,128]{2,1,0:T(8,128)} %get-tuple-element.109.g_ref, f32[9,2,288,288]{3,2,1,0:T(8,128)} %bitcast.211, f32[9,288,288]{2,1,0:T(8,128)} %bitcast.175), custom_call_target="tpu_custom_call" | custom-call | flops 56757583872 | bytes 25380864 | tf_op jit(solution)/shard_map/shampoo/pallas_call | solution.py:1685
  (213 shorter events, 40.0 us)
Async XLA Ops:
  17.5 2.2 copy-start.22
  18.5 1.9 copy-start.24
  19.8 4.1 copy-start.4
  20.5 142.7 %copy-start.5 = (bf16[144,2304]{1,0:T(8,128)(2,1)}, bf16[144,2304]{1,0:T(8,128)(2,1)S(1)}, u32[]{:S(2)}) copy-start(bf16[144,2304]{1,0:T(8,128)(2,1)S(1)} %slice.245.fada_ref) | copy-start | bytes 1990660
  23.9 2.1 copy-start.7
  26.1 146.2 %copy-start.18 = (s32[72]{0:T(128)S(1)}, s32[72]{0:T(128)}, u32[]{:S(2)}) copy-start(s32[72]{0:T(128)} %ids.7) | copy-start | bytes 868
  163.1 0.6 copy-start.14
  163.8 0.6 copy-start.15
  164.4 0.6 copy-start.16
  165.0 0.6 copy-start.17
  165.6 11.9 %copy-start.13 = (bf16[32,1152]{1,0:T(8,128)(2,1)}, bf16[32,1152]{1,0:T(8,128)(2,1)S(1)}, u32[]{:S(2)}) copy-start(bf16[32,1152]{1,0:T(8,128)(2,1)S(1)} %get-tuple-element.105.first_s_ref) | copy-start | bytes 221188
  172.2 4.4 copy-start
  177.5 4.0 copy-start.6
  181.5 1.5 copy-start.3
  189.8 1.5 copy-start.2
  191.4 6.3 copy-start.1
  191.4 16.1 %copy-start.11 = (bf16[1152,864]{1,0:T(8,128)(2,1)}, bf16[1152,864]{1,0:T(8,128)(2,1)S(1)}, u32[]{:S(2)}) copy-start(bf16[1152,864]{1,0:T(8,128)(2,1)S(1)} %get-tuple-element.74.refs_1_) | copy-start | bytes 5971972
  191.4 11.4 %copy-start.26 = (f32[16,16,1152]{2,1,0:T(8,128)S(1)}, f32[16,16,1152]{2,1,0:T(8,128)}, u32[]{:S(2)}) copy-start(f32[16,16,1152]{2,1,0:T(8,128)} %pad_maximum_fusion.1) | copy-start | bytes 3538948
  207.5 2.6 copy-start.21
  207.5 2.7 copy-start.43
  207.5 2.7 copy-start.44
  211.2 2.0 copy-start.19
  301.0 42.7 %copy-start.45 = (f32[1,1152]{1,0:T(1,128)S(1)}, f32[1,1152]{1,0:T(1,128)}, u32[]{:S(2)}) copy-start(f32[1,1152]{1,0:T(1,128)} %get-tuple-element.100) | copy-start | bytes 13828
  301.0 42.7 %copy-start.34 = (bf16[256,16]{1,0:T(8,128)(2,1)S(1)}, bf16[256,16]{1,0:T(8,128)(2,1)}, u32[]{:S(2)}) copy-start(bf16[256,16]{1,0:T(8,128)(2,1)} %get-tuple-element.97) | copy-start | bytes 24580
  301.0 42.8 %copy-start.33 = (bf16[256,16]{1,0:T(8,128)(2,1)S(1)}, bf16[256,16]{1,0:T(8,128)(2,1)}, u32[]{:S(2)}) copy-start(bf16[256,16]{1,0:T(8,128)(2,1)} %get-tuple-element.98) | copy-start | bytes 24580
  301.0 42.8 %copy-start.31 = (bf16[256,1152]{1,0:T(8,128)(2,1)S(1)}, bf16[256,1152]{1,0:T(8,128)(2,1)}, u32[]{:S(2)}) copy-start(bf16[256,1152]{1,0:T(8,128)(2,1)} %get-tuple-element.99) | copy-start | bytes 1769476
  342.1 2.1 copy-start.40
  342.2 2.2 copy-start.39
  349.8 3.6 copy-start.20
  395.6 6.3 copy-start.8
  395.6 6.3 copy-start.12
  401.9 1.8 copy-start.9
  403.6 1.6 copy-start.10
  413.5 159.0 %copy-start.38 = (f32[8096]{0:T(1024)S(1)}, f32[8096]{0:T(1024)}, u32[]{:S(2)}) copy-start(f32[8096]{0:T(1024)} %custom-call) | copy-start | bytes 97156
  413.5 165.6 %copy-start.35 = (f32[1,3456]{1,0:T(1,128)S(1)}, f32[1,3456]{1,0:T(1,128)}, u32[]{:S(2)}) copy-start(f32[1,3456]{1,0:T(1,128)} %param.30) | copy-start | bytes 41476
  413.5 165.6 %copy-start.41 = (f32[1,3456]{1,0:T(1,128)S(1)}, f32[1,3456]{1,0:T(1,128)}, u32[]{:S(2)}) copy-start(f32[1,3456]{1,0:T(1,128)} %param.37) | copy-start | bytes 41476
  413.5 165.6 %copy-start.42 = (f32[1,3456]{1,0:T(1,128)S(1)}, f32[1,3456]{1,0:T(1,128)}, u32[]{:S(2)}) copy-start(f32[1,3456]{1,0:T(1,128)} %param.36) | copy-start | bytes 41476
  413.6 166.3 %copy-start.32 = (f32[8096]{0:T(1024)S(1)}, f32[8096]{0:T(1024)}, u32[]{:S(2)}) copy-start(f32[8096]{0:T(1024)} %param.31) | copy-start | bytes 97156
  413.6 166.3 %copy-start.36 = (f32[8096]{0:T(1024)S(1)}, f32[8096]{0:T(1024)}, u32[]{:S(2)}) copy-start(f32[8096]{0:T(1024)} %param.39) | copy-start | bytes 97156
  413.6 166.3 %copy-start.37 = (f32[8096]{0:T(1024)S(1)}, f32[8096]{0:T(1024)}, u32[]{:S(2)}) copy-start(f32[8096]{0:T(1024)} %param.38) | copy-start | bytes 97156
  413.6 167.0 %copy-start.23 = (f32[2425,144]{0,1:T(8,128)S(1)}, f32[2425,144]{0,1:T(8,128)}, u32[]{:S(2)}) copy-start(f32[2425,144]{0,1:T(8,128)} %param.28) | copy-start | bytes 4190404
  413.6 167.0 %copy-start.27 = (f32[2425,144]{0,1:T(8,128)S(1)}, f32[2425,144]{0,1:T(8,128)}, u32[]{:S(2)}) copy-start(f32[2425,144]{0,1:T(8,128)} %param.33) | copy-start | bytes 4190404
  580.6 5.3 copy-start.25
  580.6 5.3 copy-start.28
  580.6 5.3 copy-start.29
  580.6 5.3 copy-start.30
